TPU v7x, 32 devices: a whole 2x2x4 slice. The times are simulated.
32 devices in a mesh: head: 4 (over y, core), tok: 8 (over z, x).
Axes of the slice: x: 2, y: 2, z: 4, core: 2. Of those that a mesh axis runs over, the one named last changes fastest.
Arguments:
- hires_tokens: bfloat16 [32768, 1024], P('tok'), may hold values from -6 to 6
- lowres_tokens: bfloat16 [2048, 1024], P('tok'), may hold values from -6 to 6
- norm_gain: float32 [1024], replicated, may hold values from 0.1 to 1.9
- w_cross_q: bfloat16 [1024, 1024], P(None, 'head'), may hold values from -0.1875 to 0.1875
- w_low_kv: bfloat16 [1024, 2, 1024], P(None, None, 'head'), may hold values from -0.1875 to 0.1875
- w_view_qkv: bfloat16 [1024, 3, 1024], P(None, None, 'head'), may hold values from -0.1875 to 0.1875
- w_out: bfloat16 [2, 1024, 1024], P(None, 'head'), may hold values from -0.125 to 0.125
- block_lists: int32 [256, 8], P('tok'), may hold values from 0 to 15, as said below
- block_counts: int32 [256], P('tok'), may hold values from 1 to 8, as said below
Outputs:
- layer_out: bfloat16 [32768, 1024], P('tok', 'head')
Inputs may be any that keep to these rules, and one draw needn't show every extreme that they name: `block_lists`: each row names 8 distinct low-resolution blocks; only the first block_counts entries of a row are used. `block_counts`: in every draw there is at least one index of tok all of whose query blocks use all 8 entries; query blocks of the other indices may use any count from 1 to 8.
All inputs are finite; a program needn't handle non-finite values.
Results may differ from a plain program's by a relative error of at most 0.009.
Values may be sent and summed in bfloat16 or wider, within the bound.
No kernel may reach another device: no remote copies, remote signals or barrier semaphores. Data moves between devices by JAX's collectives and lax.ppermute only.
A program may use at most 128 MiB of HBM per device.

v0:
```python
import functools
import math

import jax
import jax.numpy as jnp
from jax import lax
from jax.experimental import pallas as pl
from jax.experimental.pallas import tpu as pltpu
from jax.sharding import PartitionSpec as P

HD = 128
VIEWS = 8
BLOCK = 128
LOG2_SCALE = math.log2(math.e) / math.sqrt(HD)
VMEM_BYTES = 60 * 1024 * 1024
SMALL_VMEM_BYTES = 24 * 1024 * 1024
CONTRACT_LAST = (((1,), (1,)), ((), ()))


def rms_rows(row_block, norm_gain):
    values = row_block.astype(jnp.float32)
    factor = lax.rsqrt(jnp.mean(values * values, axis=-1, keepdims=True) + 1e-06)
    return (values * factor * norm_gain).astype(jnp.bfloat16)


def f32_dot(left, right):
    return jnp.dot(left, right, preferred_element_type=jnp.float32)


def block_diagonal(tiles):
    rows = []
    for index, tile in enumerate(tiles):
        zero = jnp.zeros_like(tile)
        rows.append(
            jnp.concatenate([tile if k == index else zero for k in range(len(tiles))], axis=1)
        )
    return jnp.concatenate(rows, axis=0)


def ring_place(tok, n_tok):
    half = lax.div(tok, 2)
    return jnp.where(lax.rem(tok, 2) == 0, half, n_tok - 1 - half)


def cross_kernel(lists_ref, counts_ref, tok_ref, tokens_ref, gain_ref, wq_ref, *refs):
    kv_refs = refs[:-4]
    out_ref, k_ref, vt_ref, q_ref = refs[-4:]
    step = pl.program_id(0)
    rows, cols = out_ref.shape
    heads = cols // HD
    per_step = rows // BLOCK
    listed = lists_ref.shape[1]

    @pl.when(step == 0)
    def _():
        n_tok = len(kv_refs)
        for offset, kv_ref in enumerate(kv_refs):
            chunk = kv_ref.shape[0]
            place = lax.rem(ring_place(tok_ref[0], n_tok) + offset, n_tok)
            home = jnp.where(place < (n_tok + 1) // 2, 2 * place, 2 * (n_tok - 1 - place) + 1)
            start = pl.multiple_of(home * chunk, BLOCK)
            k_ref[pl.ds(start, chunk), :] = kv_ref[:, :cols]
            vt_ref[:, pl.ds(start, chunk)] = kv_ref[:, cols:].T

    normed = rms_rows(tokens_ref[...], gain_ref[...])
    q_ref[...] = (f32_dot(normed, wq_ref[...]) * LOG2_SCALE).astype(jnp.bfloat16)

    def one_block(local, carry):
        block = step * per_step + local
        row_start = pl.multiple_of(local * BLOCK, BLOCK)
        count = counts_ref[block]
        first = lists_ref[block, 0]
        starts = [
            pl.multiple_of(jnp.where(j < count, lists_ref[block, j], first) * BLOCK, BLOCK)
            for j in range(listed)
        ]
        query = block_diagonal(
            [q_ref[pl.ds(row_start, BLOCK), h * HD : (h + 1) * HD] for h in range(heads)]
        )
        keys = jnp.concatenate([k_ref[pl.ds(s, BLOCK), :] for s in starts], axis=0)
        scores = lax.dot_general(keys, query, CONTRACT_LAST, preferred_element_type=jnp.float32)
        top = jnp.max(scores, axis=0, keepdims=True)
        weights = []
        total = jnp.zeros_like(top)
        for j in range(listed):
            shift = top + jnp.where(j < count, 0.0, 1e30)
            weight = jnp.exp2(scores[j * BLOCK : (j + 1) * BLOCK] - shift)
            total = total + jnp.sum(weight, axis=0, keepdims=True)
            weights.append(weight.astype(jnp.bfloat16))
        values_t = jnp.concatenate([vt_ref[:, pl.ds(s, BLOCK)] for s in starts], axis=1)
        mixed_t = f32_dot(values_t, jnp.concatenate(weights, axis=0)) / total
        for h in range(heads):
            part = slice(h * HD, (h + 1) * HD)
            out_ref[pl.ds(row_start, BLOCK), part] = mixed_t[part, part].T.astype(jnp.bfloat16)
        return carry

    lax.fori_loop(0, per_step, one_block, 0, unroll=True)


def cross_attention(hires_tokens, gain, w_cross_q, kv_chunks, block_lists, block_counts):
    tok_index = lax.axis_index("tok").reshape(1)
    tok_rows, width = hires_tokens.shape
    cols = w_cross_q.shape[1]
    chunk = kv_chunks[0].shape[0]
    low_rows = chunk * len(kv_chunks)
    rows = math.gcd(tok_rows, 4 * BLOCK)
    return pl.pallas_call(
        cross_kernel,
        out_shape=jax.ShapeDtypeStruct((tok_rows, cols), jnp.bfloat16),
        grid_spec=pltpu.PrefetchScalarGridSpec(
            num_scalar_prefetch=3,
            grid=(tok_rows // rows,),
            in_specs=[
                pl.BlockSpec((rows, width), lambda i, *_: (i, 0)),
                pl.BlockSpec((1, width), lambda i, *_: (0, 0)),
                pl.BlockSpec((width, cols), lambda i, *_: (0, 0)),
            ]
            + [pl.BlockSpec((chunk, 2 * cols), lambda i, *_: (0, 0)) for _ in kv_chunks],
            out_specs=pl.BlockSpec((rows, cols), lambda i, *_: (i, 0)),
            scratch_shapes=[
                pltpu.VMEM((low_rows, cols), jnp.bfloat16),
                pltpu.VMEM((cols, low_rows), jnp.bfloat16),
                pltpu.VMEM((rows, cols), jnp.bfloat16),
            ],
        ),
        compiler_params=pltpu.CompilerParams(vmem_limit_bytes=VMEM_BYTES),
        cost_estimate=pl.CostEstimate(
            flops=2 * tok_rows * cols * (width + 2 * block_lists.shape[1] * BLOCK * 2),
            bytes_accessed=2 * tok_rows * (width + cols),
            transcendentals=tok_rows * block_lists.shape[1] * BLOCK * (cols // HD),
        ),
        name="cross",
    )(block_lists, block_counts, tok_index, hires_tokens, gain, w_cross_q, *kv_chunks)


def view_kernel(tokens_ref, gain_ref, w_ref, wo_ref, out_ref, normed_ref, qkv_ref, mixed_ref):
    sources, run, width = tokens_ref.shape
    parts, cols, _ = wo_ref.shape
    part_index = pl.program_id(0)
    heads = cols // HD
    rows = sources * run
    pixels = rows // VIEWS
    group = math.gcd(pixels, 32)
    tile = math.gcd(rows, 256)

    @pl.when(pl.program_id(0) == 0)
    def _():
        gain = gain_ref[...]
        step = max(1, tile // run)
        for s in range(0, sources, step):
            tokens = tokens_ref[s : s + step].reshape(step * run, width)
            normed_ref[s * run : (s + step) * run] = rms_rows(tokens, gain)

    for start in range(0, rows, tile):
        stop = start + tile
        tokens = normed_ref[start:stop]
        for k in range(3):
            projected = f32_dot(tokens, w_ref[0, k])
            if k == 0:
                projected = projected * LOG2_SCALE
            qkv_ref[start:stop, k * cols : (k + 1) * cols] = projected.astype(jnp.bfloat16)
    size = VIEWS * group
    row_pixel = lax.broadcasted_iota(jnp.int32, (size, size), 0) % group
    col_pixel = lax.broadcasted_iota(jnp.int32, (size, size), 1) % group
    same = row_pixel == col_pixel

    def gathered(first, column):
        part = slice(column, column + HD)
        return jnp.concatenate(
            [qkv_ref[v * pixels + first : v * pixels + first + group, part] for v in range(VIEWS)],
            axis=0,
        )

    for first in range(0, pixels, group):
        for h in range(heads):
            query = gathered(first, h * HD)
            key = gathered(first, cols + h * HD)
            value = gathered(first, 2 * cols + h * HD)
            scores = lax.dot_general(query, key, CONTRACT_LAST, preferred_element_type=jnp.float32)
            scores = jnp.where(same, scores, -1e30)
            weight = jnp.exp2(scores - jnp.max(scores, axis=1, keepdims=True))
            total = jnp.sum(weight, axis=1, keepdims=True)
            mixed = (f32_dot(weight.astype(jnp.bfloat16), value) / total).astype(jnp.bfloat16)
            for v in range(VIEWS):
                rows_of = slice(v * pixels + first, v * pixels + first + group)
                mixed_ref[part_index, rows_of, h * HD : (h + 1) * HD] = (
                    mixed[v * group : (v + 1) * group]
                )

    @pl.when(part_index == parts - 1)
    def _():
        step = max(1, tile // run)
        for s in range(0, sources, step):
            rows_of = slice(s * run, (s + step) * run)
            term = f32_dot(mixed_ref[0, rows_of], wo_ref[0])
            for g in range(1, parts):
                term = term + f32_dot(mixed_ref[g, rows_of], wo_ref[g])
            term = term.astype(jnp.bfloat16)
            for g in range(parts):
                out_ref[g, s : s + step] = term[:, g * cols : (g + 1) * cols].reshape(
                    step, run, cols
                )


def view_attention(tokens, gain, w_view, w_out):
    sources, run, width = tokens.shape
    parts = w_view.shape[0]
    cols = w_view.shape[3]
    rows = sources * run
    return pl.pallas_call(
        view_kernel,
        out_shape=jax.ShapeDtypeStruct((parts, sources, run, cols), jnp.bfloat16),
        grid=(parts,),
        in_specs=[
            pl.BlockSpec((sources, run, width), lambda i: (0, 0, 0)),
            pl.BlockSpec((1, width), lambda i: (0, 0)),
            pl.BlockSpec((1, 3, width, cols), lambda i: (i, 0, 0, 0)),
            pl.BlockSpec((parts, cols, width), lambda i: (0, 0, 0)),
        ],
        out_specs=pl.BlockSpec((parts, sources, run, cols), lambda i: (0, 0, 0, 0)),
        scratch_shapes=[
            pltpu.VMEM((rows, width), jnp.bfloat16),
            pltpu.VMEM((rows, 3 * cols), jnp.bfloat16),
            pltpu.VMEM((parts, rows, cols), jnp.bfloat16),
        ],
        compiler_params=pltpu.CompilerParams(vmem_limit_bytes=VMEM_BYTES),
        cost_estimate=pl.CostEstimate(
            flops=2 * rows * (parts * cols * (3 * width + 512) + width * width),
            bytes_accessed=2 * (2 * rows * width + 4 * parts * width * cols),
            transcendentals=parts * rows * 512,
        ),
        name="view",
    )(tokens, gain, w_view, w_out)


def base_kernel(index_ref, tokens_ref, cross_ref, w_ref, out_ref):
    total = tokens_ref[...].astype(jnp.float32)
    for g in range(cross_ref.shape[0]):
        total = total + f32_dot(cross_ref[g], w_ref[g])
    out_ref[...] = total


def residual_and_cross(hires_tokens, cross_all, w_columns):
    parts, tok_rows, cols = cross_all.shape
    rows = math.gcd(tok_rows, 512)
    head_index = lax.axis_index("head").reshape(1)
    return pl.pallas_call(
        base_kernel,
        out_shape=jax.ShapeDtypeStruct((tok_rows, cols), jnp.float32),
        grid_spec=pltpu.PrefetchScalarGridSpec(
            num_scalar_prefetch=1,
            grid=(tok_rows // rows,),
            in_specs=[
                pl.BlockSpec((rows, cols), lambda i, index: (i, index[0])),
                pl.BlockSpec((parts, rows, cols), lambda i, index: (0, i, 0)),
                pl.BlockSpec((parts, cols, cols), lambda i, index: (0, 0, 0)),
            ],
            out_specs=pl.BlockSpec((rows, cols), lambda i, index: (i, 0)),
        ),
        compiler_params=pltpu.CompilerParams(vmem_limit_bytes=SMALL_VMEM_BYTES),
        cost_estimate=pl.CostEstimate(
            flops=2 * parts * tok_rows * cols * cols,
            bytes_accessed=2 * tok_rows * cols * (parts + 3),
            transcendentals=0,
        ),
        name="base",
    )(head_index, hires_tokens, cross_all, w_columns)


def add_kernel(base_ref, *refs):
    view_refs, out_ref = refs[:-1], refs[-1]
    for chunk, view_ref in enumerate(view_refs):
        @pl.when(pl.program_id(1) == chunk)
        def _():
            out_ref[...] = (base_ref[...] + view_ref[0].astype(jnp.float32)).astype(jnp.bfloat16)


def add_view(base, view_terms):
    tok_rows, cols = base.shape
    n_head, rows, _ = view_terms[0].shape
    chunks = len(view_terms)
    own = pl.BlockSpec((rows, cols), lambda h, c: (h * chunks + c, 0))
    return pl.pallas_call(
        add_kernel,
        out_shape=jax.ShapeDtypeStruct((tok_rows, cols), jnp.bfloat16),
        grid=(n_head, chunks),
        in_specs=[own] + [pl.BlockSpec((1, rows, cols), lambda h, c: (h, 0, 0))] * chunks,
        out_specs=own,
        compiler_params=pltpu.CompilerParams(vmem_limit_bytes=SMALL_VMEM_BYTES),
        cost_estimate=pl.CostEstimate(
            flops=tok_rows * cols, bytes_accessed=8 * tok_rows * cols, transcendentals=0
        ),
        name="add",
    )(base, *view_terms)


def ring_chunks(own, n_tok):
    order = list(range(0, n_tok, 2)) + list(range(1, n_tok, 2))[::-1]
    upward = [(order[p], order[(p + 1) % n_tok]) for p in range(n_tok)]
    downward = [(order[p], order[p - 1]) for p in range(n_tok)]
    behind, ahead = [own], [own]
    for step in range(n_tok // 2):
        behind.append(lax.ppermute(behind[-1], "tok", upward))
        if step < (n_tok - 1) // 2:
            ahead.append(lax.ppermute(ahead[-1], "tok", downward))
    return ahead + behind[:0:-1]


def shards(
    n_head,
    n_tok,
    hires_tokens,
    lowres_tokens,
    norm_gain,
    w_cross_q,
    w_low_kv,
    w_view_qkv,
    w_out,
    block_lists,
    block_counts,
):
    tok_rows, width = hires_tokens.shape
    cols = w_cross_q.shape[1]
    quarter = tok_rows // n_head
    head_index = lax.axis_index("head")
    gain = norm_gain.reshape(1, width)

    w_view = lax.all_gather(w_view_qkv.transpose(1, 0, 2), "head", axis=0, tiled=False)
    low_kv = f32_dot(
        rms_rows(lowres_tokens, norm_gain), w_low_kv.reshape(width, 2 * cols)
    ).astype(jnp.bfloat16)
    kv_chunks = ring_chunks(low_kv, n_tok)
    kv_chunks, hires_tokens, w_out = lax.optimization_barrier((kv_chunks, hires_tokens, w_out))
    w_view_out = lax.all_gather(w_out[1], "head", axis=0, tiled=False)

    run = quarter // n_tok
    chunks = 2 if run % 32 == 0 else 1
    run = run // chunks
    arrived = []
    for c in range(chunks):
        start = head_index * quarter + c * n_tok * run
        rows = lax.dynamic_slice_in_dim(hires_tokens, start, n_tok * run, 0)
        arrived.append(
            lax.all_to_all(
                rows.reshape(n_tok, run, width), "tok", split_axis=0, concat_axis=0, tiled=True
            )
        )
    cross_out = cross_attention(
        hires_tokens, gain, w_cross_q, kv_chunks, block_lists, block_counts
    )
    cross_out, arrived, w_out = lax.optimization_barrier((cross_out, arrived, w_out))
    cross_all = lax.all_gather(cross_out, "head", axis=0, tiled=False)
    w_columns = lax.all_to_all(
        w_out[0].reshape(cols, n_head, width // n_head).transpose(1, 0, 2),
        "head", split_axis=0, concat_axis=0, tiled=True,
    )
    view_terms = []
    for tokens in arrived:
        term = view_attention(tokens, gain, w_view, w_view_out)
        term = lax.all_to_all(
            term.reshape(n_head * n_tok, run, cols),
            ("head", "tok"), split_axis=0, concat_axis=0, tiled=True,
        )
        view_terms.append(term.reshape(n_head, n_tok * run, cols))
    base = residual_and_cross(hires_tokens, cross_all, w_columns)
    return add_view(base, view_terms)


def solution(mesh):
    in_specs = (
        P("tok", None),
        P("tok", None),
        P(),
        P(None, "head"),
        P(None, None, "head"),
        P(None, None, "head"),
        P(None, "head", None),
        P("tok", None),
        P("tok"),
    )
    out_specs = P("tok", "head")
    body = functools.partial(shards, mesh.shape["head"], mesh.shape["tok"])
    return jax.shard_map(body, mesh=mesh, in_specs=in_specs, out_specs=out_specs, check_vma=False)
```

profile of v0, /device:TPU:0, one launch (start us, length us, event | category | flops | bytes accessed | tf_op | source)
XLA Modules:
  0.0 221.1 jit_solution(4134469560524194516)
XLA Ops:
  6.5 1.5 copy.17
  8.1 1.2 fusion
  9.3 1.5 convolution_convert_fusion.refs_0_
  10.9 3.1 %collective-permute-start.3 = (bf16[256,512]{1,0:T(8,128)(2,1)S(1)}, bf16[256,512]{1,0:T(8,128)(2,1)S(1)}, u32[]{:S(2)}, u32[]{:S(2)}) collective-permute-start(bf16[256,512]{1,0:T(8,128)(2,1)S(1)} %convolution_convert_fusion.refs_0_), channel_id=1, source_target_pairs={{0,2},{2,4},{4,6},{6,7},{7,5},{5,3},{3,1},{1,0},{8,10},{10,12},{12... | collective-permute-start | bytes 786440 | tf_op jit(solution)/shard_map/ppermute | solution.py:303
  13.9 0.0 collective-permute-start
  13.9 6.2 %collective-permute-done.3.refs_7_ = bf16[256,512]{1,0:T(8,128)(2,1)S(1)} collective-permute-done((bf16[256,512]{1,0:T(8,128)(2,1)S(1)}, bf16[256,512]{1,0:T(8,128)(2,1)S(1)}, u32[]{:S(2)}, u32[]{:S(2)}) %collective-permute-start.3) | collective-permute-done | bytes 262176 | tf_op jit(solution)/shard_map/ppermute | solution.py:303
  20.2 1.8 collective-permute-start.4
  22.0 0.2 collective-permute-start.1
  22.2 5.5 %collective-permute-done.4.refs_6_ = bf16[256,512]{1,0:T(8,128)(2,1)S(1)} collective-permute-done((bf16[256,512]{1,0:T(8,128)(2,1)S(1)}, bf16[256,512]{1,0:T(8,128)(2,1)S(1)}, u32[]{:S(2)}, u32[]{:S(2)}) %collective-permute-start.4) | collective-permute-done | bytes 262176 | tf_op jit(solution)/shard_map/ppermute | solution.py:303
  27.7 1.5 collective-permute-start.5
  29.2 0.5 collective-permute-start.2
  29.7 4.5 %collective-permute-done.5.refs_5_ = bf16[256,512]{1,0:T(8,128)(2,1)S(1)} collective-permute-done((bf16[256,512]{1,0:T(8,128)(2,1)S(1)}, bf16[256,512]{1,0:T(8,128)(2,1)S(1)}, u32[]{:S(2)}, u32[]{:S(2)}) %collective-permute-start.5) | collective-permute-done | bytes 262176 | tf_op jit(solution)/shard_map/ppermute | solution.py:303
  34.2 1.7 collective-permute-start.6
  36.0 0.0 collective-permute-done.2.refs_3_
  36.0 0.7 copy-done.13
  36.7 4.0 %collective-permute-done.6.refs_4_ = bf16[256,512]{1,0:T(8,128)(2,1)} collective-permute-done((bf16[256,512]{1,0:T(8,128)(2,1)S(1)}, bf16[256,512]{1,0:T(8,128)(2,1)}, u32[]{:S(2)}, u32[]{:S(2)}) %collective-permute-start.6) | collective-permute-done | bytes 262176 | tf_op jit(solution)/shard_map/ppermute | solution.py:303
  40.7 0.9 slice.7
  41.6 0.0 all-gather.6.cloned.1.call-update
  41.6 0.0 all-gather.10.cloned.1.call-start
  41.7 0.7 all-gather.10.cloned.1.call-update
  42.4 0.0 copy-start.6
  42.4 2.7 %constant_dynamic-slice_fusion = (bf16[512,1024]{1,0:T(8,128)(2,1)}, bf16[512,1024]{1,0:T(8,128)(2,1)S(1)}) fusion(bf16[4096,1024]{1,0:T(8,128)(2,1)} %tokens_ref.1, s32[]{:T(128)S(6)} %select_n.7, s32[]{:T(128)S(6)} %select_n.6), kind=kLoop, calls=%fused_computation.9 | loop fusion | bytes 4194312 | tf_op jit(solution)/shard_map/dynamic_slice | solution.py:342
  45.1 27.6 %all_to_all.25.tokens_ref = bf16[8,64,1024]{2,1,0:T(8,128)(2,1)} all-to-all(bf16[8,64,1024]{2,1,0:T(8,128)(2,1)S(1)} %bitcast.20), channel_id=1, replica_groups=mesh['head'=4,'tok'=8] {'tok'}, dimensions={0} | all-to-all | bytes 2097152 | tf_op jit(solution)/shard_map/all_to_all | solution.py:344
  72.7 3.6 %all-to-all-start.1 = ((bf16[8,64,1024]{2,1,0:T(8,128)(2,1)}), bf16[8,64,1024]{2,1,0:T(8,128)(2,1)S(1)}, u32[]{:S(2)}, u32[]{:S(2)}) async-start(bf16[8,64,1024]{2,1,0:T(8,128)(2,1)} %bitcast.4), calls=%async_computation.1 | async-start | bytes 2097152 | tf_op jit(solution)/shard_map/all_to_all | solution.py:344
  76.3 0.0 all-gather.8.cloned.1.call-start
  76.4 0.7 copy.14.lists_ref
  77.0 26.6 %cross.1 = bf16[4096,256]{1,0:T(8,128)(2,1)} custom-call(s32[32,8]{1,0:T(8,128)} %copy.14.lists_ref, s32[32]{0:T(128)} %counts_ref.1, s32[1]{0:T(128)} %bitcast.1.tok_ref, bf16[4096,1024]{1,0:T(8,128)(2,1)} %tokens_ref.1, f32[1,1024]{1,0:T(1,128)} %bitcast.29, bf16[1024,256]{1,0:T(8,128)(2,1)} %wq_ref.1, bf16[256,512]{1,0:T(8,128)(2,1)} %copy-done.7, ...), custom_call_target="tpu_custom_call" | custom-call | flops 10737418240 | bytes 10485760 | tf_op jit(solution)/shard_map/cross/pallas_call | solution.py:107
  103.7 0.0 all-to-all-done.1.tokens_ref
  103.7 1.0 copy-done.5
  104.6 0.0 all-gather.8.cloned.1.call-update
  104.6 0.5 copy.15
  105.2 1.0 copy.16
  106.2 3.5 %all-to-all-start.2 = ((bf16[4,256,256]{2,1,0:T(8,128)(2,1)}), bf16[4,256,256]{2,1,0:T(8,128)(2,1)S(1)}, u32[]{:S(2)}, u32[]{:S(2)}) async-start(bf16[4,256,256]{2,1,0:T(8,128)(2,1)} %bitcast.7), calls=%async_computation.2 | async-start | bytes 1048576 | tf_op jit(solution)/shard_map/all_to_all | solution.py:353
  109.7 0.0 all-gather.6.cloned.1.call-done.wo_ref
  109.7 4.0 %all-gather.10.cloned.1.call-done = bf16[12,1024,256]{2,1,0:T(8,128)(2,1)} async-done(((bf16[3,1024,256]{2,1,0:T(8,128)(2,1)}), bf16[12,1024,256]{2,1,0:T(8,128)(2,1)}) %all-gather.10.cloned.1.call-update) | async-done | bytes 6291472 | tf_op jit(solution)/shard_map/all_gather | solution.py:328
  113.7 11.5 %view.2 = bf16[4,8,64,256]{3,2,1,0:T(8,128)(2,1)} custom-call(bf16[8,64,1024]{2,1,0:T(8,128)(2,1)} %all_to_all.25.tokens_ref, f32[1,1024]{1,0:T(1,128)} %bitcast.30, bf16[4,3,1024,256]{3,2,1,0:T(8,128)(2,1)} %bitcast.27, bf16[4,256,1024]{2,1,0:T(8,128)(2,1)} %all-gather.6.cloned.1.call-done.wo_ref), custom_call_target="tpu_custom_call" | custom-call | flops 4831838208 | bytes 10485760 | tf_op jit(solution)/shard_map/view/pallas_call | solution.py:210
  125.2 4.6 %all-to-all-start.3 = ((bf16[32,64,256]{2,1,0:T(8,128)(2,1)}), bf16[32,64,256]{2,1,0:T(8,128)(2,1)S(1)}, u32[]{:S(2)}, u32[]{:S(2)}) async-start(bf16[32,64,256]{2,1,0:T(8,128)(2,1)} %bitcast.25), calls=%async_computation.3 | async-start | bytes 2097152 | tf_op jit(solution)/shard_map/all_to_all | solution.py:360
  129.8 11.5 %view.3 = bf16[4,8,64,256]{3,2,1,0:T(8,128)(2,1)} custom-call(bf16[8,64,1024]{2,1,0:T(8,128)(2,1)} %copy-done.5, f32[1,1024]{1,0:T(1,128)} %bitcast.31, bf16[4,3,1024,256]{3,2,1,0:T(8,128)(2,1)} %bitcast.28, bf16[4,256,1024]{2,1,0:T(8,128)(2,1)} %all-gather.6.cloned.1.call-done.wo_ref), custom_call_target="tpu_custom_call" | custom-call | flops 4831838208 | bytes 10485760 | tf_op jit(solution)/shard_map/view/pallas_call | solution.py:210
  141.3 16.1 %all-to-all-done.3 = bf16[32,64,256]{2,1,0:T(8,128)(2,1)S(1)} async-done(((bf16[32,64,256]{2,1,0:T(8,128)(2,1)}), bf16[32,64,256]{2,1,0:T(8,128)(2,1)S(1)}, u32[]{:S(2)}, u32[]{:S(2)}) %all-to-all-start.3) | async-done | bytes 1048608 | tf_op jit(solution)/shard_map/all_to_all | solution.py:360
  157.4 2.6 %all-to-all-start.4 = ((bf16[32,64,256]{2,1,0:T(8,128)(2,1)}), bf16[32,64,256]{2,1,0:T(8,128)(2,1)S(1)}, u32[]{:S(2)}, u32[]{:S(2)}) async-start(bf16[32,64,256]{2,1,0:T(8,128)(2,1)} %bitcast.24), calls=%async_computation.4 | async-start | bytes 2097152 | tf_op jit(solution)/shard_map/all_to_all | solution.py:360
  160.1 36.0 %all-gather.8.cloned.1.call-done = bf16[16384,256]{1,0:T(8,128)(2,1)} async-done(((bf16[4096,256]{1,0:T(8,128)(2,1)}), bf16[16384,256]{1,0:T(8,128)(2,1)}) %all-gather.8.cloned.1.call-update) | async-done | bytes 8388624 | tf_op jit(solution)/shard_map/all_gather | solution.py:352
  196.1 3.4 %copy-done.2 = bf16[4096,1024]{1,0:T(8,128)(2,1)S(1)} copy-done((bf16[4096,1024]{1,0:T(8,128)(2,1)S(1)}, bf16[4096,1024]{1,0:T(8,128)(2,1)}, u32[]{:S(2)}) %copy-start.2) | copy-done | bytes 8388632
  199.5 3.4 %copy-done.3 = bf16[16384,256]{1,0:T(8,128)(2,1)S(1)} copy-done((bf16[16384,256]{1,0:T(8,128)(2,1)S(1)}, bf16[16384,256]{1,0:T(8,128)(2,1)}, u32[]{:S(2)}) %copy-start.3) | copy-done | bytes 8388632
  202.9 4.5 %base.1.base_ref = f32[4096,256]{1,0:T(8,128)S(1)} custom-call(s32[1]{0:T(128)} %bitcast.index_ref, bf16[4096,1024]{1,0:T(8,128)(2,1)S(1)} %copy-done.2, bf16[4,4096,256]{2,1,0:T(8,128)(2,1)S(1)} %bitcast.17, bf16[4,256,256]{2,1,0:T(8,128)(2,1)S(1)} %all-to-all-done.2.w_ref), custom_call_target="tpu_custom_call" | custom-call | flops 2147483648 | bytes 14680064 | tf_op jit(solution)/shard_map/base/pallas_call | solution.py:247
  207.4 2.0 copy-done
  209.3 0.0 all-to-all-done.4
  209.3 2.2 copy-done.1
  211.5 3.1 %add.30 = bf16[4096,256]{1,0:T(8,128)(2,1)} custom-call(f32[4096,256]{1,0:T(8,128)S(1)} %copy-done.1, bf16[4,512,256]{2,1,0:T(8,128)(2,1)S(1)} %bitcast.18, bf16[4,512,256]{2,1,0:T(8,128)(2,1)S(1)} %bitcast.19), custom_call_target="tpu_custom_call" | custom-call | flops 1048576 | bytes 8388608 | tf_op jit(solution)/shard_map/add/pallas_call | solution.py:283
  (27 shorter events, 0.1 us)
Async XLA Ops:
  6.5 34.2 %copy-start.4 = (bf16[2,256,1024]{2,1,0:T(8,128)(2,1)S(1)}, bf16[2,256,1024]{2,1,0:T(8,128)(2,1)}, u32[]{:S(2)}) copy-start(bf16[2,256,1024]{2,1,0:T(8,128)(2,1)} %param.15) | copy-start | bytes 3145732
  6.5 103.2 %all-gather.6.cloned.1.call-start = ((), (), s32[]{:S(2)}) async-start(), calls=%async_computation.5 | async-start | bytes 2621440 | tf_op jit(solution)/shard_map/all_gather | solution.py:334
  10.9 61.8 %copy-start.7 = (bf16[256,512]{1,0:T(8,128)(2,1)}, bf16[256,512]{1,0:T(8,128)(2,1)S(1)}, u32[]{:S(2)}) copy-start(bf16[256,512]{1,0:T(8,128)(2,1)S(1)} %convolution_convert_fusion.refs_0_) | copy-start | bytes 786436
  10.9 9.3 %collective-permute-start.3 = (bf16[256,512]{1,0:T(8,128)(2,1)S(1)}, bf16[256,512]{1,0:T(8,128)(2,1)S(1)}, u32[]{:S(2)}, u32[]{:S(2)}) collective-permute-start(bf16[256,512]{1,0:T(8,128)(2,1)S(1)} %convolution_convert_fusion.refs_0_), channel_id=1, source_target_pairs={{0,2},{2,4},{4,6},{6,7},{7,5},{5,3},{3,1},{1,0},{8,10},{10,12},{12... | collective-permute-start | bytes 786440 | tf_op jit(solution)/shard_map/ppermute | solution.py:303
  13.9 8.1 %collective-permute-start = (bf16[256,512]{1,0:T(8,128)(2,1)S(1)}, bf16[256,512]{1,0:T(8,128)(2,1)S(1)}, u32[]{:S(2)}, u32[]{:S(2)}) collective-permute-start(bf16[256,512]{1,0:T(8,128)(2,1)S(1)} %convolution_convert_fusion.refs_0_), channel_id=1, source_target_pairs={{0,1},{2,0},{4,2},{6,4},{7,6},{5,7},{3,5},{1,3},{8,9},{10,8},{12,1... | collective-permute-start | bytes 786440 | tf_op jit(solution)/shard_map/ppermute | solution.py:305
  20.2 52.5 %copy-start.8 = (bf16[256,512]{1,0:T(8,128)(2,1)}, bf16[256,512]{1,0:T(8,128)(2,1)S(1)}, u32[]{:S(2)}) copy-start(bf16[256,512]{1,0:T(8,128)(2,1)S(1)} %collective-permute-done.3.refs_7_) | copy-start | bytes 786436
  20.2 7.5 %collective-permute-start.4 = (bf16[256,512]{1,0:T(8,128)(2,1)S(1)}, bf16[256,512]{1,0:T(8,128)(2,1)S(1)}, u32[]{:S(2)}, u32[]{:S(2)}) collective-permute-start(bf16[256,512]{1,0:T(8,128)(2,1)S(1)} %collective-permute-done.3.refs_7_), channel_id=1, source_target_pairs={{0,2},{2,4},{4,6},{6,7},{7,5},{5,3},{3,1},{1,0},{8,10},{10,12},{12... | collective-permute-start | bytes 786440 | tf_op jit(solution)/shard_map/ppermute | solution.py:303
  22.0 50.7 %copy-start.9 = (bf16[256,512]{1,0:T(8,128)(2,1)}, bf16[256,512]{1,0:T(8,128)(2,1)S(1)}, u32[]{:S(2)}) copy-start(bf16[256,512]{1,0:T(8,128)(2,1)S(1)} %collective-permute-done.refs_1_) | copy-start | bytes 786436
  22.0 7.2 %collective-permute-start.1 = (bf16[256,512]{1,0:T(8,128)(2,1)S(1)}, bf16[256,512]{1,0:T(8,128)(2,1)S(1)}, u32[]{:S(2)}, u32[]{:S(2)}) collective-permute-start(bf16[256,512]{1,0:T(8,128)(2,1)S(1)} %collective-permute-done.refs_1_), channel_id=1, source_target_pairs={{0,1},{2,0},{4,2},{6,4},{7,6},{5,7},{3,5},{1,3},{8,9},{10,8},{12,1... | collective-permute-start | bytes 786440 | tf_op jit(solution)/shard_map/ppermute | solution.py:305
  27.7 45.0 %copy-start.10 = (bf16[256,512]{1,0:T(8,128)(2,1)}, bf16[256,512]{1,0:T(8,128)(2,1)S(1)}, u32[]{:S(2)}) copy-start(bf16[256,512]{1,0:T(8,128)(2,1)S(1)} %collective-permute-done.4.refs_6_) | copy-start | bytes 786436
  27.7 6.6 %collective-permute-start.5 = (bf16[256,512]{1,0:T(8,128)(2,1)S(1)}, bf16[256,512]{1,0:T(8,128)(2,1)S(1)}, u32[]{:S(2)}, u32[]{:S(2)}) collective-permute-start(bf16[256,512]{1,0:T(8,128)(2,1)S(1)} %collective-permute-done.4.refs_6_), channel_id=1, source_target_pairs={{0,2},{2,4},{4,6},{6,7},{7,5},{5,3},{3,1},{1,0},{8,10},{10,12},{12... | collective-permute-start | bytes 786440 | tf_op jit(solution)/shard_map/ppermute | solution.py:303
  29.2 43.5 %copy-start.11 = (bf16[256,512]{1,0:T(8,128)(2,1)}, bf16[256,512]{1,0:T(8,128)(2,1)S(1)}, u32[]{:S(2)}) copy-start(bf16[256,512]{1,0:T(8,128)(2,1)S(1)} %collective-permute-done.1.refs_2_) | copy-start | bytes 786436
  29.2 6.8 %collective-permute-start.2 = (bf16[256,512]{1,0:T(8,128)(2,1)S(1)}, bf16[256,512]{1,0:T(8,128)(2,1)S(1)}, u32[]{:S(2)}, u32[]{:S(2)}) collective-permute-start(bf16[256,512]{1,0:T(8,128)(2,1)S(1)} %collective-permute-done.1.refs_2_), channel_id=1, source_target_pairs={{0,1},{2,0},{4,2},{6,4},{7,6},{5,7},{3,5},{1,3},{8,9},{10,8},{12,1... | collective-permute-start | bytes 786440 | tf_op jit(solution)/shard_map/ppermute | solution.py:305
  34.2 1.7 copy-start.12
  34.2 6.5 %collective-permute-start.6 = (bf16[256,512]{1,0:T(8,128)(2,1)S(1)}, bf16[256,512]{1,0:T(8,128)(2,1)}, u32[]{:S(2)}, u32[]{:S(2)}) collective-permute-start(bf16[256,512]{1,0:T(8,128)(2,1)S(1)} %collective-permute-done.5.refs_5_), channel_id=1, source_target_pairs={{0,2},{2,4},{4,6},{6,7},{7,5},{5,3},{3,1},{1,0},{8,10},{10,12},{12... | collective-permute-start | bytes 786440 | tf_op jit(solution)/shard_map/ppermute | solution.py:303
  36.0 0.7 copy-start.13
  41.6 72.1 %all-gather.10.cloned.1.call-start = ((), (), s32[]{:S(2)}) async-start(), calls=%async_computation.7 | async-start | bytes 7864320 | tf_op jit(solution)/shard_map/all_gather | solution.py:328
  42.4 34.0 %copy-start.6 = (s32[32,8]{0,1:T(8,128)S(1)}, s32[32,8]{0,1:T(8,128)}, u32[]{:S(2)}) copy-start(s32[32,8]{0,1:T(8,128)} %param.16) | copy-start | bytes 3076
  72.7 31.0 %all-to-all-start.1 = ((bf16[8,64,1024]{2,1,0:T(8,128)(2,1)}), bf16[8,64,1024]{2,1,0:T(8,128)(2,1)S(1)}, u32[]{:S(2)}, u32[]{:S(2)}) async-start(bf16[8,64,1024]{2,1,0:T(8,128)(2,1)} %bitcast.4), calls=%async_computation.1 | async-start | bytes 2097152 | tf_op jit(solution)/shard_map/all_to_all | solution.py:344
  76.3 119.8 %all-gather.8.cloned.1.call-start = ((), (), s32[]{:S(2)}) async-start(), calls=%async_computation.6 | async-start | bytes 10485760 | tf_op jit(solution)/shard_map/all_gather | solution.py:352
  103.7 1.0 copy-start.5
  106.2 19.0 %all-to-all-start.2 = ((bf16[4,256,256]{2,1,0:T(8,128)(2,1)}), bf16[4,256,256]{2,1,0:T(8,128)(2,1)S(1)}, u32[]{:S(2)}, u32[]{:S(2)}) async-start(bf16[4,256,256]{2,1,0:T(8,128)(2,1)} %bitcast.7), calls=%async_computation.2 | async-start | bytes 1048576 | tf_op jit(solution)/shard_map/all_to_all | solution.py:353
  125.2 32.2 %all-to-all-start.3 = ((bf16[32,64,256]{2,1,0:T(8,128)(2,1)}), bf16[32,64,256]{2,1,0:T(8,128)(2,1)S(1)}, u32[]{:S(2)}, u32[]{:S(2)}) async-start(bf16[32,64,256]{2,1,0:T(8,128)(2,1)} %bitcast.25), calls=%async_computation.3 | async-start | bytes 2097152 | tf_op jit(solution)/shard_map/all_to_all | solution.py:360
  157.4 51.9 %all-to-all-start.4 = ((bf16[32,64,256]{2,1,0:T(8,128)(2,1)}), bf16[32,64,256]{2,1,0:T(8,128)(2,1)S(1)}, u32[]{:S(2)}, u32[]{:S(2)}) async-start(bf16[32,64,256]{2,1,0:T(8,128)(2,1)} %bitcast.24), calls=%async_computation.4 | async-start | bytes 2097152 | tf_op jit(solution)/shard_map/all_to_all | solution.py:360
  196.1 3.4 %copy-start.2 = (bf16[4096,1024]{1,0:T(8,128)(2,1)S(1)}, bf16[4096,1024]{1,0:T(8,128)(2,1)}, u32[]{:S(2)}) copy-start(bf16[4096,1024]{1,0:T(8,128)(2,1)} %tokens_ref.1) | copy-start | bytes 25165828
  199.5 3.4 %copy-start.3 = (bf16[16384,256]{1,0:T(8,128)(2,1)S(1)}, bf16[16384,256]{1,0:T(8,128)(2,1)}, u32[]{:S(2)}) copy-start(bf16[16384,256]{1,0:T(8,128)(2,1)} %all-gather.8.cloned.1.call-done) | copy-start | bytes 25165828
  207.4 2.0 copy-start
  209.3 2.2 copy-start.1
Sparse Core Ops, SparseCore 0:
  41.7 23.9 all-gather.5
  67.3 46.3 all-gather.9
  115.3 80.7 all-gather.7
where the time goes:
time: 222 us; the launch traced here: 221 us
  waiting for transfers between devices  77.2 us (35%)
  Pallas kernels  57.1 us (26%)
  blocking collectives  27.6 us (12%)
  starting transfers between devices  23.3 us (10%)
  local copies, waits for them, and re-layouts  19.9 us (9%)
  between operations  13.3 us (6%)
    all_gather x1, waiting for transfers between devices, shards(): cross_all = lax.all_gather(cross_out, 'head', axis=0, tiled=False)  36 us
    all_to_all x1, blocking collectives, shards(): lax.all_to_all(rows.reshape(n_tok, run, width), 'tok', split_axis=0, conc...  27.6 us
    pallas_call x1, Pallas kernels, cross_attention(): pl.pallas_call(cross_kernel, out_shape=jax.ShapeDtypeStruct((tok_rows, co...  26.6 us
    pallas_call x2, Pallas kernels, view_attention(): pl.pallas_call(view_kernel, out_shape=jax.ShapeDtypeStruct((parts, source...  22.9 us
    ppermute x4, waiting for transfers between devices, ring_chunks(): behind.append(lax.ppermute(behind[-1], 'tok', upward))  20.3 us
    all_to_all x2, waiting for transfers between devices, shards(): lax.all_to_all(term.reshape(n_head * n_tok, run, cols), ('head', 'tok'),...  16.1 us
    unnamed x30, local copies, waits for them, and re-layouts  14.8 us
    ppermute x4, starting transfers between devices, ring_chunks(): behind.append(lax.ppermute(behind[-1], 'tok', upward))  8.13 us
  transfers between devices with their start and end apart: 14, of which 7 were waited for; matrix products, arithmetic and copies ran while one was open for 2% of the time, Pallas kernels for 24%

commit v1 on v0

--- a/solution.py
+++ b/solution.py
@@ -13,7 +13,6 @@
 BLOCK = 128
 LOG2_SCALE = math.log2(math.e) / math.sqrt(HD)
 VMEM_BYTES = 60 * 1024 * 1024
-SMALL_VMEM_BYTES = 24 * 1024 * 1024
 CONTRACT_LAST = (((1,), (1,)), ((), ()))
 
 
@@ -233,17 +232,19 @@
     )(tokens, gain, w_view, w_out)
 
 
-def base_kernel(index_ref, tokens_ref, cross_ref, w_ref, out_ref):
+def base_kernel(index_ref, tokens_ref, cross_ref, *refs):
+    w_refs, out_ref = refs[:-1], refs[-1]
+    parts = len(w_refs)
     total = tokens_ref[...].astype(jnp.float32)
-    for g in range(cross_ref.shape[0]):
-        total = total + f32_dot(cross_ref[g], w_ref[g])
+    for k, w_ref in enumerate(w_refs):
+        group = lax.rem(index_ref[0] + parts - k, parts)
+        total = total + f32_dot(cross_ref[group], w_ref[...])
     out_ref[...] = total
 
 
-def residual_and_cross(hires_tokens, cross_all, w_columns):
+def residual_and_cross(head_index, hires_tokens, cross_all, w_columns):
     parts, tok_rows, cols = cross_all.shape
     rows = math.gcd(tok_rows, 512)
-    head_index = lax.axis_index("head").reshape(1)
     return pl.pallas_call(
         base_kernel,
         out_shape=jax.ShapeDtypeStruct((tok_rows, cols), jnp.float32),
@@ -253,45 +254,59 @@
             in_specs=[
                 pl.BlockSpec((rows, cols), lambda i, index: (i, index[0])),
                 pl.BlockSpec((parts, rows, cols), lambda i, index: (0, i, 0)),
-                pl.BlockSpec((parts, cols, cols), lambda i, index: (0, 0, 0)),
-            ],
+            ]
+            + [pl.BlockSpec((cols, cols), lambda i, index: (0, 0))] * parts,
             out_specs=pl.BlockSpec((rows, cols), lambda i, index: (i, 0)),
         ),
-        compiler_params=pltpu.CompilerParams(vmem_limit_bytes=SMALL_VMEM_BYTES),
+        compiler_params=pltpu.CompilerParams(vmem_limit_bytes=VMEM_BYTES),
         cost_estimate=pl.CostEstimate(
             flops=2 * parts * tok_rows * cols * cols,
             bytes_accessed=2 * tok_rows * cols * (parts + 3),
             transcendentals=0,
         ),
         name="base",
-    )(head_index, hires_tokens, cross_all, w_columns)
-
-
-def add_kernel(base_ref, *refs):
-    view_refs, out_ref = refs[:-1], refs[-1]
-    for chunk, view_ref in enumerate(view_refs):
-        @pl.when(pl.program_id(1) == chunk)
-        def _():
-            out_ref[...] = (base_ref[...] + view_ref[0].astype(jnp.float32)).astype(jnp.bfloat16)
-
-
-def add_view(base, view_terms):
+    )(head_index.reshape(1), hires_tokens, cross_all, *w_columns)
+
+
+def add_kernel(base_ref, view_ref, *refs):
+    refs[-1][...] = (base_ref[...] + view_ref[0].astype(jnp.float32)).astype(jnp.bfloat16)
+
+
+def add_view(base, view_term, chunk, chunks, earlier):
     tok_rows, cols = base.shape
-    n_head, rows, _ = view_terms[0].shape
-    chunks = len(view_terms)
-    own = pl.BlockSpec((rows, cols), lambda h, c: (h * chunks + c, 0))
+    n_head, rows, _ = view_term.shape
+    own = pl.BlockSpec((rows, cols), lambda h: (h * chunks + chunk, 0))
+    in_specs = [own, pl.BlockSpec((1, rows, cols), lambda h: (h, 0, 0))]
+    operands = [base, view_term]
+    if earlier is not None:
+        in_specs.append(pl.BlockSpec(memory_space=pl.ANY))
+        operands.append(earlier)
     return pl.pallas_call(
         add_kernel,
         out_shape=jax.ShapeDtypeStruct((tok_rows, cols), jnp.bfloat16),
-        grid=(n_head, chunks),
-        in_specs=[own] + [pl.BlockSpec((1, rows, cols), lambda h, c: (h, 0, 0))] * chunks,
+        grid=(n_head,),
+        in_specs=in_specs,
         out_specs=own,
-        compiler_params=pltpu.CompilerParams(vmem_limit_bytes=SMALL_VMEM_BYTES),
+        input_output_aliases={} if earlier is None else {2: 0},
+        compiler_params=pltpu.CompilerParams(vmem_limit_bytes=VMEM_BYTES),
         cost_estimate=pl.CostEstimate(
-            flops=tok_rows * cols, bytes_accessed=8 * tok_rows * cols, transcendentals=0
+            flops=n_head * rows * cols, bytes_accessed=8 * n_head * rows * cols, transcendentals=0
         ),
         name="add",
-    )(base, *view_terms)
+    )(*operands)
+
+
+def column_blocks(rows_of_w, head_index, n_head):
+    cols = rows_of_w.shape[1] // n_head
+    blocks = []
+    for k in range(n_head):
+        start = lax.rem(head_index + k, n_head) * cols
+        block = lax.dynamic_slice_in_dim(rows_of_w, start, cols, 1)
+        if k:
+            pairs = [(h, (h + k) % n_head) for h in range(n_head)]
+            block = lax.ppermute(block, "head", pairs)
+        blocks.append(block)
+    return blocks
 
 
 def ring_chunks(own, n_tok):
@@ -330,30 +345,31 @@
         rms_rows(lowres_tokens, norm_gain), w_low_kv.reshape(width, 2 * cols)
     ).astype(jnp.bfloat16)
     kv_chunks = ring_chunks(low_kv, n_tok)
-    kv_chunks, hires_tokens, w_out = lax.optimization_barrier((kv_chunks, hires_tokens, w_out))
     w_view_out = lax.all_gather(w_out[1], "head", axis=0, tiled=False)
+    kv_chunks, hires_tokens = lax.optimization_barrier((kv_chunks, hires_tokens))
 
     run = quarter // n_tok
     chunks = 2 if run % 32 == 0 else 1
     run = run // chunks
-    arrived = []
-    for c in range(chunks):
-        start = head_index * quarter + c * n_tok * run
-        rows = lax.dynamic_slice_in_dim(hires_tokens, start, n_tok * run, 0)
-        arrived.append(
-            lax.all_to_all(
-                rows.reshape(n_tok, run, width), "tok", split_axis=0, concat_axis=0, tiled=True
-            )
+
+    def arrive(chunk, tokens):
+        start = head_index * quarter + chunk * n_tok * run
+        rows = lax.dynamic_slice_in_dim(tokens, start, n_tok * run, 0)
+        return lax.all_to_all(
+            rows.reshape(n_tok, run, width), "tok", split_axis=0, concat_axis=0, tiled=True
         )
+
+    arrived = [arrive(0, hires_tokens)]
     cross_out = cross_attention(
         hires_tokens, gain, w_cross_q, kv_chunks, block_lists, block_counts
     )
-    cross_out, arrived, w_out = lax.optimization_barrier((cross_out, arrived, w_out))
+    cross_out, arrived, w_out, hires_tokens = lax.optimization_barrier(
+        (cross_out, arrived, w_out, hires_tokens)
+    )
     cross_all = lax.all_gather(cross_out, "head", axis=0, tiled=False)
-    w_columns = lax.all_to_all(
-        w_out[0].reshape(cols, n_head, width // n_head).transpose(1, 0, 2),
-        "head", split_axis=0, concat_axis=0, tiled=True,
-    )
+    for chunk in range(1, chunks):
+        arrived.append(arrive(chunk, hires_tokens))
+    w_columns = column_blocks(w_out[0], head_index, n_head)
     view_terms = []
     for tokens in arrived:
         term = view_attention(tokens, gain, w_view, w_view_out)
@@ -362,8 +378,11 @@
             ("head", "tok"), split_axis=0, concat_axis=0, tiled=True,
         )
         view_terms.append(term.reshape(n_head, n_tok * run, cols))
-    base = residual_and_cross(hires_tokens, cross_all, w_columns)
-    return add_view(base, view_terms)
+    base = residual_and_cross(head_index, hires_tokens, cross_all, w_columns)
+    layer_out = None
+    for chunk, view_term in enumerate(view_terms):
+        layer_out = add_view(base, view_term, chunk, chunks, layer_out)
+    return layer_out
 
 
 def solution(mesh):

time: 222 us -> 196 us (0.88)
  blocking collectives: 27.6 us -> 0 us
  Pallas kernels: 57.1 us -> 66.8 us
  local copies, waits for them, and re-layouts: 19.9 us -> 11 us
  starting transfers between devices: 23.3 us -> 28.9 us
  waiting for transfers between devices: 77.2 us -> 74.2 us
    all_gather x1, waiting for transfers between devices: 36 us -> 5.13 us  [shards(): cross_all = lax.all_gather(cross_out, 'head', axis=0, tiled=False)]
    all_to_all x1 -> x0, blocking collectives: 27.6 us -> none  [shards(): lax.all_to_all(rows.reshape(n_tok, run, width), 'tok', split_axis=0, conc...]
    ppermute x0 -> x3, waiting for transfers between devices: none -> 20.5 us  [column_blocks(): block = lax.ppermute(block, 'head', pairs)]
    unnamed x30 -> x38, local copies, waits for them, and re-layouts: 14.8 us -> 3.2 us
    all_to_all x2, waiting for transfers between devices: 0.01 us -> 10.3 us  [arrive(): lax.all_to_all(rows.reshape(n_tok, run, width), 'tok', split_axis=0, conc...]
    pallas_call x1, Pallas kernels: 4.48 us -> 9.63 us  [residual_and_cross(): pl.pallas_call(base_kernel, out_shape=jax.ShapeDtypeStruct((tok_rows, col...]
    pallas_call x1 -> x2, Pallas kernels: 3.08 us -> 7.54 us  [add_view(): pl.pallas_call(add_kernel, out_shape=jax.ShapeDtypeStruct((tok_rows, cols...]
    all_to_all x2, starting transfers between devices: 7.07 us -> 11.3 us  [arrive(): lax.all_to_all(rows.reshape(n_tok, run, width), 'tok', split_axis=0, conc...]
  transfers between devices with their start and end apart: 14 -> 17, of which waited for: 7 -> 10; matrix products, arithmetic and copies ran while one was open for 2% -> 4% of each run, Pallas kernels for 24% -> 32%
where the time goes in v1:
time: 196 us; the launch traced here: 195 us
  waiting for transfers between devices  74.2 us (38%)
  Pallas kernels  66.8 us (34%)
  starting transfers between devices  28.9 us (15%)
  between operations  13.3 us (7%)
  local copies, waits for them, and re-layouts  11 us (6%)
    pallas_call x1, Pallas kernels, cross_attention(): pl.pallas_call(cross_kernel, out_shape=jax.ShapeDtypeStruct((tok_rows, co...  26.6 us
    pallas_call x2, Pallas kernels, view_attention(): pl.pallas_call(view_kernel, out_shape=jax.ShapeDtypeStruct((parts, source...  23 us
    ppermute x4, waiting for transfers between devices, ring_chunks(): behind.append(lax.ppermute(behind[-1], 'tok', upward))  21.4 us
    ppermute x3, waiting for transfers between devices, column_blocks(): block = lax.ppermute(block, 'head', pairs)  20.5 us
    all_to_all x2, waiting for transfers between devices, shards(): lax.all_to_all(term.reshape(n_head * n_tok, run, cols), ('head', 'tok'),...  16 us
    all_to_all x2, starting transfers between devices, arrive(): lax.all_to_all(rows.reshape(n_tok, run, width), 'tok', split_axis=0, conc...  11.3 us
    all_to_all x2, waiting for transfers between devices, arrive(): lax.all_to_all(rows.reshape(n_tok, run, width), 'tok', split_axis=0, conc...  10.3 us
    pallas_call x1, Pallas kernels, residual_and_cross(): pl.pallas_call(base_kernel, out_shape=jax.ShapeDtypeStruct((tok_rows, col...  9.63 us
  transfers between devices with their start and end apart: 17, of which 10 were waited for; matrix products, arithmetic and copies ran while one was open for 4% of the time, Pallas kernels for 32%

profile of v1, /device:TPU:0, one launch (start us, length us, event | category | flops | bytes accessed | tf_op | source)
XLA Modules:
  0.0 194.9 jit_solution(16199844753043382112)
XLA Ops:
  6.5 1.9 slice.7
  8.5 0.0 all-gather.6.cloned.1.call-update
  8.5 0.0 all-gather.10.cloned.1.call-start
  8.5 0.7 all-gather.10.cloned.1.call-update
  9.2 0.0 copy-start.8
  9.3 1.5 copy.13
  10.7 0.2 fusion
  10.9 0.5 convolution_convert_fusion.refs_0_
  11.4 3.1 %collective-permute-start.3 = (bf16[256,512]{1,0:T(8,128)(2,1)S(1)}, bf16[256,512]{1,0:T(8,128)(2,1)S(1)}, u32[]{:S(2)}, u32[]{:S(2)}) collective-permute-start(bf16[256,512]{1,0:T(8,128)(2,1)S(1)} %convolution_convert_fusion.refs_0_), channel_id=1, source_target_pairs={{0,2},{2,4},{4,6},{6,7},{7,5},{5,3},{3,1},{1,0},{8,10},{10,12},{12... | collective-permute-start | bytes 786440 | tf_op jit(solution)/shard_map/ppermute | solution.py:318
  14.5 0.0 collective-permute-start
  14.5 6.2 %collective-permute-done.3.refs_7_ = bf16[256,512]{1,0:T(8,128)(2,1)S(1)} collective-permute-done((bf16[256,512]{1,0:T(8,128)(2,1)S(1)}, bf16[256,512]{1,0:T(8,128)(2,1)S(1)}, u32[]{:S(2)}, u32[]{:S(2)}) %collective-permute-start.3) | collective-permute-done | bytes 262176 | tf_op jit(solution)/shard_map/ppermute | solution.py:318
  20.7 1.8 collective-permute-start.4
  22.6 0.2 collective-permute-start.1
  22.8 5.4 %collective-permute-done.4.refs_6_ = bf16[256,512]{1,0:T(8,128)(2,1)S(1)} collective-permute-done((bf16[256,512]{1,0:T(8,128)(2,1)S(1)}, bf16[256,512]{1,0:T(8,128)(2,1)S(1)}, u32[]{:S(2)}, u32[]{:S(2)}) %collective-permute-start.4) | collective-permute-done | bytes 262176 | tf_op jit(solution)/shard_map/ppermute | solution.py:318
  28.2 1.5 collective-permute-start.5
  29.7 0.5 collective-permute-start.2
  30.2 4.6 %collective-permute-done.5.refs_5_ = bf16[256,512]{1,0:T(8,128)(2,1)S(1)} collective-permute-done((bf16[256,512]{1,0:T(8,128)(2,1)S(1)}, bf16[256,512]{1,0:T(8,128)(2,1)S(1)}, u32[]{:S(2)}, u32[]{:S(2)}) %collective-permute-start.5) | collective-permute-done | bytes 262176 | tf_op jit(solution)/shard_map/ppermute | solution.py:318
  34.9 1.2 collective-permute-start.6
  36.1 5.1 %collective-permute-done.6.refs_4_ = bf16[256,512]{1,0:T(8,128)(2,1)S(1)} collective-permute-done((bf16[256,512]{1,0:T(8,128)(2,1)S(1)}, bf16[256,512]{1,0:T(8,128)(2,1)S(1)}, u32[]{:S(2)}, u32[]{:S(2)}) %collective-permute-start.6) | collective-permute-done | bytes 262176 | tf_op jit(solution)/shard_map/ppermute | solution.py:318
  41.2 2.5 %constant_dynamic-slice_fusion.1 = bf16[512,1024]{1,0:T(8,128)(2,1)} fusion(bf16[4096,1024]{1,0:T(8,128)(2,1)} %tokens_ref.1, s32[]{:T(128)S(6)} %select_n.18), kind=kLoop, calls=%fused_computation.13 | loop fusion | bytes 2097156 | tf_op jit(solution)/shard_map/dynamic_slice | solution.py:357
  43.7 5.5 %all-to-all-start = ((bf16[8,64,1024]{2,1,0:T(8,128)(2,1)}), bf16[8,64,1024]{2,1,0:T(8,128)(2,1)S(1)}, u32[]{:S(2)}, u32[]{:S(2)}) async-start(bf16[8,64,1024]{2,1,0:T(8,128)(2,1)} %bitcast.3), calls=%async_computation | async-start | bytes 2097152 | tf_op jit(solution)/shard_map/all_to_all | solution.py:358
  49.2 0.0 all-gather.8.cloned.1.call-start
  49.2 0.7 copy.12.lists_ref
  50.0 26.6 %cross.1 = bf16[4096,256]{1,0:T(8,128)(2,1)} custom-call(s32[32,8]{1,0:T(8,128)} %copy.12.lists_ref, s32[32]{0:T(128)} %counts_ref.1, s32[1]{0:T(128)} %bitcast.1.tok_ref, bf16[4096,1024]{1,0:T(8,128)(2,1)} %tokens_ref.1, f32[1,1024]{1,0:T(1,128)} %bitcast.33, bf16[1024,256]{1,0:T(8,128)(2,1)} %wq_ref.1, bf16[256,512]{1,0:T(8,128)(2,1)} %copy-done.9, ...), custom_call_target="tpu_custom_call" | custom-call | flops 10737418240 | bytes 10485760 | tf_op jit(solution)/shard_map/cross/pallas_call | solution.py:106
  76.6 0.0 all-gather.8.cloned.1.call-update
  76.6 2.7 %constant_dynamic-slice_fusion = bf16[512,1024]{1,0:T(8,128)(2,1)} fusion(bf16[4096,1024]{1,0:T(8,128)(2,1)} %tokens_ref.1, s32[]{:T(128)S(6)} %select_n.23), kind=kLoop, calls=%fused_computation.12 | loop fusion | bytes 2097156 | tf_op jit(solution)/shard_map/dynamic_slice | solution.py:357
  79.3 5.8 %all-to-all-start.1 = ((bf16[8,64,1024]{2,1,0:T(8,128)(2,1)}), bf16[8,64,1024]{2,1,0:T(8,128)(2,1)S(1)}, u32[]{:S(2)}, u32[]{:S(2)}) async-start(bf16[8,64,1024]{2,1,0:T(8,128)(2,1)} %bitcast.9), calls=%async_computation.1 | async-start | bytes 2097152 | tf_op jit(solution)/shard_map/all_to_all | solution.py:358
  85.1 0.0 all-gather.6.cloned.1.call-done.wo_ref
  85.1 0.0 all-gather.10.cloned.1.call-done
  85.2 11.5 %view.3 = bf16[4,8,64,256]{3,2,1,0:T(8,128)(2,1)} custom-call(bf16[8,64,1024]{2,1,0:T(8,128)(2,1)} %copy-done.2, f32[1,1024]{1,0:T(1,128)} %bitcast.34, bf16[4,3,1024,256]{3,2,1,0:T(8,128)(2,1)} %bitcast.31, bf16[4,256,1024]{2,1,0:T(8,128)(2,1)} %all-gather.6.cloned.1.call-done.wo_ref), custom_call_target="tpu_custom_call" | custom-call | flops 4831838208 | bytes 10485760 | tf_op jit(solution)/shard_map/view/pallas_call | solution.py:209
  96.7 10.3 %all-to-all-done.1.tokens_ref = bf16[8,64,1024]{2,1,0:T(8,128)(2,1)S(1)} async-done(((bf16[8,64,1024]{2,1,0:T(8,128)(2,1)}), bf16[8,64,1024]{2,1,0:T(8,128)(2,1)S(1)}, u32[]{:S(2)}, u32[]{:S(2)}) %all-to-all-start.1) | async-done | bytes 1048608 | tf_op jit(solution)/shard_map/all_to_all | solution.py:358
  107.0 3.4 %all-to-all-start.3 = ((bf16[32,64,256]{2,1,0:T(8,128)(2,1)}), bf16[32,64,256]{2,1,0:T(8,128)(2,1)S(1)}, u32[]{:S(2)}, u32[]{:S(2)}) async-start(bf16[32,64,256]{2,1,0:T(8,128)(2,1)} %bitcast.29), calls=%async_computation.3 | async-start | bytes 2097152 | tf_op jit(solution)/shard_map/all_to_all | solution.py:376
  110.4 0.0 slice-start
  110.4 11.5 %view.2 = bf16[4,8,64,256]{3,2,1,0:T(8,128)(2,1)} custom-call(bf16[8,64,1024]{2,1,0:T(8,128)(2,1)} %copy-done.3, f32[1,1024]{1,0:T(1,128)} %bitcast.35, bf16[4,3,1024,256]{3,2,1,0:T(8,128)(2,1)} %bitcast.32, bf16[4,256,1024]{2,1,0:T(8,128)(2,1)} %all-gather.6.cloned.1.call-done.wo_ref), custom_call_target="tpu_custom_call" | custom-call | flops 4831838208 | bytes 10485760 | tf_op jit(solution)/shard_map/view/pallas_call | solution.py:209
  122.0 16.0 %all-to-all-done.3 = bf16[32,64,256]{2,1,0:T(8,128)(2,1)S(1)} async-done(((bf16[32,64,256]{2,1,0:T(8,128)(2,1)}), bf16[32,64,256]{2,1,0:T(8,128)(2,1)S(1)}, u32[]{:S(2)}, u32[]{:S(2)}) %all-to-all-start.3) | async-done | bytes 1048608 | tf_op jit(solution)/shard_map/all_to_all | solution.py:376
  138.0 2.6 %all-to-all-start.2 = ((bf16[32,64,256]{2,1,0:T(8,128)(2,1)}), bf16[32,64,256]{2,1,0:T(8,128)(2,1)S(1)}, u32[]{:S(2)}, u32[]{:S(2)}) async-start(bf16[32,64,256]{2,1,0:T(8,128)(2,1)} %bitcast.28), calls=%async_computation.2 | async-start | bytes 2097152 | tf_op jit(solution)/shard_map/all_to_all | solution.py:376
  140.7 0.7 dynamic-slice_bitcast_fusion
  141.4 0.1 collective-permute-start.7
  141.5 1.7 collective-permute-start.8
  143.2 1.3 collective-permute-start.9
  144.5 16.6 %collective-permute-done.7.refs_1_ = bf16[256,256]{1,0:T(8,128)(2,1)S(1)} collective-permute-done((bf16[256,256]{1,0:T(8,128)(2,1)S(1)}, bf16[256,256]{1,0:T(8,128)(2,1)S(1)}, u32[]{:S(2)}, u32[]{:S(2)}) %collective-permute-start.7) | collective-permute-done | bytes 131104 | tf_op jit(solution)/shard_map/ppermute | solution.py:307
  161.1 0.6 collective-permute-done.8.refs_2_
  161.7 3.4 %collective-permute-done.9.refs_3_ = bf16[256,256]{1,0:T(8,128)(2,1)S(1)} collective-permute-done((bf16[256,256]{1,0:T(8,128)(2,1)S(1)}, bf16[256,256]{1,0:T(8,128)(2,1)S(1)}, u32[]{:S(2)}, u32[]{:S(2)}) %collective-permute-start.9) | collective-permute-done | bytes 131104 | tf_op jit(solution)/shard_map/ppermute | solution.py:307
  165.1 5.1 %all-gather.8.cloned.1.call-done = bf16[16384,256]{1,0:T(8,128)(2,1)} async-done(((bf16[4096,256]{1,0:T(8,128)(2,1)}), bf16[16384,256]{1,0:T(8,128)(2,1)}) %all-gather.8.cloned.1.call-update) | async-done | bytes 8388624 | tf_op jit(solution)/shard_map/all_gather | solution.py:369
  170.2 9.6 %base.1.base_ref = f32[4096,256]{1,0:T(8,128)} custom-call(s32[1]{0:T(128)} %bitcast.index_ref, bf16[4096,1024]{1,0:T(8,128)(2,1)} %tokens_ref.1, bf16[4,4096,256]{2,1,0:T(8,128)(2,1)} %bitcast.23, bf16[256,256]{1,0:T(8,128)(2,1)} %get-tuple-element.34.refs_0_, bf16[256,256]{1,0:T(8,128)(2,1)} %copy-done.5, bf16[256,256]{1,0:T(8,128)(2,1)} %copy-done.6, ...), custom_call_target="tpu_custom_call" | custom-call | flops 2147483648 | bytes 14680064 | tf_op jit(solution)/shard_map/base/pallas_call | solution.py:248
  179.8 3.8 %add.59.refs_0_ = bf16[4096,256]{1,0:T(8,128)(2,1)} custom-call(f32[4096,256]{1,0:T(8,128)} %base.1.base_ref, bf16[4,512,256]{2,1,0:T(8,128)(2,1)} %bitcast.24), custom_call_target="tpu_custom_call" | custom-call | flops 524288 | bytes 4194304 | tf_op jit(solution)/shard_map/add/pallas_call | solution.py:284
  183.6 1.0 copy-done.1
  184.6 3.8 %add.60 = bf16[4096,256]{1,0:T(8,128)(2,1)} custom-call(f32[4096,256]{1,0:T(8,128)} %base.1.base_ref, bf16[4,512,256]{2,1,0:T(8,128)(2,1)} %bitcast.25, bf16[4096,256]{1,0:T(8,128)(2,1)} %add.59.refs_0_), custom_call_target="tpu_custom_call", output_to_operand_aliasing={{}: (2, {})} | custom-call | flops 524288 | bytes 4194304 | tf_op jit(solution)/shard_map/add/pallas_call | solution.py:284
  (42 shorter events, 0.1 us)
Async XLA Ops:
  6.5 4.2 %copy-start.4 = (bf16[256,1024]{1,0:T(8,128)(2,1)S(1)}, bf16[256,1024]{1,0:T(8,128)(2,1)}, u32[]{:S(2)}) copy-start(bf16[256,1024]{1,0:T(8,128)(2,1)} %param.10) | copy-start | bytes 1572868
  6.5 4.4 %copy-start.17 = (f32[1024]{0:T(1024)S(1)}, f32[1024]{0:T(1024)}, u32[]{:S(2)}) copy-start(f32[1024]{0:T(1024)} %param.11) | copy-start | bytes 12292
  6.5 78.6 %all-gather.6.cloned.1.call-start = ((), (), s32[]{:S(2)}) async-start(), calls=%async_computation.4 | async-start | bytes 2621440 | tf_op jit(solution)/shard_map/all_gather | solution.py:348
  8.5 76.7 %all-gather.10.cloned.1.call-start = ((), (), s32[]{:S(2)}) async-start(), calls=%async_computation.6 | async-start | bytes 7864320 | tf_op jit(solution)/shard_map/all_gather | solution.py:343
  9.2 40.0 %copy-start.8 = (s32[32,8]{0,1:T(8,128)S(1)}, s32[32,8]{0,1:T(8,128)}, u32[]{:S(2)}) copy-start(s32[32,8]{0,1:T(8,128)} %param.16) | copy-start | bytes 3076
  11.4 38.5 %copy-start.9 = (bf16[256,512]{1,0:T(8,128)(2,1)}, bf16[256,512]{1,0:T(8,128)(2,1)S(1)}, u32[]{:S(2)}) copy-start(bf16[256,512]{1,0:T(8,128)(2,1)S(1)} %convolution_convert_fusion.refs_0_) | copy-start | bytes 786436
  11.4 9.3 %collective-permute-start.3 = (bf16[256,512]{1,0:T(8,128)(2,1)S(1)}, bf16[256,512]{1,0:T(8,128)(2,1)S(1)}, u32[]{:S(2)}, u32[]{:S(2)}) collective-permute-start(bf16[256,512]{1,0:T(8,128)(2,1)S(1)} %convolution_convert_fusion.refs_0_), channel_id=1, source_target_pairs={{0,2},{2,4},{4,6},{6,7},{7,5},{5,3},{3,1},{1,0},{8,10},{10,12},{12... | collective-permute-start | bytes 786440 | tf_op jit(solution)/shard_map/ppermute | solution.py:318
  14.5 8.0 %collective-permute-start = (bf16[256,512]{1,0:T(8,128)(2,1)S(1)}, bf16[256,512]{1,0:T(8,128)(2,1)S(1)}, u32[]{:S(2)}, u32[]{:S(2)}) collective-permute-start(bf16[256,512]{1,0:T(8,128)(2,1)S(1)} %convolution_convert_fusion.refs_0_), channel_id=1, source_target_pairs={{0,1},{2,0},{4,2},{6,4},{7,6},{5,7},{3,5},{1,3},{8,9},{10,8},{12,1... | collective-permute-start | bytes 786440 | tf_op jit(solution)/shard_map/ppermute | solution.py:320
  20.7 29.2 %copy-start.10 = (bf16[256,512]{1,0:T(8,128)(2,1)}, bf16[256,512]{1,0:T(8,128)(2,1)S(1)}, u32[]{:S(2)}) copy-start(bf16[256,512]{1,0:T(8,128)(2,1)S(1)} %collective-permute-done.3.refs_7_) | copy-start | bytes 786436
  20.7 7.5 %collective-permute-start.4 = (bf16[256,512]{1,0:T(8,128)(2,1)S(1)}, bf16[256,512]{1,0:T(8,128)(2,1)S(1)}, u32[]{:S(2)}, u32[]{:S(2)}) collective-permute-start(bf16[256,512]{1,0:T(8,128)(2,1)S(1)} %collective-permute-done.3.refs_7_), channel_id=1, source_target_pairs={{0,2},{2,4},{4,6},{6,7},{7,5},{5,3},{3,1},{1,0},{8,10},{10,12},{12... | collective-permute-start | bytes 786440 | tf_op jit(solution)/shard_map/ppermute | solution.py:318
  22.6 27.4 %copy-start.11 = (bf16[256,512]{1,0:T(8,128)(2,1)}, bf16[256,512]{1,0:T(8,128)(2,1)S(1)}, u32[]{:S(2)}) copy-start(bf16[256,512]{1,0:T(8,128)(2,1)S(1)} %collective-permute-done.refs_1_) | copy-start | bytes 786436
  22.6 7.2 %collective-permute-start.1 = (bf16[256,512]{1,0:T(8,128)(2,1)S(1)}, bf16[256,512]{1,0:T(8,128)(2,1)S(1)}, u32[]{:S(2)}, u32[]{:S(2)}) collective-permute-start(bf16[256,512]{1,0:T(8,128)(2,1)S(1)} %collective-permute-done.refs_1_), channel_id=1, source_target_pairs={{0,1},{2,0},{4,2},{6,4},{7,6},{5,7},{3,5},{1,3},{8,9},{10,8},{12,1... | collective-permute-start | bytes 786440 | tf_op jit(solution)/shard_map/ppermute | solution.py:320
  28.2 21.7 %copy-start.12 = (bf16[256,512]{1,0:T(8,128)(2,1)}, bf16[256,512]{1,0:T(8,128)(2,1)S(1)}, u32[]{:S(2)}) copy-start(bf16[256,512]{1,0:T(8,128)(2,1)S(1)} %collective-permute-done.4.refs_6_) | copy-start | bytes 786436
  28.2 6.7 %collective-permute-start.5 = (bf16[256,512]{1,0:T(8,128)(2,1)S(1)}, bf16[256,512]{1,0:T(8,128)(2,1)S(1)}, u32[]{:S(2)}, u32[]{:S(2)}) collective-permute-start(bf16[256,512]{1,0:T(8,128)(2,1)S(1)} %collective-permute-done.4.refs_6_), channel_id=1, source_target_pairs={{0,2},{2,4},{4,6},{6,7},{7,5},{5,3},{3,1},{1,0},{8,10},{10,12},{12... | collective-permute-start | bytes 786440 | tf_op jit(solution)/shard_map/ppermute | solution.py:318
  29.7 20.2 %copy-start.13 = (bf16[256,512]{1,0:T(8,128)(2,1)}, bf16[256,512]{1,0:T(8,128)(2,1)S(1)}, u32[]{:S(2)}) copy-start(bf16[256,512]{1,0:T(8,128)(2,1)S(1)} %collective-permute-done.1.refs_2_) | copy-start | bytes 786436
  29.7 6.4 %collective-permute-start.2 = (bf16[256,512]{1,0:T(8,128)(2,1)S(1)}, bf16[256,512]{1,0:T(8,128)(2,1)S(1)}, u32[]{:S(2)}, u32[]{:S(2)}) collective-permute-start(bf16[256,512]{1,0:T(8,128)(2,1)S(1)} %collective-permute-done.1.refs_2_), channel_id=1, source_target_pairs={{0,1},{2,0},{4,2},{6,4},{7,6},{5,7},{3,5},{1,3},{8,9},{10,8},{12,1... | collective-permute-start | bytes 786440 | tf_op jit(solution)/shard_map/ppermute | solution.py:320
  34.9 15.1 %copy-start.14 = (bf16[256,512]{1,0:T(8,128)(2,1)}, bf16[256,512]{1,0:T(8,128)(2,1)S(1)}, u32[]{:S(2)}) copy-start(bf16[256,512]{1,0:T(8,128)(2,1)S(1)} %collective-permute-done.5.refs_5_) | copy-start | bytes 786436
  34.9 6.4 %collective-permute-start.6 = (bf16[256,512]{1,0:T(8,128)(2,1)S(1)}, bf16[256,512]{1,0:T(8,128)(2,1)S(1)}, u32[]{:S(2)}, u32[]{:S(2)}) collective-permute-start(bf16[256,512]{1,0:T(8,128)(2,1)S(1)} %collective-permute-done.5.refs_5_), channel_id=1, source_target_pairs={{0,2},{2,4},{4,6},{6,7},{7,5},{5,3},{3,1},{1,0},{8,10},{10,12},{12... | collective-permute-start | bytes 786440 | tf_op jit(solution)/shard_map/ppermute | solution.py:318
  36.1 13.9 %copy-start.15 = (bf16[256,512]{1,0:T(8,128)(2,1)}, bf16[256,512]{1,0:T(8,128)(2,1)S(1)}, u32[]{:S(2)}) copy-start(bf16[256,512]{1,0:T(8,128)(2,1)S(1)} %collective-permute-done.2.refs_3_) | copy-start | bytes 786436
  41.2 8.7 %copy-start.16 = (bf16[256,512]{1,0:T(8,128)(2,1)}, bf16[256,512]{1,0:T(8,128)(2,1)S(1)}, u32[]{:S(2)}) copy-start(bf16[256,512]{1,0:T(8,128)(2,1)S(1)} %collective-permute-done.6.refs_4_) | copy-start | bytes 786436
  43.7 32.9 %all-to-all-start = ((bf16[8,64,1024]{2,1,0:T(8,128)(2,1)}), bf16[8,64,1024]{2,1,0:T(8,128)(2,1)S(1)}, u32[]{:S(2)}, u32[]{:S(2)}) async-start(bf16[8,64,1024]{2,1,0:T(8,128)(2,1)} %bitcast.3), calls=%async_computation | async-start | bytes 2097152 | tf_op jit(solution)/shard_map/all_to_all | solution.py:358
  49.2 121.0 %all-gather.8.cloned.1.call-start = ((), (), s32[]{:S(2)}) async-start(), calls=%async_computation.5 | async-start | bytes 10485760 | tf_op jit(solution)/shard_map/all_gather | solution.py:369
  76.6 8.6 %copy-start.2 = (bf16[8,64,1024]{2,1,0:T(8,128)(2,1)}, bf16[8,64,1024]{2,1,0:T(8,128)(2,1)S(1)}, u32[]{:S(2)}) copy-start(bf16[8,64,1024]{2,1,0:T(8,128)(2,1)S(1)} %all-to-all-done.tokens_ref) | copy-start | bytes 3145732
  79.3 27.7 %all-to-all-start.1 = ((bf16[8,64,1024]{2,1,0:T(8,128)(2,1)}), bf16[8,64,1024]{2,1,0:T(8,128)(2,1)S(1)}, u32[]{:S(2)}, u32[]{:S(2)}) async-start(bf16[8,64,1024]{2,1,0:T(8,128)(2,1)} %bitcast.9), calls=%async_computation.1 | async-start | bytes 2097152 | tf_op jit(solution)/shard_map/all_to_all | solution.py:358
  107.0 3.4 %copy-start.3 = (bf16[8,64,1024]{2,1,0:T(8,128)(2,1)}, bf16[8,64,1024]{2,1,0:T(8,128)(2,1)S(1)}, u32[]{:S(2)}) copy-start(bf16[8,64,1024]{2,1,0:T(8,128)(2,1)S(1)} %all-to-all-done.1.tokens_ref) | copy-start | bytes 3145732
  107.0 31.0 %all-to-all-start.3 = ((bf16[32,64,256]{2,1,0:T(8,128)(2,1)}), bf16[32,64,256]{2,1,0:T(8,128)(2,1)S(1)}, u32[]{:S(2)}, u32[]{:S(2)}) async-start(bf16[32,64,256]{2,1,0:T(8,128)(2,1)} %bitcast.29), calls=%async_computation.3 | async-start | bytes 2097152 | tf_op jit(solution)/shard_map/all_to_all | solution.py:376
  110.4 30.3 %slice-start = ((bf16[2,256,1024]{2,1,0:T(8,128)(2,1)}), bf16[1,256,1024]{2,1,0:T(8,128)(2,1)S(1)}, s32[]{:S(2)}) async-start(bf16[2,256,1024]{2,1,0:T(8,128)(2,1)} %param.15), calls=%async_computation.7 | async-start | bytes 1048576 | tf_op jit(solution)/shard_map/slice | solution.py:372
  138.0 41.9 %copy-start = (bf16[32,64,256]{2,1,0:T(8,128)(2,1)}, bf16[32,64,256]{2,1,0:T(8,128)(2,1)S(1)}, u32[]{:S(2)}) copy-start(bf16[32,64,256]{2,1,0:T(8,128)(2,1)S(1)} %all-to-all-done.3) | copy-start | bytes 3145732
  138.0 45.6 %all-to-all-start.2 = ((bf16[32,64,256]{2,1,0:T(8,128)(2,1)}), bf16[32,64,256]{2,1,0:T(8,128)(2,1)S(1)}, u32[]{:S(2)}, u32[]{:S(2)}) async-start(bf16[32,64,256]{2,1,0:T(8,128)(2,1)} %bitcast.28), calls=%async_computation.2 | async-start | bytes 2097152 | tf_op jit(solution)/shard_map/all_to_all | solution.py:376
  141.4 19.7 %collective-permute-start.7 = (bf16[256,256]{1,0:T(8,128)(2,1)S(1)}, bf16[256,256]{1,0:T(8,128)(2,1)S(1)}, u32[]{:S(2)}, u32[]{:S(2)}) collective-permute-start(bf16[256,256]{1,0:T(8,128)(2,1)S(1)} %get-tuple-element.33), channel_id=1, source_target_pairs={{0,8},{8,16},{16,24},{24,0},{1,9},{9,17},{17,25},{25,1},{2,10},{10... | collective-permute-start | bytes 393224 | tf_op jit(solution)/shard_map/ppermute | solution.py:307
  141.5 20.2 %collective-permute-start.8 = (bf16[256,256]{1,0:T(8,128)(2,1)S(1)}, bf16[256,256]{1,0:T(8,128)(2,1)S(1)}, u32[]{:S(2)}, u32[]{:S(2)}) collective-permute-start(bf16[256,256]{1,0:T(8,128)(2,1)S(1)} %get-tuple-element.32), channel_id=1, source_target_pairs={{0,16},{8,24},{16,0},{24,8},{1,17},{9,25},{17,1},{25,9},{2,18},{10... | collective-permute-start | bytes 393224 | tf_op jit(solution)/shard_map/ppermute | solution.py:307
  143.2 21.9 %collective-permute-start.9 = (bf16[256,256]{1,0:T(8,128)(2,1)S(1)}, bf16[256,256]{1,0:T(8,128)(2,1)S(1)}, u32[]{:S(2)}, u32[]{:S(2)}) collective-permute-start(bf16[256,256]{1,0:T(8,128)(2,1)S(1)} %get-tuple-element.31), channel_id=1, source_target_pairs={{0,24},{8,0},{16,8},{24,16},{1,25},{9,1},{17,9},{25,17},{2,26},{10... | collective-permute-start | bytes 393224 | tf_op jit(solution)/shard_map/ppermute | solution.py:307
  161.1 9.1 %copy-start.5 = (bf16[256,256]{1,0:T(8,128)(2,1)}, bf16[256,256]{1,0:T(8,128)(2,1)S(1)}, u32[]{:S(2)}) copy-start(bf16[256,256]{1,0:T(8,128)(2,1)S(1)} %collective-permute-done.7.refs_1_) | copy-start | bytes 393220
  161.7 8.5 %copy-start.6 = (bf16[256,256]{1,0:T(8,128)(2,1)}, bf16[256,256]{1,0:T(8,128)(2,1)S(1)}, u32[]{:S(2)}) copy-start(bf16[256,256]{1,0:T(8,128)(2,1)S(1)} %collective-permute-done.8.refs_2_) | copy-start | bytes 393220
  165.1 5.1 %copy-start.7 = (bf16[256,256]{1,0:T(8,128)(2,1)}, bf16[256,256]{1,0:T(8,128)(2,1)S(1)}, u32[]{:S(2)}) copy-start(bf16[256,256]{1,0:T(8,128)(2,1)S(1)} %collective-permute-done.9.refs_3_) | copy-start | bytes 393220
  183.6 1.0 copy-start.1
Sparse Core Ops, SparseCore 0:
  8.9 25.2 all-gather.5
  35.8 46.3 all-gather.9
  83.8 86.3 all-gather.7

commit v2 on v1

--- a/solution.py
+++ b/solution.py
@@ -41,7 +41,7 @@
     return jnp.where(lax.rem(tok, 2) == 0, half, n_tok - 1 - half)
 
 
-def cross_kernel(lists_ref, counts_ref, tok_ref, tokens_ref, gain_ref, wq_ref, *refs):
+def cross_kernel(first_step, lists_ref, counts_ref, tok_ref, tokens_ref, gain_ref, wq_ref, *refs):
     kv_refs = refs[:-4]
     out_ref, k_ref, vt_ref, q_ref = refs[-4:]
     step = pl.program_id(0)
@@ -65,7 +65,7 @@
     q_ref[...] = (f32_dot(normed, wq_ref[...]) * LOG2_SCALE).astype(jnp.bfloat16)
 
     def one_block(local, carry):
-        block = step * per_step + local
+        block = (first_step + step) * per_step + local
         row_start = pl.multiple_of(local * BLOCK, BLOCK)
         count = counts_ref[block]
         first = lists_ref[block, 0]
@@ -96,21 +96,25 @@
     lax.fori_loop(0, per_step, one_block, 0, unroll=True)
 
 
-def cross_attention(hires_tokens, gain, w_cross_q, kv_chunks, block_lists, block_counts):
+def cross_attention(
+    hires_tokens, gain, w_cross_q, kv_chunks, block_lists, block_counts, part, parts
+):
     tok_index = lax.axis_index("tok").reshape(1)
     tok_rows, width = hires_tokens.shape
     cols = w_cross_q.shape[1]
     chunk = kv_chunks[0].shape[0]
     low_rows = chunk * len(kv_chunks)
+    tok_rows = tok_rows // parts
     rows = math.gcd(tok_rows, 4 * BLOCK)
+    first = part * tok_rows // rows
     return pl.pallas_call(
-        cross_kernel,
+        functools.partial(cross_kernel, first),
         out_shape=jax.ShapeDtypeStruct((tok_rows, cols), jnp.bfloat16),
         grid_spec=pltpu.PrefetchScalarGridSpec(
             num_scalar_prefetch=3,
             grid=(tok_rows // rows,),
             in_specs=[
-                pl.BlockSpec((rows, width), lambda i, *_: (i, 0)),
+                pl.BlockSpec((rows, width), lambda i, *_: (first + i, 0)),
                 pl.BlockSpec((1, width), lambda i, *_: (0, 0)),
                 pl.BlockSpec((width, cols), lambda i, *_: (0, 0)),
             ]
@@ -132,9 +136,10 @@
     )(block_lists, block_counts, tok_index, hires_tokens, gain, w_cross_q, *kv_chunks)
 
 
-def view_kernel(tokens_ref, gain_ref, w_ref, wo_ref, out_ref, normed_ref, qkv_ref, mixed_ref):
-    sources, run, width = tokens_ref.shape
-    parts, cols, _ = wo_ref.shape
+def view_kernel(tok_ref, gain_ref, w_ref, wo_ref, *refs):
+    token_refs = refs[:-4]
+    out_ref, normed_ref, qkv_ref, mixed_ref = refs[-4:]
+    parts, sources, run, cols = out_ref.shape
     part_index = pl.program_id(0)
     heads = cols // HD
     rows = sources * run
@@ -145,10 +150,16 @@
     @pl.when(pl.program_id(0) == 0)
     def _():
         gain = gain_ref[...]
-        step = max(1, tile // run)
-        for s in range(0, sources, step):
-            tokens = tokens_ref[s : s + step].reshape(step * run, width)
-            normed_ref[s * run : (s + step) * run] = rms_rows(tokens, gain)
+        if len(token_refs) == 1:
+            step = max(1, tile // run)
+            for s in range(0, sources, step):
+                tokens = token_refs[0][s : s + step].reshape(step * run, gain.shape[1])
+                normed_ref[s * run : (s + step) * run] = rms_rows(tokens, gain)
+        else:
+            for k, token_ref in enumerate(token_refs):
+                source = partner(tok_ref[0], k, sources, -1)
+                start = pl.multiple_of(source * run, run)
+                normed_ref[pl.ds(start, run), :] = rms_rows(token_ref[...], gain)
 
     for start in range(0, rows, tile):
         stop = start + tile
@@ -191,37 +202,41 @@
         step = max(1, tile // run)
         for s in range(0, sources, step):
             rows_of = slice(s * run, (s + step) * run)
-            term = f32_dot(mixed_ref[0, rows_of], wo_ref[0])
-            for g in range(1, parts):
-                term = term + f32_dot(mixed_ref[g, rows_of], wo_ref[g])
-            term = term.astype(jnp.bfloat16)
-            for g in range(parts):
-                out_ref[g, s : s + step] = term[:, g * cols : (g + 1) * cols].reshape(
-                    step, run, cols
-                )
-
-
-def view_attention(tokens, gain, w_view, w_out):
-    sources, run, width = tokens.shape
-    parts = w_view.shape[0]
-    cols = w_view.shape[3]
-    rows = sources * run
+            for column in range(parts):
+                w_rows = slice(column * cols, (column + 1) * cols)
+                term = f32_dot(mixed_ref[0, rows_of], wo_ref[0, 0, w_rows])
+                for g in range(1, parts):
+                    term = term + f32_dot(mixed_ref[g, rows_of], wo_ref[g, 0, w_rows])
+                out_ref[column, s : s + step] = term.astype(jnp.bfloat16).reshape(step, run, cols)
+
+
+def view_attention(tokens, gain, weights, n_tok):
+    run, width = tokens[0].shape[-2:]
+    parts, _, _, cols = weights.shape
+    rows = n_tok * run
+    token_specs = [
+        pl.BlockSpec(block.shape, lambda i, tok, rank=block.ndim: (0,) * rank) for block in tokens
+    ]
+    tok_index = lax.axis_index("tok").reshape(1)
     return pl.pallas_call(
         view_kernel,
-        out_shape=jax.ShapeDtypeStruct((parts, sources, run, cols), jnp.bfloat16),
-        grid=(parts,),
-        in_specs=[
-            pl.BlockSpec((sources, run, width), lambda i: (0, 0, 0)),
-            pl.BlockSpec((1, width), lambda i: (0, 0)),
-            pl.BlockSpec((1, 3, width, cols), lambda i: (i, 0, 0, 0)),
-            pl.BlockSpec((parts, cols, width), lambda i: (0, 0, 0)),
-        ],
-        out_specs=pl.BlockSpec((parts, sources, run, cols), lambda i: (0, 0, 0, 0)),
-        scratch_shapes=[
-            pltpu.VMEM((rows, width), jnp.bfloat16),
-            pltpu.VMEM((rows, 3 * cols), jnp.bfloat16),
-            pltpu.VMEM((parts, rows, cols), jnp.bfloat16),
-        ],
+        out_shape=jax.ShapeDtypeStruct((parts, n_tok, run, cols), jnp.bfloat16),
+        grid_spec=pltpu.PrefetchScalarGridSpec(
+            num_scalar_prefetch=1,
+            grid=(parts,),
+            in_specs=[
+                pl.BlockSpec((1, width), lambda i, tok: (0, 0)),
+                pl.BlockSpec((1, 3, width, cols), lambda i, tok: (i, 0, 0, 0)),
+                pl.BlockSpec((parts, 1, width, cols), lambda i, tok: (0, 3, 0, 0)),
+            ]
+            + token_specs,
+            out_specs=pl.BlockSpec((parts, n_tok, run, cols), lambda i, tok: (0, 0, 0, 0)),
+            scratch_shapes=[
+                pltpu.VMEM((rows, width), jnp.bfloat16),
+                pltpu.VMEM((rows, 3 * cols), jnp.bfloat16),
+                pltpu.VMEM((parts, rows, cols), jnp.bfloat16),
+            ],
+        ),
         compiler_params=pltpu.CompilerParams(vmem_limit_bytes=VMEM_BYTES),
         cost_estimate=pl.CostEstimate(
             flops=2 * rows * (parts * cols * (3 * width + 512) + width * width),
@@ -229,7 +244,7 @@
             transcendentals=parts * rows * 512,
         ),
         name="view",
-    )(tokens, gain, w_view, w_out)
+    )(tok_index, gain, weights, weights, *tokens)
 
 
 def base_kernel(index_ref, tokens_ref, cross_ref, *refs):
@@ -237,14 +252,15 @@
     parts = len(w_refs)
     total = tokens_ref[...].astype(jnp.float32)
     for k, w_ref in enumerate(w_refs):
-        group = lax.rem(index_ref[0] + parts - k, parts)
+        group = partner(index_ref[0], k, parts, -1)
         total = total + f32_dot(cross_ref[group], w_ref[...])
     out_ref[...] = total
 
 
-def residual_and_cross(head_index, hires_tokens, cross_all, w_columns):
+def residual_and_cross(head_index, hires_tokens, cross_all, w_columns, part):
     parts, tok_rows, cols = cross_all.shape
     rows = math.gcd(tok_rows, 512)
+    first = part * tok_rows // rows
     return pl.pallas_call(
         base_kernel,
         out_shape=jax.ShapeDtypeStruct((tok_rows, cols), jnp.float32),
@@ -252,7 +268,7 @@
             num_scalar_prefetch=1,
             grid=(tok_rows // rows,),
             in_specs=[
-                pl.BlockSpec((rows, cols), lambda i, index: (i, index[0])),
+                pl.BlockSpec((rows, cols), lambda i, index: (first + i, index[0])),
                 pl.BlockSpec((parts, rows, cols), lambda i, index: (0, i, 0)),
             ]
             + [pl.BlockSpec((cols, cols), lambda i, index: (0, 0))] * parts,
@@ -268,26 +284,38 @@
     )(head_index.reshape(1), hires_tokens, cross_all, *w_columns)
 
 
-def add_kernel(base_ref, view_ref, *refs):
-    refs[-1][...] = (base_ref[...] + view_ref[0].astype(jnp.float32)).astype(jnp.bfloat16)
-
-
-def add_view(base, view_term, chunk, chunks, earlier):
-    tok_rows, cols = base.shape
+def add_kernel(steps, n_bases, *refs):
+    view_ref, out_ref = refs[n_bases], refs[-1]
+    for part in range(n_bases):
+        @pl.when(lax.div(pl.program_id(0), steps) == part)
+        def _():
+            terms = refs[part][...] + view_ref[0].astype(jnp.float32)
+            out_ref[...] = terms.astype(jnp.bfloat16)
+
+
+def add_view(bases, view_term, chunk, chunks, earlier):
+    cols = bases[0].shape[1]
     n_head, rows, _ = view_term.shape
-    own = pl.BlockSpec((rows, cols), lambda h: (h * chunks + chunk, 0))
-    in_specs = [own, pl.BlockSpec((1, rows, cols), lambda h: (h, 0, 0))]
-    operands = [base, view_term]
+    steps = n_head // len(bases)
+    in_specs = [
+        pl.BlockSpec(
+            (rows, cols),
+            lambda h, part=part: (jnp.clip(h - part * steps, 0, steps - 1) * chunks + chunk, 0),
+        )
+        for part in range(len(bases))
+    ]
+    in_specs.append(pl.BlockSpec((1, rows, cols), lambda h: (h, 0, 0)))
+    operands = [*bases, view_term]
     if earlier is not None:
         in_specs.append(pl.BlockSpec(memory_space=pl.ANY))
         operands.append(earlier)
     return pl.pallas_call(
-        add_kernel,
-        out_shape=jax.ShapeDtypeStruct((tok_rows, cols), jnp.bfloat16),
+        functools.partial(add_kernel, steps, len(bases)),
+        out_shape=jax.ShapeDtypeStruct((n_head * chunks * rows, cols), jnp.bfloat16),
         grid=(n_head,),
         in_specs=in_specs,
-        out_specs=own,
-        input_output_aliases={} if earlier is None else {2: 0},
+        out_specs=pl.BlockSpec((rows, cols), lambda h: (h * chunks + chunk, 0)),
+        input_output_aliases={} if earlier is None else {len(operands) - 1: 0},
         compiler_params=pltpu.CompilerParams(vmem_limit_bytes=VMEM_BYTES),
         cost_estimate=pl.CostEstimate(
             flops=n_head * rows * cols, bytes_accessed=8 * n_head * rows * cols, transcendentals=0
@@ -296,17 +324,17 @@
     )(*operands)
 
 
-def column_blocks(rows_of_w, head_index, n_head):
-    cols = rows_of_w.shape[1] // n_head
-    blocks = []
-    for k in range(n_head):
-        start = lax.rem(head_index + k, n_head) * cols
-        block = lax.dynamic_slice_in_dim(rows_of_w, start, cols, 1)
-        if k:
-            pairs = [(h, (h + k) % n_head) for h in range(n_head)]
-            block = lax.ppermute(block, "head", pairs)
-        blocks.append(block)
-    return blocks
+def partner(index, k, n, sign):
+    if n & (n - 1) == 0:
+        return index ^ k
+    return lax.rem(index + n + sign * k, n) if k else index
+
+
+def exchange(block, axis, k, n):
+    if k == 0:
+        return block
+    pairs = [(i, i ^ k if n & (n - 1) == 0 else (i + k) % n) for i in range(n)]
+    return lax.ppermute(block, axis, pairs)
 
 
 def ring_chunks(own, n_tok):
@@ -338,50 +366,77 @@
     cols = w_cross_q.shape[1]
     quarter = tok_rows // n_head
     head_index = lax.axis_index("head")
+    tok_index = lax.axis_index("tok")
     gain = norm_gain.reshape(1, width)
 
-    w_view = lax.all_gather(w_view_qkv.transpose(1, 0, 2), "head", axis=0, tiled=False)
+    run = quarter // n_tok
+    chunks = 2 if run % 32 == 0 else 1
+    run = run // chunks
+    parts = 2 if n_head % 2 == 0 else 1
+
     low_kv = f32_dot(
         rms_rows(lowres_tokens, norm_gain), w_low_kv.reshape(width, 2 * cols)
     ).astype(jnp.bfloat16)
+    own_weights = jnp.concatenate(
+        [
+            w_view_qkv.transpose(1, 0, 2),
+            w_out[1].reshape(cols, n_head, cols).transpose(1, 0, 2).reshape(1, width, cols),
+        ],
+        axis=0,
+    )
+    weights = lax.all_gather(own_weights, "head", axis=0, tiled=False)
     kv_chunks = ring_chunks(low_kv, n_tok)
-    w_view_out = lax.all_gather(w_out[1], "head", axis=0, tiled=False)
-    kv_chunks, hires_tokens = lax.optimization_barrier((kv_chunks, hires_tokens))
-
-    run = quarter // n_tok
-    chunks = 2 if run % 32 == 0 else 1
-    run = run // chunks
-
-    def arrive(chunk, tokens):
-        start = head_index * quarter + chunk * n_tok * run
-        rows = lax.dynamic_slice_in_dim(tokens, start, n_tok * run, 0)
-        return lax.all_to_all(
-            rows.reshape(n_tok, run, width), "tok", split_axis=0, concat_axis=0, tiled=True
-        )
-
-    arrived = [arrive(0, hires_tokens)]
-    cross_out = cross_attention(
-        hires_tokens, gain, w_cross_q, kv_chunks, block_lists, block_counts
+
+    def rows_for(chunk, place, count):
+        start = head_index * quarter + (chunk * n_tok + place) * run
+        return lax.dynamic_slice_in_dim(hires_tokens, start, count * run, 0)
+
+    first_rows = rows_for(0, 0, n_tok).reshape(n_tok, run, width)
+    later_rows = [
+        [rows_for(chunk, partner(tok_index, k, n_tok, 1), 1) for k in range(n_tok)]
+        for chunk in range(1, chunks)
+    ]
+    w_columns = [
+        lax.dynamic_slice_in_dim(w_out[0], partner(head_index, k, n_head, 1) * cols, cols, 1)
+        for k in range(n_head)
+    ]
+    kv_chunks, first_rows, later_rows, w_columns = lax.optimization_barrier(
+        (kv_chunks, first_rows, later_rows, w_columns)
     )
-    cross_out, arrived, w_out, hires_tokens = lax.optimization_barrier(
-        (cross_out, arrived, w_out, hires_tokens)
-    )
-    cross_all = lax.all_gather(cross_out, "head", axis=0, tiled=False)
-    for chunk in range(1, chunks):
-        arrived.append(arrive(chunk, hires_tokens))
-    w_columns = column_blocks(w_out[0], head_index, n_head)
+
+    arrived = [[lax.all_to_all(first_rows, "tok", split_axis=0, concat_axis=0, tiled=True)]]
+    cross_parts = []
+    for part in range(parts):
+        out = cross_attention(
+            hires_tokens, gain, w_cross_q, kv_chunks, block_lists, block_counts, part, parts
+        )
+        if part == 0:
+            out, later_rows, w_columns, kv_chunks = lax.optimization_barrier(
+                (out, later_rows, w_columns, kv_chunks)
+            )
+            for rows in later_rows:
+                arrived.append([exchange(block, "tok", k, n_tok) for k, block in enumerate(rows)])
+            w_columns = [exchange(block, "head", k, n_head) for k, block in enumerate(w_columns)]
+        out, weights = lax.optimization_barrier((out, weights))
+        cross_parts.append(lax.all_gather(out, "head", axis=0, tiled=False))
+        if part == parts - 1:
+            arrived[0], out = lax.optimization_barrier((arrived[0], out))
     view_terms = []
     for tokens in arrived:
-        term = view_attention(tokens, gain, w_view, w_view_out)
+        term = view_attention(tokens, gain, weights, n_tok)
+        _, cross_parts = lax.optimization_barrier((term, cross_parts))
         term = lax.all_to_all(
             term.reshape(n_head * n_tok, run, cols),
             ("head", "tok"), split_axis=0, concat_axis=0, tiled=True,
         )
         view_terms.append(term.reshape(n_head, n_tok * run, cols))
-    base = residual_and_cross(head_index, hires_tokens, cross_all, w_columns)
+    bases = [
+        residual_and_cross(head_index, hires_tokens, cross_all, w_columns, part)
+        for part, cross_all in enumerate(cross_parts)
+    ]
     layer_out = None
     for chunk, view_term in enumerate(view_terms):
-        layer_out = add_view(base, view_term, chunk, chunks, layer_out)
+        layer_out = add_view(bases, view_term, chunk, chunks, layer_out)
     return layer_out
 
 

time: 196 us -> 228 us (1.16)
  blocking collectives: 0 us -> 29.3 us
  waiting for transfers between devices: 74.2 us -> 65.5 us
  Pallas kernels: 66.8 us -> 71.7 us
  starting transfers between devices: 28.9 us -> 33.1 us
    all_to_all x0 -> x1, blocking collectives: none -> 29.3 us  [shards(): lax.all_to_all(first_rows, 'tok', split_axis=0, concat_axis=0, tiled=True)]
    ppermute x3 -> x10, waiting for transfers between devices: 20.5 us -> 47.8 us  [exchange(): return lax.ppermute(block, axis, pairs)]
    all_to_all x2, waiting for transfers between devices: 16 us -> 0.01 us  [shards(): lax.all_to_all(term.reshape(n_head * n_tok, run, cols), ('head', 'tok'),...]
    ppermute x3 -> x10, starting transfers between devices: 3.12 us -> 15.4 us  [exchange(): return lax.ppermute(block, axis, pairs)]
    all_to_all x2 -> x0, starting transfers between devices: 11.3 us -> none  [arrive(): lax.all_to_all(rows.reshape(n_tok, run, width), 'tok', split_axis=0, conc...]
    all_to_all x2 -> x0, waiting for transfers between devices: 10.3 us -> none  [arrive(): lax.all_to_all(rows.reshape(n_tok, run, width), 'tok', split_axis=0, conc...]
    all_gather x3, waiting for transfers between devices: 5.16 us -> 0.01 us  [the longest x2 0.01 us: shards(): cross_parts.append(lax.all_gather(out, 'head', axis=0, tiled=False))]
    ppermute x4, waiting for transfers between devices: 21.4 us -> 17 us  [ring_chunks(): behind.append(lax.ppermute(behind[-1], 'tok', upward))]
  transfers between devices with their start and end apart: 17 -> 22, of which waited for: 10 -> 11; matrix products, arithmetic and copies ran while one was open for 4% -> 2% of each run, Pallas kernels for 32% -> 30%
where the time goes in v2:
time: 228 us; the launch traced here: 227 us
  Pallas kernels  71.7 us (31%)
  waiting for transfers between devices  65.5 us (29%)
  starting transfers between devices  33.1 us (15%)
  blocking collectives  29.3 us (13%)
  between operations  13.3 us (6%)
  local copies, waits for them, and re-layouts  11.7 us (5%)
    ppermute x10, waiting for transfers between devices, exchange(): return lax.ppermute(block, axis, pairs)  47.8 us
    pallas_call x2, Pallas kernels, cross_attention(): pl.pallas_call(functools.partial(cross_kernel, first), out_shape=jax.Shap...  30.5 us
    all_to_all x1, blocking collectives, shards(): lax.all_to_all(first_rows, 'tok', split_axis=0, concat_axis=0, tiled=True)  29.3 us
    pallas_call x2, Pallas kernels, view_attention(): pl.pallas_call(view_kernel, out_shape=jax.ShapeDtypeStruct((parts, n_tok,...  22.8 us
    ppermute x4, waiting for transfers between devices, ring_chunks(): behind.append(lax.ppermute(behind[-1], 'tok', upward))  17 us
    ppermute x10, starting transfers between devices, exchange(): return lax.ppermute(block, axis, pairs)  15.4 us
    pallas_call x2, Pallas kernels, residual_and_cross(): pl.pallas_call(base_kernel, out_shape=jax.ShapeDtypeStruct((tok_rows, col...  10.6 us
    all_to_all x2, starting transfers between devices, shards(): lax.all_to_all(term.reshape(n_head * n_tok, run, cols), ('head', 'tok'),...  9.27 us
  transfers between devices with their start and end apart: 22, of which 11 were waited for; matrix products, arithmetic and copies ran while one was open for 2% of the time, Pallas kernels for 30%

profile of v2, /device:TPU:0, one launch (start us, length us, event | category | flops | bytes accessed | tf_op | source)
XLA Modules:
  0.0 226.7 jit_solution(6176127220811562226)
XLA Ops:
  6.5 1.4 fusion.6
  8.4 1.5 pad_maximum_fusion
  10.0 1.1 copy-done.3
  11.6 0.5 convolution_convert_fusion.refs_0_
  12.1 3.1 %collective-permute-start.3 = (bf16[256,512]{1,0:T(8,128)(2,1)S(1)}, bf16[256,512]{1,0:T(8,128)(2,1)S(1)}, u32[]{:S(2)}, u32[]{:S(2)}) collective-permute-start(bf16[256,512]{1,0:T(8,128)(2,1)S(1)} %convolution_convert_fusion.refs_0_), channel_id=1, source_target_pairs={{0,2},{2,4},{4,6},{6,7},{7,5},{5,3},{3,1},{1,0},{8,10},{10,12},{12... | collective-permute-start | bytes 786440 | tf_op jit(solution)/shard_map/ppermute | solution.py:346
  15.1 6.2 %collective-permute-done.3.refs_7_ = bf16[256,512]{1,0:T(8,128)(2,1)S(1)} collective-permute-done((bf16[256,512]{1,0:T(8,128)(2,1)S(1)}, bf16[256,512]{1,0:T(8,128)(2,1)S(1)}, u32[]{:S(2)}, u32[]{:S(2)}) %collective-permute-start.3) | collective-permute-done | bytes 262176 | tf_op jit(solution)/shard_map/ppermute | solution.py:346
  21.4 1.8 collective-permute-start.4
  23.4 5.4 %collective-permute-done.4.refs_6_ = bf16[256,512]{1,0:T(8,128)(2,1)S(1)} collective-permute-done((bf16[256,512]{1,0:T(8,128)(2,1)S(1)}, bf16[256,512]{1,0:T(8,128)(2,1)S(1)}, u32[]{:S(2)}, u32[]{:S(2)}) %collective-permute-start.4) | collective-permute-done | bytes 262176 | tf_op jit(solution)/shard_map/ppermute | solution.py:346
  28.9 1.5 collective-permute-start.5
  30.4 0.7 copy.15.lists_ref
  31.0 1.3 constant_dynamic-slice_fusion.8
  32.3 0.6 collective-permute-start.2
  32.9 2.7 %collective-permute-done.5.refs_5_ = bf16[256,512]{1,0:T(8,128)(2,1)} collective-permute-done((bf16[256,512]{1,0:T(8,128)(2,1)S(1)}, bf16[256,512]{1,0:T(8,128)(2,1)}, u32[]{:S(2)}, u32[]{:S(2)}) %collective-permute-start.5) | collective-permute-done | bytes 262176 | tf_op jit(solution)/shard_map/ppermute | solution.py:346
  35.6 1.2 collective-permute-start.6
  36.8 0.7 dynamic-slice_bitcast_fusion
  37.6 2.0 constant_dynamic-slice_fusion
  39.6 2.6 %collective-permute-done.6.refs_4_ = bf16[256,512]{1,0:T(8,128)(2,1)S(1)} collective-permute-done((bf16[256,512]{1,0:T(8,128)(2,1)}, bf16[256,512]{1,0:T(8,128)(2,1)S(1)}, u32[]{:S(2)}, u32[]{:S(2)}) %collective-permute-start.6) | collective-permute-done | bytes 262176 | tf_op jit(solution)/shard_map/ppermute | solution.py:346
  42.2 0.7 copy-done.22
  42.9 15.2 %cross.2 = bf16[2048,256]{1,0:T(8,128)(2,1)} custom-call(s32[32,8]{1,0:T(8,128)} %copy.15.lists_ref, s32[32]{0:T(128)} %counts_ref.3, s32[1]{0:T(128)} %bitcast.1.tok_ref, bf16[4096,1024]{1,0:T(8,128)(2,1)} %tokens_ref.7, f32[1,1024]{1,0:T(1,128)} %bitcast.41, bf16[1024,256]{1,0:T(8,128)(2,1)} %wq_ref.3, bf16[256,512]{1,0:T(8,128)(2,1)} %copy-done.17, ...), custom_call_target="tpu_custom_call" | custom-call | flops 5368709120 | bytes 5242880 | tf_op jit(solution)/shard_map/cross/pallas_call | solution.py:110
  58.1 15.3 %cross.3 = bf16[2048,256]{1,0:T(8,128)(2,1)} custom-call(s32[32,8]{1,0:T(8,128)} %copy.15.lists_ref, s32[32]{0:T(128)} %counts_ref.3, s32[1]{0:T(128)} %bitcast.1.tok_ref, bf16[4096,1024]{1,0:T(8,128)(2,1)} %tokens_ref.7, f32[1,1024]{1,0:T(1,128)} %bitcast.42, bf16[1024,256]{1,0:T(8,128)(2,1)} %wq_ref.3, bf16[256,512]{1,0:T(8,128)(2,1)} %copy-done.17, ...), custom_call_target="tpu_custom_call" | custom-call | flops 5368709120 | bytes 5242880 | tf_op jit(solution)/shard_map/cross/pallas_call | solution.py:110
  73.5 0.7 all-gather.9.cloned.1.call-update
  74.2 29.3 %all_to_all.15.refs_0_ = bf16[8,64,1024]{2,1,0:T(8,128)(2,1)} all-to-all(bf16[8,64,1024]{2,1,0:T(8,128)(2,1)S(1)} %bitcast.36), channel_id=1, replica_groups=mesh['head'=4,'tok'=8] {'tok'}, dimensions={0} | all-to-all | bytes 2097152 | tf_op jit(solution)/shard_map/all_to_all | solution.py:407
  103.4 11.4 %view.3 = bf16[4,8,64,256]{3,2,1,0:T(8,128)(2,1)} custom-call(s32[1]{0:T(128)} %bitcast.1.tok_ref, f32[1,1024]{1,0:T(1,128)} %bitcast.43, bf16[4,4,1024,256]{3,2,1,0:T(8,128)(2,1)} %bitcast.26, bf16[4,4,1024,256]{3,2,1,0:T(8,128)(2,1)} %bitcast.27, bf16[8,64,1024]{2,1,0:T(8,128)(2,1)} %all_to_all.15.refs_0_), custom_call_target="tpu_custom_call" | custom-call | flops 4831838208 | bytes 10485760 | tf_op jit(solution)/shard_map/view/pallas_call | solution.py:221
  114.8 2.9 %all-to-all-start.2 = ((bf16[32,64,256]{2,1,0:T(8,128)(2,1)}), bf16[32,64,256]{2,1,0:T(8,128)(2,1)S(1)}, u32[]{:S(2)}, u32[]{:S(2)}) async-start(bf16[32,64,256]{2,1,0:T(8,128)(2,1)} %bitcast.33), calls=%async_computation.2 | async-start | bytes 2097152 | tf_op jit(solution)/shard_map/all_to_all | solution.py:428
  117.8 1.7 collective-permute-start.7
  119.4 1.5 collective-permute-start.8
  120.9 0.4 collective-permute-start.9
  121.3 2.5 %collective-permute-start.10 = (bf16[64,1024]{1,0:T(8,128)(2,1)S(1)}, bf16[64,1024]{1,0:T(8,128)(2,1)S(1)}, u32[]{:S(2)}, u32[]{:S(2)}) collective-permute-start(bf16[64,1024]{1,0:T(8,128)(2,1)S(1)} %get-tuple-element.91), channel_id=1, source_target_pairs={{0,4},{1,5},{2,6},{3,7},{4,0},{5,1},{6,2},{7,3},{8,12},{9,13},{10,... | collective-permute-start | bytes 393224 | tf_op jit(solution)/shard_map/ppermute | solution.py:337
  123.8 1.5 collective-permute-start.11
  125.3 8.4 %collective-permute-done.7.refs_1_ = bf16[64,1024]{1,0:T(8,128)(2,1)S(1)} collective-permute-done((bf16[64,1024]{1,0:T(8,128)(2,1)S(1)}, bf16[64,1024]{1,0:T(8,128)(2,1)S(1)}, u32[]{:S(2)}, u32[]{:S(2)}) %collective-permute-start.7) | collective-permute-done | bytes 131104 | tf_op jit(solution)/shard_map/ppermute | solution.py:337
  133.7 1.4 collective-permute-start.12
  135.1 3.4 %collective-permute-done.8.refs_2_ = bf16[64,1024]{1,0:T(8,128)(2,1)S(1)} collective-permute-done((bf16[64,1024]{1,0:T(8,128)(2,1)S(1)}, bf16[64,1024]{1,0:T(8,128)(2,1)S(1)}, u32[]{:S(2)}, u32[]{:S(2)}) %collective-permute-start.8) | collective-permute-done | bytes 131104 | tf_op jit(solution)/shard_map/ppermute | solution.py:337
  138.4 4.5 %collective-permute-start.13 = (bf16[64,1024]{1,0:T(8,128)(2,1)S(1)}, bf16[64,1024]{1,0:T(8,128)(2,1)S(1)}, u32[]{:S(2)}, u32[]{:S(2)}) collective-permute-start(bf16[64,1024]{1,0:T(8,128)(2,1)S(1)} %get-tuple-element.94), channel_id=1, source_target_pairs={{0,7},{1,6},{2,5},{3,4},{4,3},{5,2},{6,1},{7,0},{8,15},{9,14},{10,... | collective-permute-start | bytes 393224 | tf_op jit(solution)/shard_map/ppermute | solution.py:337
  143.1 15.2 %collective-permute-done.10.refs_4_ = bf16[64,1024]{1,0:T(8,128)(2,1)S(1)} collective-permute-done((bf16[64,1024]{1,0:T(8,128)(2,1)S(1)}, bf16[64,1024]{1,0:T(8,128)(2,1)S(1)}, u32[]{:S(2)}, u32[]{:S(2)}) %collective-permute-start.10) | collective-permute-done | bytes 131104 | tf_op jit(solution)/shard_map/ppermute | solution.py:337
  158.4 4.3 %collective-permute-done.11.refs_5_ = bf16[64,1024]{1,0:T(8,128)(2,1)S(1)} collective-permute-done((bf16[64,1024]{1,0:T(8,128)(2,1)S(1)}, bf16[64,1024]{1,0:T(8,128)(2,1)S(1)}, u32[]{:S(2)}, u32[]{:S(2)}) %collective-permute-start.11) | collective-permute-done | bytes 131104 | tf_op jit(solution)/shard_map/ppermute | solution.py:337
  162.7 0.6 copy-done.12
  163.4 0.6 copy-done.14
  164.0 11.4 %view.2 = bf16[4,8,64,256]{3,2,1,0:T(8,128)(2,1)} custom-call(s32[1]{0:T(128)} %bitcast.1.tok_ref, f32[1,1024]{1,0:T(1,128)} %bitcast.44, bf16[4,4,1024,256]{3,2,1,0:T(8,128)(2,1)} %bitcast.28, bf16[4,4,1024,256]{3,2,1,0:T(8,128)(2,1)} %bitcast.29, bf16[64,1024]{1,0:T(8,128)(2,1)} %get-tuple-element.87.refs_0_, bf16[64,1024]{1,0:T(8,128)(2,1)} %copy-done.8, ...), custom_call_target="tpu_custom_call" | custom-call | flops 4831838208 | bytes 10485760 | tf_op jit(solution)/shard_map/view/pallas_call | solution.py:221
  175.4 6.3 %all-to-all-start.1 = ((bf16[32,64,256]{2,1,0:T(8,128)(2,1)}), bf16[32,64,256]{2,1,0:T(8,128)(2,1)S(1)}, u32[]{:S(2)}, u32[]{:S(2)}) async-start(bf16[32,64,256]{2,1,0:T(8,128)(2,1)} %bitcast.34), calls=%async_computation.1 | async-start | bytes 2097152 | tf_op jit(solution)/shard_map/all_to_all | solution.py:428
  182.1 1.7 collective-permute-start.15
  183.8 13.3 %collective-permute-done.15.refs_2_ = bf16[256,256]{1,0:T(8,128)(2,1)S(1)} collective-permute-done((bf16[256,256]{1,0:T(8,128)(2,1)S(1)}, bf16[256,256]{1,0:T(8,128)(2,1)S(1)}, u32[]{:S(2)}, u32[]{:S(2)}) %collective-permute-start.15) | collective-permute-done | bytes 131104 | tf_op jit(solution)/shard_map/ppermute | solution.py:337
  197.1 3.0 %collective-permute-done.16.refs_3_ = bf16[256,256]{1,0:T(8,128)(2,1)S(1)} collective-permute-done((bf16[256,256]{1,0:T(8,128)(2,1)S(1)}, bf16[256,256]{1,0:T(8,128)(2,1)S(1)}, u32[]{:S(2)}, u32[]{:S(2)}) %collective-permute-start.16) | collective-permute-done | bytes 131104 | tf_op jit(solution)/shard_map/ppermute | solution.py:337
  200.1 0.7 copy-done.6
  200.8 5.3 %base.2.refs_0_ = f32[2048,256]{1,0:T(8,128)} custom-call(s32[1]{0:T(128)} %bitcast.index_ref, bf16[4096,1024]{1,0:T(8,128)(2,1)} %tokens_ref.7, bf16[4,2048,256]{2,1,0:T(8,128)(2,1)} %bitcast.31, bf16[256,256]{1,0:T(8,128)(2,1)} %get-tuple-element.102.refs_0_, bf16[256,256]{1,0:T(8,128)(2,1)} %copy-done.4, bf16[256,256]{1,0:T(8,128)(2,1)} %copy-done.5, ...), custom_call_target="tpu_custom_call" | custom-call | flops 1073741824 | bytes 7340032 | tf_op jit(solution)/shard_map/base/pallas_call | solution.py:264
  206.1 5.3 %base.3.refs_1_ = f32[2048,256]{1,0:T(8,128)} custom-call(s32[1]{0:T(128)} %bitcast.index_ref, bf16[4096,1024]{1,0:T(8,128)(2,1)} %tokens_ref.7, bf16[4,2048,256]{2,1,0:T(8,128)(2,1)} %bitcast.30, bf16[256,256]{1,0:T(8,128)(2,1)} %get-tuple-element.102.refs_0_, bf16[256,256]{1,0:T(8,128)(2,1)} %copy-done.4, bf16[256,256]{1,0:T(8,128)(2,1)} %copy-done.5, ...), custom_call_target="tpu_custom_call" | custom-call | flops 1073741824 | bytes 7340032 | tf_op jit(solution)/shard_map/base/pallas_call | solution.py:264
  211.4 3.9 %add.133.refs_3_ = bf16[4096,256]{1,0:T(8,128)(2,1)} custom-call(f32[2048,256]{1,0:T(8,128)} %base.2.refs_0_, f32[2048,256]{1,0:T(8,128)} %base.3.refs_1_, bf16[4,512,256]{2,1,0:T(8,128)(2,1)} %bitcast.32), custom_call_target="tpu_custom_call" | custom-call | flops 524288 | bytes 4194304 | tf_op jit(solution)/shard_map/add/pallas_call | solution.py:312
  215.3 1.0 copy-done.1
  216.3 3.9 %add.134 = bf16[4096,256]{1,0:T(8,128)(2,1)} custom-call(f32[2048,256]{1,0:T(8,128)} %base.2.refs_0_, f32[2048,256]{1,0:T(8,128)} %base.3.refs_1_, bf16[4,512,256]{2,1,0:T(8,128)(2,1)} %bitcast.35, bf16[4096,256]{1,0:T(8,128)(2,1)} %add.133.refs_3_), custom_call_target="tpu_custom_call", output_to_operand_aliasing={{}: (3, {})} | custom-call | flops 524288 | bytes 4194304 | tf_op jit(solution)/shard_map/add/pallas_call | solution.py:312
  (66 shorter events, 1.9 us)
Async XLA Ops:
  6.5 1.9 copy-start.2
  6.5 66.9 %all-gather.7.cloned.1.call-start = ((), (), s32[]{:S(2)}) async-start(), calls=%async_computation.3 | async-start | bytes 10485760 | tf_op jit(solution)/shard_map/all_gather | solution.py:387
  9.9 1.2 copy-start.3
  9.9 1.5 copy-start.7
  9.9 1.7 copy-start.15
  9.9 173.8 %all-gather.11.cloned.1.call-start = ((), (), s32[]{:S(2)}) async-start(), calls=%async_computation.5 | async-start | bytes 5242880 | tf_op jit(solution)/shard_map/all_gather | solution.py:421
  11.1 19.2 %copy-start.16 = (s32[32,8]{0,1:T(8,128)S(1)}, s32[32,8]{0,1:T(8,128)}, u32[]{:S(2)}) copy-start(s32[32,8]{0,1:T(8,128)} %param.16) | copy-start | bytes 3076
  12.1 27.5 %copy-start.17 = (bf16[256,512]{1,0:T(8,128)(2,1)}, bf16[256,512]{1,0:T(8,128)(2,1)S(1)}, u32[]{:S(2)}) copy-start(bf16[256,512]{1,0:T(8,128)(2,1)S(1)} %convolution_convert_fusion.refs_0_) | copy-start | bytes 786436
  12.1 9.3 %collective-permute-start.3 = (bf16[256,512]{1,0:T(8,128)(2,1)S(1)}, bf16[256,512]{1,0:T(8,128)(2,1)S(1)}, u32[]{:S(2)}, u32[]{:S(2)}) collective-permute-start(bf16[256,512]{1,0:T(8,128)(2,1)S(1)} %convolution_convert_fusion.refs_0_), channel_id=1, source_target_pairs={{0,2},{2,4},{4,6},{6,7},{7,5},{5,3},{3,1},{1,0},{8,10},{10,12},{12... | collective-permute-start | bytes 786440 | tf_op jit(solution)/shard_map/ppermute | solution.py:346
  15.1 8.1 %collective-permute-start = (bf16[256,512]{1,0:T(8,128)(2,1)S(1)}, bf16[256,512]{1,0:T(8,128)(2,1)S(1)}, u32[]{:S(2)}, u32[]{:S(2)}) collective-permute-start(bf16[256,512]{1,0:T(8,128)(2,1)S(1)} %convolution_convert_fusion.refs_0_), channel_id=1, source_target_pairs={{0,1},{2,0},{4,2},{6,4},{7,6},{5,7},{3,5},{1,3},{8,9},{10,8},{12,1... | collective-permute-start | bytes 786440 | tf_op jit(solution)/shard_map/ppermute | solution.py:348
  21.4 18.2 %copy-start.18 = (bf16[256,512]{1,0:T(8,128)(2,1)}, bf16[256,512]{1,0:T(8,128)(2,1)S(1)}, u32[]{:S(2)}) copy-start(bf16[256,512]{1,0:T(8,128)(2,1)S(1)} %collective-permute-done.3.refs_7_) | copy-start | bytes 786436
  21.4 7.5 %collective-permute-start.4 = (bf16[256,512]{1,0:T(8,128)(2,1)S(1)}, bf16[256,512]{1,0:T(8,128)(2,1)S(1)}, u32[]{:S(2)}, u32[]{:S(2)}) collective-permute-start(bf16[256,512]{1,0:T(8,128)(2,1)S(1)} %collective-permute-done.3.refs_7_), channel_id=1, source_target_pairs={{0,2},{2,4},{4,6},{6,7},{7,5},{5,3},{3,1},{1,0},{8,10},{10,12},{12... | collective-permute-start | bytes 786440 | tf_op jit(solution)/shard_map/ppermute | solution.py:346
  23.2 13.6 %copy-start.19 = (bf16[256,512]{1,0:T(8,128)(2,1)}, bf16[256,512]{1,0:T(8,128)(2,1)S(1)}, u32[]{:S(2)}) copy-start(bf16[256,512]{1,0:T(8,128)(2,1)S(1)} %collective-permute-done.refs_1_) | copy-start | bytes 786436
  23.2 9.1 %collective-permute-start.1 = (bf16[256,512]{1,0:T(8,128)(2,1)S(1)}, bf16[256,512]{1,0:T(8,128)(2,1)}, u32[]{:S(2)}, u32[]{:S(2)}) collective-permute-start(bf16[256,512]{1,0:T(8,128)(2,1)S(1)} %collective-permute-done.refs_1_), channel_id=1, source_target_pairs={{0,1},{2,0},{4,2},{6,4},{7,6},{5,7},{3,5},{1,3},{8,9},{10,8},{12,1... | collective-permute-start | bytes 786440 | tf_op jit(solution)/shard_map/ppermute | solution.py:348
  28.8 8.0 %copy-start.20 = (bf16[256,512]{1,0:T(8,128)(2,1)}, bf16[256,512]{1,0:T(8,128)(2,1)S(1)}, u32[]{:S(2)}) copy-start(bf16[256,512]{1,0:T(8,128)(2,1)S(1)} %collective-permute-done.4.refs_6_) | copy-start | bytes 786436
  28.9 6.8 %collective-permute-start.5 = (bf16[256,512]{1,0:T(8,128)(2,1)S(1)}, bf16[256,512]{1,0:T(8,128)(2,1)}, u32[]{:S(2)}, u32[]{:S(2)}) collective-permute-start(bf16[256,512]{1,0:T(8,128)(2,1)S(1)} %collective-permute-done.4.refs_6_), channel_id=1, source_target_pairs={{0,2},{2,4},{4,6},{6,7},{7,5},{5,3},{3,1},{1,0},{8,10},{10,12},{12... | collective-permute-start | bytes 786440 | tf_op jit(solution)/shard_map/ppermute | solution.py:346
  32.3 7.3 %collective-permute-start.2 = (bf16[256,512]{1,0:T(8,128)(2,1)}, bf16[256,512]{1,0:T(8,128)(2,1)S(1)}, u32[]{:S(2)}, u32[]{:S(2)}) collective-permute-start(bf16[256,512]{1,0:T(8,128)(2,1)} %collective-permute-done.1.refs_2_), channel_id=1, source_target_pairs={{0,1},{2,0},{4,2},{6,4},{7,6},{5,7},{3,5},{1,3},{8,9},{10,8},{12,1... | collective-permute-start | bytes 786440 | tf_op jit(solution)/shard_map/ppermute | solution.py:348
  35.6 6.6 %collective-permute-start.6 = (bf16[256,512]{1,0:T(8,128)(2,1)}, bf16[256,512]{1,0:T(8,128)(2,1)S(1)}, u32[]{:S(2)}, u32[]{:S(2)}) collective-permute-start(bf16[256,512]{1,0:T(8,128)(2,1)} %collective-permute-done.5.refs_5_), channel_id=1, source_target_pairs={{0,2},{2,4},{4,6},{6,7},{7,5},{5,3},{3,1},{1,0},{8,10},{10,12},{12... | collective-permute-start | bytes 786440 | tf_op jit(solution)/shard_map/ppermute | solution.py:346
  39.6 2.6 %copy-start.21 = (bf16[256,512]{1,0:T(8,128)(2,1)}, bf16[256,512]{1,0:T(8,128)(2,1)S(1)}, u32[]{:S(2)}) copy-start(bf16[256,512]{1,0:T(8,128)(2,1)S(1)} %collective-permute-done.2.refs_3_) | copy-start | bytes 786436
  42.2 0.7 copy-start.22
  73.4 110.3 %all-gather.9.cloned.1.call-start = ((), (), s32[]{:S(2)}) async-start(), calls=%async_computation.4 | async-start | bytes 5242880 | tf_op jit(solution)/shard_map/all_gather | solution.py:421
  114.8 60.6 %all-to-all-start.2 = ((bf16[32,64,256]{2,1,0:T(8,128)(2,1)}), bf16[32,64,256]{2,1,0:T(8,128)(2,1)S(1)}, u32[]{:S(2)}, u32[]{:S(2)}) async-start(bf16[32,64,256]{2,1,0:T(8,128)(2,1)} %bitcast.33), calls=%async_computation.2 | async-start | bytes 2097152 | tf_op jit(solution)/shard_map/all_to_all | solution.py:428
  117.8 15.9 %collective-permute-start.7 = (bf16[64,1024]{1,0:T(8,128)(2,1)S(1)}, bf16[64,1024]{1,0:T(8,128)(2,1)S(1)}, u32[]{:S(2)}, u32[]{:S(2)}) collective-permute-start(bf16[64,1024]{1,0:T(8,128)(2,1)S(1)} %get-tuple-element.88), channel_id=1, source_target_pairs={{0,1},{1,0},{2,3},{3,2},{4,5},{5,4},{6,7},{7,6},{8,9},{9,8},{10,11... | collective-permute-start | bytes 393224 | tf_op jit(solution)/shard_map/ppermute | solution.py:337
  119.4 19.0 %collective-permute-start.8 = (bf16[64,1024]{1,0:T(8,128)(2,1)S(1)}, bf16[64,1024]{1,0:T(8,128)(2,1)S(1)}, u32[]{:S(2)}, u32[]{:S(2)}) collective-permute-start(bf16[64,1024]{1,0:T(8,128)(2,1)S(1)} %get-tuple-element.89), channel_id=1, source_target_pairs={{0,2},{1,3},{2,0},{3,1},{4,6},{5,7},{6,4},{7,5},{8,10},{9,11},{10,... | collective-permute-start | bytes 393224 | tf_op jit(solution)/shard_map/ppermute | solution.py:337
  120.9 22.2 %collective-permute-start.9 = (bf16[64,1024]{1,0:T(8,128)(2,1)S(1)}, bf16[64,1024]{1,0:T(8,128)(2,1)S(1)}, u32[]{:S(2)}, u32[]{:S(2)}) collective-permute-start(bf16[64,1024]{1,0:T(8,128)(2,1)S(1)} %get-tuple-element.90), channel_id=1, source_target_pairs={{0,3},{1,2},{2,1},{3,0},{4,7},{5,6},{6,5},{7,4},{8,11},{9,10},{10,... | collective-permute-start | bytes 393224 | tf_op jit(solution)/shard_map/ppermute | solution.py:337
  121.3 37.0 %collective-permute-start.10 = (bf16[64,1024]{1,0:T(8,128)(2,1)S(1)}, bf16[64,1024]{1,0:T(8,128)(2,1)S(1)}, u32[]{:S(2)}, u32[]{:S(2)}) collective-permute-start(bf16[64,1024]{1,0:T(8,128)(2,1)S(1)} %get-tuple-element.91), channel_id=1, source_target_pairs={{0,4},{1,5},{2,6},{3,7},{4,0},{5,1},{6,2},{7,3},{8,12},{9,13},{10,... | collective-permute-start | bytes 393224 | tf_op jit(solution)/shard_map/ppermute | solution.py:337
  123.8 38.8 %collective-permute-start.11 = (bf16[64,1024]{1,0:T(8,128)(2,1)S(1)}, bf16[64,1024]{1,0:T(8,128)(2,1)S(1)}, u32[]{:S(2)}, u32[]{:S(2)}) collective-permute-start(bf16[64,1024]{1,0:T(8,128)(2,1)S(1)} %get-tuple-element.92), channel_id=1, source_target_pairs={{0,5},{1,4},{2,7},{3,6},{4,1},{5,0},{6,3},{7,2},{8,13},{9,12},{10,... | collective-permute-start | bytes 393224 | tf_op jit(solution)/shard_map/ppermute | solution.py:337
  133.7 29.0 %copy-start.8 = (bf16[64,1024]{1,0:T(8,128)(2,1)}, bf16[64,1024]{1,0:T(8,128)(2,1)S(1)}, u32[]{:S(2)}) copy-start(bf16[64,1024]{1,0:T(8,128)(2,1)S(1)} %collective-permute-done.7.refs_1_) | copy-start | bytes 393220
  133.7 28.9 %collective-permute-start.12 = (bf16[64,1024]{1,0:T(8,128)(2,1)S(1)}, bf16[64,1024]{1,0:T(8,128)(2,1)S(1)}, u32[]{:S(2)}, u32[]{:S(2)}) collective-permute-start(bf16[64,1024]{1,0:T(8,128)(2,1)S(1)} %get-tuple-element.93), channel_id=1, source_target_pairs={{0,6},{1,7},{2,4},{3,5},{4,2},{5,3},{6,0},{7,1},{8,14},{9,15},{10,... | collective-permute-start | bytes 393224 | tf_op jit(solution)/shard_map/ppermute | solution.py:337
  138.4 24.3 %copy-start.9 = (bf16[64,1024]{1,0:T(8,128)(2,1)}, bf16[64,1024]{1,0:T(8,128)(2,1)S(1)}, u32[]{:S(2)}) copy-start(bf16[64,1024]{1,0:T(8,128)(2,1)S(1)} %collective-permute-done.8.refs_2_) | copy-start | bytes 393220
  138.4 24.2 %collective-permute-start.13 = (bf16[64,1024]{1,0:T(8,128)(2,1)S(1)}, bf16[64,1024]{1,0:T(8,128)(2,1)S(1)}, u32[]{:S(2)}, u32[]{:S(2)}) collective-permute-start(bf16[64,1024]{1,0:T(8,128)(2,1)S(1)} %get-tuple-element.94), channel_id=1, source_target_pairs={{0,7},{1,6},{2,5},{3,4},{4,3},{5,2},{6,1},{7,0},{8,15},{9,14},{10,... | collective-permute-start | bytes 393224 | tf_op jit(solution)/shard_map/ppermute | solution.py:337
  143.1 19.5 %copy-start.10 = (bf16[64,1024]{1,0:T(8,128)(2,1)}, bf16[64,1024]{1,0:T(8,128)(2,1)S(1)}, u32[]{:S(2)}) copy-start(bf16[64,1024]{1,0:T(8,128)(2,1)S(1)} %collective-permute-done.9.refs_3_) | copy-start | bytes 393220
  158.4 4.3 %copy-start.11 = (bf16[64,1024]{1,0:T(8,128)(2,1)}, bf16[64,1024]{1,0:T(8,128)(2,1)S(1)}, u32[]{:S(2)}) copy-start(bf16[64,1024]{1,0:T(8,128)(2,1)S(1)} %collective-permute-done.10.refs_4_) | copy-start | bytes 393220
  162.6 0.6 copy-start.12
  162.7 0.7 copy-start.13
  163.4 0.7 copy-start.14
  175.4 30.7 %copy-start = (bf16[32,64,256]{2,1,0:T(8,128)(2,1)}, bf16[32,64,256]{2,1,0:T(8,128)(2,1)S(1)}, u32[]{:S(2)}) copy-start(bf16[32,64,256]{2,1,0:T(8,128)(2,1)S(1)} %all-to-all-done.2) | copy-start | bytes 3145732
  175.4 39.9 %all-to-all-start.1 = ((bf16[32,64,256]{2,1,0:T(8,128)(2,1)}), bf16[32,64,256]{2,1,0:T(8,128)(2,1)S(1)}, u32[]{:S(2)}, u32[]{:S(2)}) async-start(bf16[32,64,256]{2,1,0:T(8,128)(2,1)} %bitcast.34), calls=%async_computation.1 | async-start | bytes 2097152 | tf_op jit(solution)/shard_map/all_to_all | solution.py:428
  181.8 2.0 collective-permute-start.14
  182.1 15.0 %collective-permute-start.15 = (bf16[256,256]{1,0:T(8,128)(2,1)S(1)}, bf16[256,256]{1,0:T(8,128)(2,1)S(1)}, u32[]{:S(2)}, u32[]{:S(2)}) collective-permute-start(bf16[256,256]{1,0:T(8,128)(2,1)S(1)} %get-tuple-element.104), channel_id=1, source_target_pairs={{0,16},{8,24},{16,0},{24,8},{1,17},{9,25},{17,1},{25,9},{2,18},{10... | collective-permute-start | bytes 393224 | tf_op jit(solution)/shard_map/ppermute | solution.py:337
  183.8 16.4 %collective-permute-start.16 = (bf16[256,256]{1,0:T(8,128)(2,1)S(1)}, bf16[256,256]{1,0:T(8,128)(2,1)S(1)}, u32[]{:S(2)}, u32[]{:S(2)}) collective-permute-start(bf16[256,256]{1,0:T(8,128)(2,1)S(1)} %get-tuple-element.105), channel_id=1, source_target_pairs={{0,24},{8,16},{16,8},{24,0},{1,25},{9,17},{17,9},{25,1},{2,26},{10... | collective-permute-start | bytes 393224 | tf_op jit(solution)/shard_map/ppermute | solution.py:337
  183.8 16.3 %copy-start.4 = (bf16[256,256]{1,0:T(8,128)(2,1)}, bf16[256,256]{1,0:T(8,128)(2,1)S(1)}, u32[]{:S(2)}) copy-start(bf16[256,256]{1,0:T(8,128)(2,1)S(1)} %collective-permute-done.14.refs_1_) | copy-start | bytes 393220
  197.1 3.0 %copy-start.5 = (bf16[256,256]{1,0:T(8,128)(2,1)}, bf16[256,256]{1,0:T(8,128)(2,1)S(1)}, u32[]{:S(2)}) copy-start(bf16[256,256]{1,0:T(8,128)(2,1)S(1)} %collective-permute-done.15.refs_2_) | copy-start | bytes 393220
  200.1 0.7 copy-start.6
  215.3 1.0 copy-start.1
Sparse Core Ops, SparseCore 0:
  10.1 60.9 all-gather.6
  73.5 35.4 all-gather.10
  110.6 45.1 all-gather.8

commit v3 on v0

v3 whole, which is shorter than its diff:
```python
import functools
import math

import jax
import jax.numpy as jnp
from jax import lax
from jax.experimental import pallas as pl
from jax.experimental.pallas import tpu as pltpu
from jax.sharding import PartitionSpec as P

HD = 128
VIEWS = 8
BLOCK = 128
LOG2_SCALE = math.log2(math.e) / math.sqrt(HD)
VMEM_BYTES = 60 * 1024 * 1024
CONTRACT_LAST = (((1,), (1,)), ((), ()))


def rms_rows(row_block, norm_gain):
    values = row_block.astype(jnp.float32)
    factor = lax.rsqrt(jnp.mean(values * values, axis=-1, keepdims=True) + 1e-06)
    return (values * factor * norm_gain).astype(jnp.bfloat16)


def f32_dot(left, right):
    return jnp.dot(left, right, preferred_element_type=jnp.float32)


def block_diagonal(tiles):
    rows = []
    for index, tile in enumerate(tiles):
        zero = jnp.zeros_like(tile)
        rows.append(
            jnp.concatenate([tile if k == index else zero for k in range(len(tiles))], axis=1)
        )
    return jnp.concatenate(rows, axis=0)


def ring_place(tok, n_tok):
    half = lax.div(tok, 2)
    return jnp.where(lax.rem(tok, 2) == 0, half, n_tok - 1 - half)


def cross_kernel(
    first_step, lists_ref, counts_ref, tok_ref, tokens_ref, gain_ref, wq_ref, wo_ref, *refs
):
    kv_refs = refs[:-5]
    out_ref, k_ref, vt_ref, q_ref, mixed_ref = refs[-5:]
    step = pl.program_id(0)
    rows, cols = mixed_ref.shape
    heads = cols // HD
    per_step = rows // BLOCK
    listed = lists_ref.shape[1]

    @pl.when(step == 0)
    def _():
        n_tok = len(kv_refs)
        for offset, kv_ref in enumerate(kv_refs):
            chunk = kv_ref.shape[0]
            place = lax.rem(ring_place(tok_ref[0], n_tok) + offset, n_tok)
            home = jnp.where(place < (n_tok + 1) // 2, 2 * place, 2 * (n_tok - 1 - place) + 1)
            start = pl.multiple_of(home * chunk, BLOCK)
            k_ref[pl.ds(start, chunk), :] = kv_ref[:, :cols]
            vt_ref[:, pl.ds(start, chunk)] = kv_ref[:, cols:].T

    normed = rms_rows(tokens_ref[...], gain_ref[...])
    q_ref[...] = (f32_dot(normed, wq_ref[...]) * LOG2_SCALE).astype(jnp.bfloat16)

    def one_block(local, carry):
        block = (first_step + step) * per_step + local
        row_start = pl.multiple_of(local * BLOCK, BLOCK)
        count = counts_ref[block]
        first = lists_ref[block, 0]
        starts = [
            pl.multiple_of(jnp.where(j < count, lists_ref[block, j], first) * BLOCK, BLOCK)
            for j in range(listed)
        ]
        query = block_diagonal(
            [q_ref[pl.ds(row_start, BLOCK), h * HD : (h + 1) * HD] for h in range(heads)]
        )
        keys = jnp.concatenate([k_ref[pl.ds(s, BLOCK), :] for s in starts], axis=0)
        scores = lax.dot_general(keys, query, CONTRACT_LAST, preferred_element_type=jnp.float32)
        top = jnp.max(scores, axis=0, keepdims=True)
        weights = []
        total = jnp.zeros_like(top)
        for j in range(listed):
            shift = top + jnp.where(j < count, 0.0, 1e30)
            weight = jnp.exp2(scores[j * BLOCK : (j + 1) * BLOCK] - shift)
            total = total + jnp.sum(weight, axis=0, keepdims=True)
            weights.append(weight.astype(jnp.bfloat16))
        values_t = jnp.concatenate([vt_ref[:, pl.ds(s, BLOCK)] for s in starts], axis=1)
        mixed_t = f32_dot(values_t, jnp.concatenate(weights, axis=0)) / total
        for h in range(heads):
            part = slice(h * HD, (h + 1) * HD)
            mixed_ref[pl.ds(row_start, BLOCK), part] = mixed_t[part, part].T.astype(jnp.bfloat16)
        return carry

    lax.fori_loop(0, per_step, one_block, 0, unroll=True)
    out_ref[...] = f32_dot(mixed_ref[...], wo_ref[0]).astype(jnp.bfloat16)


def cross_attention(
    hires_tokens, gain, w_cross_q, w_out, kv_chunks, block_lists, block_counts, part, parts
):
    tok_index = lax.axis_index("tok").reshape(1)
    tok_rows, width = hires_tokens.shape
    cols = w_cross_q.shape[1]
    chunk = kv_chunks[0].shape[0]
    low_rows = chunk * len(kv_chunks)
    tok_rows = tok_rows // parts
    rows = math.gcd(tok_rows, 4 * BLOCK)
    first = part * tok_rows // rows
    return pl.pallas_call(
        functools.partial(cross_kernel, first),
        out_shape=jax.ShapeDtypeStruct((tok_rows, width), jnp.bfloat16),
        grid_spec=pltpu.PrefetchScalarGridSpec(
            num_scalar_prefetch=3,
            grid=(tok_rows // rows,),
            in_specs=[
                pl.BlockSpec((rows, width), lambda i, *_: (first + i, 0)),
                pl.BlockSpec((1, width), lambda i, *_: (0, 0)),
                pl.BlockSpec((width, cols), lambda i, *_: (0, 0)),
                pl.BlockSpec((1, cols, width), lambda i, *_: (0, 0, 0)),
            ]
            + [pl.BlockSpec((chunk, 2 * cols), lambda i, *_: (0, 0)) for _ in kv_chunks],
            out_specs=pl.BlockSpec((rows, width), lambda i, *_: (i, 0)),
            scratch_shapes=[
                pltpu.VMEM((low_rows, cols), jnp.bfloat16),
                pltpu.VMEM((cols, low_rows), jnp.bfloat16),
                pltpu.VMEM((rows, cols), jnp.bfloat16),
                pltpu.VMEM((rows, cols), jnp.bfloat16),
            ],
        ),
        compiler_params=pltpu.CompilerParams(vmem_limit_bytes=VMEM_BYTES),
        cost_estimate=pl.CostEstimate(
            flops=2 * tok_rows * cols * (2 * width + 2 * block_lists.shape[1] * BLOCK * 2),
            bytes_accessed=4 * tok_rows * width,
            transcendentals=tok_rows * block_lists.shape[1] * BLOCK * (cols // HD),
        ),
        name="cross",
    )(block_lists, block_counts, tok_index, hires_tokens, gain, w_cross_q, w_out, *kv_chunks)


def view_kernel(
    tokens_ref, gain_ref, w_ref, wo_ref, out_ref, normed_ref, qkv_ref, mixed_ref
):
    parts, sources, run, cols = out_ref.shape
    part_index = pl.program_id(0)
    heads = cols // HD
    rows = sources * run
    pixels = rows // VIEWS
    group = math.gcd(pixels, 32)
    tile = math.gcd(rows, 256)

    @pl.when(pl.program_id(0) == 0)
    def _():
        gain = gain_ref[...]
        step = max(1, tile // run)
        for s in range(0, sources, step):
            tokens = tokens_ref[s : s + step].reshape(step * run, gain.shape[1])
            normed_ref[s * run : (s + step) * run] = rms_rows(tokens, gain)

    for start in range(0, rows, tile):
        stop = start + tile
        tokens = normed_ref[start:stop]
        for k in range(3):
            projected = f32_dot(tokens, w_ref[0, k])
            if k == 0:
                projected = projected * LOG2_SCALE
            qkv_ref[start:stop, k * cols : (k + 1) * cols] = projected.astype(jnp.bfloat16)
    size = VIEWS * group
    row_pixel = lax.broadcasted_iota(jnp.int32, (size, size), 0) % group
    col_pixel = lax.broadcasted_iota(jnp.int32, (size, size), 1) % group
    same = row_pixel == col_pixel

    def gathered(first, column):
        part = slice(column, column + HD)
        return jnp.concatenate(
            [qkv_ref[v * pixels + first : v * pixels + first + group, part] for v in range(VIEWS)],
            axis=0,
        )

    for first in range(0, pixels, group):
        for h in range(heads):
            query = gathered(first, h * HD)
            key = gathered(first, cols + h * HD)
            value = gathered(first, 2 * cols + h * HD)
            scores = lax.dot_general(query, key, CONTRACT_LAST, preferred_element_type=jnp.float32)
            scores = jnp.where(same, scores, -1e30)
            weight = jnp.exp2(scores - jnp.max(scores, axis=1, keepdims=True))
            total = jnp.sum(weight, axis=1, keepdims=True)
            mixed = (f32_dot(weight.astype(jnp.bfloat16), value) / total).astype(jnp.bfloat16)
            for v in range(VIEWS):
                rows_of = slice(v * pixels + first, v * pixels + first + group)
                mixed_ref[part_index, rows_of, h * HD : (h + 1) * HD] = (
                    mixed[v * group : (v + 1) * group]
                )

    @pl.when(part_index == parts - 1)
    def _():
        step = max(1, tile // run)
        for s in range(0, sources, step):
            rows_of = slice(s * run, (s + step) * run)
            for column in range(parts):
                w_rows = slice(column * cols, (column + 1) * cols)
                term = f32_dot(mixed_ref[0, rows_of], wo_ref[0, 0, w_rows])
                for g in range(1, parts):
                    term = term + f32_dot(mixed_ref[g, rows_of], wo_ref[g, 0, w_rows])
                out_ref[column, s : s + step] = term.astype(jnp.bfloat16).reshape(step, run, cols)


def view_attention(tokens, gain, weights):
    n_tok, run, width = tokens.shape
    parts, _, _, cols = weights.shape
    rows = n_tok * run
    return pl.pallas_call(
        view_kernel,
        out_shape=jax.ShapeDtypeStruct((parts, n_tok, run, cols), jnp.bfloat16),
        grid=(parts,),
        in_specs=[
            pl.BlockSpec((n_tok, run, width), lambda i: (0, 0, 0)),
            pl.BlockSpec((1, width), lambda i: (0, 0)),
            pl.BlockSpec((1, 3, width, cols), lambda i: (i, 0, 0, 0)),
            pl.BlockSpec((parts, 1, width, cols), lambda i: (0, 3, 0, 0)),
        ],
        out_specs=pl.BlockSpec((parts, n_tok, run, cols), lambda i: (0, 0, 0, 0)),
        scratch_shapes=[
            pltpu.VMEM((rows, width), jnp.bfloat16),
            pltpu.VMEM((rows, 3 * cols), jnp.bfloat16),
            pltpu.VMEM((parts, rows, cols), jnp.bfloat16),
        ],
        compiler_params=pltpu.CompilerParams(vmem_limit_bytes=VMEM_BYTES),
        cost_estimate=pl.CostEstimate(
            flops=2 * rows * (parts * cols * (3 * width + 512) + width * width),
            bytes_accessed=2 * (2 * rows * width + 4 * parts * width * cols),
            transcendentals=parts * rows * 512,
        ),
        name="view",
    )(tokens, gain, weights, weights)


def add_kernel(chunks, steps, n_parts, index_ref, tokens_ref, *refs):
    cross_refs, view_refs, out_ref = refs[:n_parts], refs[n_parts:-1], refs[-1]
    h, c = pl.program_id(0), pl.program_id(1)
    for part in range(n_parts):
        for chunk in range(chunks):
            @pl.when((lax.div(h, steps) == part) & (c == chunk))
            def _():
                terms = cross_refs[part][...].astype(jnp.float32)
                terms = terms + view_refs[chunk][0].astype(jnp.float32)
                out_ref[...] = (tokens_ref[...].astype(jnp.float32) + terms).astype(jnp.bfloat16)


def add_terms(head_index, hires_tokens, cross_terms, view_terms):
    cols = cross_terms[0].shape[1]
    n_head, rows, _ = view_terms[0].shape
    chunks, n_parts = len(view_terms), len(cross_terms)
    steps = n_head // n_parts
    cross_specs = [
        pl.BlockSpec(
            (rows, cols),
            lambda h, c, index, part=part: (
                jnp.clip(h * chunks + c - part * steps * chunks, 0, steps * chunks - 1), 0
            ),
        )
        for part in range(n_parts)
    ]
    view_spec = pl.BlockSpec((1, rows, cols), lambda h, c, index: (h, 0, 0))
    return pl.pallas_call(
        functools.partial(add_kernel, chunks, steps, n_parts),
        out_shape=jax.ShapeDtypeStruct((n_head * chunks * rows, cols), jnp.bfloat16),
        grid_spec=pltpu.PrefetchScalarGridSpec(
            num_scalar_prefetch=1,
            grid=(n_head, chunks),
            in_specs=[pl.BlockSpec((rows, cols), lambda h, c, index: (h * chunks + c, index[0]))]
            + cross_specs
            + [view_spec] * chunks,
            out_specs=pl.BlockSpec((rows, cols), lambda h, c, index: (h * chunks + c, 0)),
        ),
        compiler_params=pltpu.CompilerParams(vmem_limit_bytes=VMEM_BYTES),
        cost_estimate=pl.CostEstimate(
            flops=2 * n_head * chunks * rows * cols,
            bytes_accessed=8 * n_head * chunks * rows * cols,
            transcendentals=0,
        ),
        name="add",
    )(head_index.reshape(1), hires_tokens, *cross_terms, *view_terms)


def ring_chunks(own, n_tok):
    order = list(range(0, n_tok, 2)) + list(range(1, n_tok, 2))[::-1]
    upward = [(order[p], order[(p + 1) % n_tok]) for p in range(n_tok)]
    downward = [(order[p], order[p - 1]) for p in range(n_tok)]
    behind, ahead = [own], [own]
    for step in range(n_tok // 2):
        behind.append(lax.ppermute(behind[-1], "tok", upward))
        if step < (n_tok - 1) // 2:
            ahead.append(lax.ppermute(ahead[-1], "tok", downward))
    return ahead + behind[:0:-1]


def shards(
    n_head,
    n_tok,
    hires_tokens,
    lowres_tokens,
    norm_gain,
    w_cross_q,
    w_low_kv,
    w_view_qkv,
    w_out,
    block_lists,
    block_counts,
):
    tok_rows, width = hires_tokens.shape
    cols = w_cross_q.shape[1]
    quarter = tok_rows // n_head
    head_index = lax.axis_index("head")
    gain = norm_gain.reshape(1, width)

    run = quarter // n_tok
    chunks = 2 if run % 32 == 0 else 1
    run = run // chunks
    parts = 2 if n_head % 2 == 0 else 1

    low_kv = f32_dot(
        rms_rows(lowres_tokens, norm_gain), w_low_kv.reshape(width, 2 * cols)
    ).astype(jnp.bfloat16)
    own_weights = jnp.concatenate(
        [
            w_view_qkv.transpose(1, 0, 2),
            w_out[1].reshape(cols, n_head, cols).transpose(1, 0, 2).reshape(1, width, cols),
        ],
        axis=0,
    )
    weights = lax.all_gather(own_weights, "head", axis=0, tiled=False)
    kv_chunks = ring_chunks(low_kv, n_tok)

    rows_of_chunk = [
        lax.dynamic_slice_in_dim(
            hires_tokens, head_index * quarter + chunk * n_tok * run, n_tok * run, 0
        ).reshape(n_tok, run, width)
        for chunk in range(chunks)
    ]
    kv_chunks, rows_of_chunk = lax.optimization_barrier((kv_chunks, rows_of_chunk))

    def arrive(rows):
        return lax.all_to_all(rows, "tok", split_axis=0, concat_axis=0, tiled=True)

    arrived = [arrive(rows_of_chunk[0])]
    partials = []
    for part in range(parts):
        partials.append(
            cross_attention(
                hires_tokens, gain, w_cross_q, w_out, kv_chunks, block_lists, block_counts,
                part, parts,
            )
        )
    partials, arrived, rows_of_chunk = lax.optimization_barrier((partials, arrived, rows_of_chunk))
    arrived.extend(arrive(rows) for rows in rows_of_chunk[1:])
    partials, weights = lax.optimization_barrier((partials, weights))
    cross_terms = [
        lax.psum_scatter(partial, "head", scatter_dimension=1, tiled=True) for partial in partials
    ]
    view_terms = []
    for tokens in arrived:
        term = view_attention(tokens, gain, weights)
        term = lax.all_to_all(
            term.reshape(n_head * n_tok, run, cols),
            ("head", "tok"), split_axis=0, concat_axis=0, tiled=True,
        )
        view_terms.append(term.reshape(n_head, n_tok * run, cols))
    return add_terms(head_index, hires_tokens, cross_terms, view_terms)


def solution(mesh):
    in_specs = (
        P("tok", None),
        P("tok", None),
        P(),
        P(None, "head"),
        P(None, None, "head"),
        P(None, None, "head"),
        P(None, "head", None),
        P("tok", None),
        P("tok"),
    )
    out_specs = P("tok", "head")
    body = functools.partial(shards, mesh.shape["head"], mesh.shape["tok"])
    return jax.shard_map(body, mesh=mesh, in_specs=in_specs, out_specs=out_specs, check_vma=False)
```

time: 222 us -> 202 us (0.910)
  waiting for transfers between devices: 77.2 us -> 37 us
  blocking collectives: 27.6 us -> 59.1 us
  local copies, waits for them, and re-layouts: 19.9 us -> 8.14 us
  Pallas kernels: 57.1 us -> 64.1 us
  starting transfers between devices: 23.3 us -> 17.4 us
    all_gather x3 -> x1, waiting for transfers between devices: 40.1 us -> 0.02 us  [shards(): weights = lax.all_gather(own_weights, 'head', axis=0, tiled=False)]
    all_to_all x1 -> x2, blocking collectives: 27.6 us -> 59.1 us  [the longest x1 30.9 us: shards(): lax.all_to_all(term.reshape(n_head * n_tok, run, cols), ('head', 'tok'),...]
    unnamed x30 -> x32, local copies, waits for them, and re-layouts: 14.8 us -> 3.78 us
    pallas_call x5, Pallas kernels: 57.1 us -> 64.1 us  [the longest x2 34.2 us: cross_attention(): pl.pallas_call(functools.partial(cross_kernel, first), out_shape=jax.Shap...]
    all_to_all x2 -> x1, starting transfers between devices: 7.25 us -> 3.56 us  [shards(): lax.all_to_all(term.reshape(n_head * n_tok, run, cols), ('head', 'tok'),...]
    all_to_all x2 -> x1, starting transfers between devices: 7.07 us -> 5.47 us  [arrive(): return lax.all_to_all(rows, 'tok', split_axis=0, concat_axis=0, tiled=True)]
    all_to_all x2 -> x1, waiting for transfers between devices: 16.1 us -> 16 us  [shards(): lax.all_to_all(term.reshape(n_head * n_tok, run, cols), ('head', 'tok'),...]
  transfers between devices with their start and end apart: 14 -> 12, of which waited for: 7 -> 6; matrix products, arithmetic and copies ran while one was open for 2% -> 2% of each run, Pallas kernels for 24% -> 28%
where the time goes in v3:
time: 202 us; the launch traced here: 201 us
  Pallas kernels  64.1 us (32%)
  blocking collectives  59.1 us (29%)
  waiting for transfers between devices  37 us (18%)
  starting transfers between devices  17.4 us (9%)
  between operations  13.3 us (7%)
  local copies, waits for them, and re-layouts  8.14 us (4%)
    pallas_call x2, Pallas kernels, cross_attention(): pl.pallas_call(functools.partial(cross_kernel, first), out_shape=jax.Shap...  34.2 us
    all_to_all x1, blocking collectives, shards(): lax.all_to_all(term.reshape(n_head * n_tok, run, cols), ('head', 'tok'),...  30.9 us
    all_to_all x1, blocking collectives, arrive(): return lax.all_to_all(rows, 'tok', split_axis=0, concat_axis=0, tiled=True)  28.2 us
    pallas_call x2, Pallas kernels, view_attention(): pl.pallas_call(view_kernel, out_shape=jax.ShapeDtypeStruct((parts, n_tok,...  23 us
    ppermute x4, waiting for transfers between devices, ring_chunks(): behind.append(lax.ppermute(behind[-1], 'tok', upward))  18.6 us
    all_to_all x1, waiting for transfers between devices, shards(): lax.all_to_all(term.reshape(n_head * n_tok, run, cols), ('head', 'tok'),...  16 us
    ppermute x4, starting transfers between devices, ring_chunks(): behind.append(lax.ppermute(behind[-1], 'tok', upward))  7.65 us
    pallas_call x1, Pallas kernels, add_terms(): pl.pallas_call(functools.partial(add_kernel, chunks, steps, n_parts), out...  6.88 us
  transfers between devices with their start and end apart: 12, of which 6 were waited for; matrix products, arithmetic and copies ran while one was open for 2% of the time, Pallas kernels for 28%

profile of v3, /device:TPU:0, one launch (start us, length us, event | category | flops | bytes accessed | tf_op | source)
XLA Modules:
  0.0 201.2 jit_solution(9437791302963835624)
XLA Ops:
  6.5 0.0 all-gather.3.cloned.1.call-start
  6.5 1.2 slice.3
  7.7 0.4 reshape_squeeze.3
  8.1 0.1 copy.15
  8.2 1.5 pad_maximum_fusion
  9.7 0.0 all-gather.3.cloned.1.call-update
  9.7 1.2 copy-done.3
  10.9 0.2 copy.16
  11.2 0.2 fusion
  11.4 0.0 copy-done.5
  11.4 0.5 convolution_convert_fusion.refs_0_
  11.9 3.1 %collective-permute-start.3 = (bf16[256,512]{1,0:T(8,128)(2,1)S(1)}, bf16[256,512]{1,0:T(8,128)(2,1)S(1)}, u32[]{:S(2)}, u32[]{:S(2)}) collective-permute-start(bf16[256,512]{1,0:T(8,128)(2,1)S(1)} %convolution_convert_fusion.refs_0_), channel_id=1, source_target_pairs={{0,2},{2,4},{4,6},{6,7},{7,5},{5,3},{3,1},{1,0},{8,10},{10,12},{12... | collective-permute-start | bytes 786440 | tf_op jit(solution)/shard_map/ppermute | solution.py:296
  14.9 0.0 collective-permute-start
  14.9 6.2 %collective-permute-done.3.refs_7_ = bf16[256,512]{1,0:T(8,128)(2,1)S(1)} collective-permute-done((bf16[256,512]{1,0:T(8,128)(2,1)S(1)}, bf16[256,512]{1,0:T(8,128)(2,1)S(1)}, u32[]{:S(2)}, u32[]{:S(2)}) %collective-permute-start.3) | collective-permute-done | bytes 262176 | tf_op jit(solution)/shard_map/ppermute | solution.py:296
  21.2 1.8 collective-permute-start.4
  23.0 0.0 collective-permute-done.refs_1_
  23.0 0.2 collective-permute-start.1
  23.2 5.4 %collective-permute-done.4.refs_6_ = bf16[256,512]{1,0:T(8,128)(2,1)S(1)} collective-permute-done((bf16[256,512]{1,0:T(8,128)(2,1)S(1)}, bf16[256,512]{1,0:T(8,128)(2,1)S(1)}, u32[]{:S(2)}, u32[]{:S(2)}) %collective-permute-start.4) | collective-permute-done | bytes 262176 | tf_op jit(solution)/shard_map/ppermute | solution.py:296
  28.6 1.5 collective-permute-start.5
  30.2 0.0 collective-permute-done.1.refs_2_
  30.2 0.5 collective-permute-start.2
  30.7 4.6 %collective-permute-done.5.refs_5_ = bf16[256,512]{1,0:T(8,128)(2,1)S(1)} collective-permute-done((bf16[256,512]{1,0:T(8,128)(2,1)S(1)}, bf16[256,512]{1,0:T(8,128)(2,1)S(1)}, u32[]{:S(2)}, u32[]{:S(2)}) %collective-permute-start.5) | collective-permute-done | bytes 262176 | tf_op jit(solution)/shard_map/ppermute | solution.py:296
  35.3 1.2 collective-permute-start.6
  36.5 2.7 %constant_dynamic-slice_fusion = (bf16[512,1024]{1,0:T(8,128)(2,1)S(1)}, bf16[512,1024]{1,0:T(8,128)(2,1)}) fusion(bf16[4096,1024]{1,0:T(8,128)(2,1)} %tokens_ref.5, s32[]{:T(128)S(6)} %select_n.7, s32[]{:T(128)S(6)} %select_n.6), kind=kLoop, calls=%fused_computation.10 | loop fusion | bytes 4194312 | tf_op jit(solution)/shard_map/dynamic_slice | solution.py:340
  39.3 0.0 copy-done.7
  39.3 0.0 copy-start.6
  39.3 0.0 collective-permute-done.2.refs_3_
  39.3 0.0 copy-start.13
  39.3 2.3 %collective-permute-done.6.refs_4_ = bf16[256,512]{1,0:T(8,128)(2,1)S(1)} collective-permute-done((bf16[256,512]{1,0:T(8,128)(2,1)S(1)}, bf16[256,512]{1,0:T(8,128)(2,1)S(1)}, u32[]{:S(2)}, u32[]{:S(2)}) %collective-permute-start.6) | collective-permute-done | bytes 262176 | tf_op jit(solution)/shard_map/ppermute | solution.py:296
  41.7 0.7 copy-done.14
  42.4 5.5 %all-to-all-start = ((bf16[8,64,1024]{2,1,0:T(8,128)(2,1)}), bf16[8,64,1024]{2,1,0:T(8,128)(2,1)S(1)}, u32[]{:S(2)}, u32[]{:S(2)}) async-start(bf16[8,64,1024]{2,1,0:T(8,128)(2,1)} %bitcast.3), calls=%async_computation | async-start | bytes 2097152 | tf_op jit(solution)/shard_map/all_to_all | solution.py:348
  47.8 0.0 reduce-scatter.3.cloned.1.call-start
  47.9 0.7 copy.13.lists_ref
  48.6 17.1 %cross.3 = bf16[2048,1024]{1,0:T(8,128)(2,1)} custom-call(s32[32,8]{1,0:T(8,128)} %copy.13.lists_ref, s32[32]{0:T(128)} %counts_ref.3, s32[1]{0:T(128)} %bitcast.1.tok_ref, bf16[4096,1024]{1,0:T(8,128)(2,1)} %tokens_ref.5, f32[1,1024]{1,0:T(1,128)} %bitcast.30, bf16[1024,256]{1,0:T(8,128)(2,1)} %wq_ref.3, bf16[2,256,1024]{2,1,0:T(8,128)(2,1)} %wo_ref.3, ...), custom_call_target="tpu_custom_call" | custom-call | flops 6442450944 | bytes 8388608 | tf_op jit(solution)/shard_map/cross/pallas_call | solution.py:113
  65.7 17.1 %cross.2 = bf16[2048,1024]{1,0:T(8,128)(2,1)} custom-call(s32[32,8]{1,0:T(8,128)} %copy.13.lists_ref, s32[32]{0:T(128)} %counts_ref.3, s32[1]{0:T(128)} %bitcast.1.tok_ref, bf16[4096,1024]{1,0:T(8,128)(2,1)} %tokens_ref.5, f32[1,1024]{1,0:T(1,128)} %bitcast.31, bf16[1024,256]{1,0:T(8,128)(2,1)} %wq_ref.3, bf16[2,256,1024]{2,1,0:T(8,128)(2,1)} %wo_ref.3, ...), custom_call_target="tpu_custom_call" | custom-call | flops 6442450944 | bytes 8388608 | tf_op jit(solution)/shard_map/cross/pallas_call | solution.py:113
  82.8 0.0 all-to-all-done.tokens_ref
  82.8 0.0 all-gather.3.cloned.1.call-done
  82.8 0.0 reduce-scatter.3.cloned.1.call-update
  82.8 0.9 copy-done
  83.8 0.7 reduce-scatter.5.cloned.1.call-update
  84.5 28.2 %all_to_all.20.tokens_ref = bf16[8,64,1024]{2,1,0:T(8,128)(2,1)} all-to-all(bf16[8,64,1024]{2,1,0:T(8,128)(2,1)S(1)} %bitcast.21), channel_id=1, replica_groups=mesh['head'=4,'tok'=8] {'tok'}, dimensions={0} | all-to-all | bytes 2097152 | tf_op jit(solution)/shard_map/all_to_all | solution.py:348
  112.7 11.4 %view.3 = bf16[4,8,64,256]{3,2,1,0:T(8,128)(2,1)} custom-call(bf16[8,64,1024]{2,1,0:T(8,128)(2,1)} %all_to_all.20.tokens_ref, f32[1,1024]{1,0:T(1,128)} %bitcast.32, bf16[4,4,1024,256]{3,2,1,0:T(8,128)(2,1)} %bitcast.17, bf16[4,4,1024,256]{3,2,1,0:T(8,128)(2,1)} %bitcast.18), custom_call_target="tpu_custom_call" | custom-call | flops 4831838208 | bytes 10485760 | tf_op jit(solution)/shard_map/view/pallas_call | solution.py:216
  124.1 3.6 %all-to-all-start.3 = ((bf16[32,64,256]{2,1,0:T(8,128)(2,1)}), bf16[32,64,256]{2,1,0:T(8,128)(2,1)S(1)}, u32[]{:S(2)}, u32[]{:S(2)}) async-start(bf16[32,64,256]{2,1,0:T(8,128)(2,1)} %bitcast.24), calls=%async_computation.5 | async-start | bytes 2097152 | tf_op jit(solution)/shard_map/all_to_all | solution.py:368
  127.7 11.6 %view.2 = bf16[4,8,64,256]{3,2,1,0:T(8,128)(2,1)} custom-call(bf16[8,64,1024]{2,1,0:T(8,128)(2,1)} %copy-done, f32[1,1024]{1,0:T(1,128)} %bitcast.33, bf16[4,4,1024,256]{3,2,1,0:T(8,128)(2,1)} %bitcast.19, bf16[4,4,1024,256]{3,2,1,0:T(8,128)(2,1)} %bitcast.20), custom_call_target="tpu_custom_call" | custom-call | flops 4831838208 | bytes 10485760 | tf_op jit(solution)/shard_map/view/pallas_call | solution.py:216
  139.3 16.0 %all-to-all-done.3 = bf16[32,64,256]{2,1,0:T(8,128)(2,1)S(1)} async-done(((bf16[32,64,256]{2,1,0:T(8,128)(2,1)}), bf16[32,64,256]{2,1,0:T(8,128)(2,1)S(1)}, u32[]{:S(2)}, u32[]{:S(2)}) %all-to-all-start.3) | async-done | bytes 1048608 | tf_op jit(solution)/shard_map/all_to_all | solution.py:368
  155.3 30.9 %all_to_all.21 = bf16[32,64,256]{2,1,0:T(8,128)(2,1)} all-to-all(bf16[32,64,256]{2,1,0:T(8,128)(2,1)} %bitcast.25), channel_id=1, replica_groups=mesh['head'=4,'tok'=8] {'head','tok'}, dimensions={0} | all-to-all | bytes 2097152 | tf_op jit(solution)/shard_map/all_to_all | solution.py:368
  186.2 1.6 reduce-scatter.5.cloned.1.call-done.refs_1_
  187.8 6.9 %add.36 = bf16[4096,256]{1,0:T(8,128)(2,1)} custom-call(s32[1]{0:T(128)} %bitcast.index_ref, bf16[4096,1024]{1,0:T(8,128)(2,1)} %tokens_ref.5, bf16[2048,256]{1,0:T(8,128)(2,1)} %reduce-scatter.3.cloned.1.call-done.refs_0_, bf16[2048,256]{1,0:T(8,128)(2,1)} %reduce-scatter.5.cloned.1.call-done.refs_1_, bf16[4,512,256]{2,1,0:T(8,128)(2,1)} %bitcast.23, ...), custom_call_target="tpu_custom_call" | custom-call | flops 2097152 | bytes 8388608 | tf_op jit(solution)/shard_map/add/pallas_call | solution.py:269
  (26 shorter events, 0.1 us)
Async XLA Ops:
  6.5 1.7 copy-start.2
  6.5 76.2 %all-gather.3.cloned.1.call-start = ((), (), s32[]{:S(2)}) async-start(), calls=%async_computation.8 | async-start | bytes 10485760 | tf_op jit(solution)/shard_map/all_gather | solution.py:336
  9.7 1.2 copy-start.3
  9.7 1.5 copy-start.4
  9.7 1.7 copy-start.5
  11.9 27.4 %copy-start.7 = (bf16[256,512]{1,0:T(8,128)(2,1)}, bf16[256,512]{1,0:T(8,128)(2,1)S(1)}, u32[]{:S(2)}) copy-start(bf16[256,512]{1,0:T(8,128)(2,1)S(1)} %convolution_convert_fusion.refs_0_) | copy-start | bytes 786436
  11.9 9.3 %collective-permute-start.3 = (bf16[256,512]{1,0:T(8,128)(2,1)S(1)}, bf16[256,512]{1,0:T(8,128)(2,1)S(1)}, u32[]{:S(2)}, u32[]{:S(2)}) collective-permute-start(bf16[256,512]{1,0:T(8,128)(2,1)S(1)} %convolution_convert_fusion.refs_0_), channel_id=1, source_target_pairs={{0,2},{2,4},{4,6},{6,7},{7,5},{5,3},{3,1},{1,0},{8,10},{10,12},{12... | collective-permute-start | bytes 786440 | tf_op jit(solution)/shard_map/ppermute | solution.py:296
  14.9 8.1 %collective-permute-start = (bf16[256,512]{1,0:T(8,128)(2,1)S(1)}, bf16[256,512]{1,0:T(8,128)(2,1)S(1)}, u32[]{:S(2)}, u32[]{:S(2)}) collective-permute-start(bf16[256,512]{1,0:T(8,128)(2,1)S(1)} %convolution_convert_fusion.refs_0_), channel_id=1, source_target_pairs={{0,1},{2,0},{4,2},{6,4},{7,6},{5,7},{3,5},{1,3},{8,9},{10,8},{12,1... | collective-permute-start | bytes 786440 | tf_op jit(solution)/shard_map/ppermute | solution.py:298
  21.2 18.1 %copy-start.8 = (bf16[256,512]{1,0:T(8,128)(2,1)}, bf16[256,512]{1,0:T(8,128)(2,1)S(1)}, u32[]{:S(2)}) copy-start(bf16[256,512]{1,0:T(8,128)(2,1)S(1)} %collective-permute-done.3.refs_7_) | copy-start | bytes 786436
  21.2 7.5 %collective-permute-start.4 = (bf16[256,512]{1,0:T(8,128)(2,1)S(1)}, bf16[256,512]{1,0:T(8,128)(2,1)S(1)}, u32[]{:S(2)}, u32[]{:S(2)}) collective-permute-start(bf16[256,512]{1,0:T(8,128)(2,1)S(1)} %collective-permute-done.3.refs_7_), channel_id=1, source_target_pairs={{0,2},{2,4},{4,6},{6,7},{7,5},{5,3},{3,1},{1,0},{8,10},{10,12},{12... | collective-permute-start | bytes 786440 | tf_op jit(solution)/shard_map/ppermute | solution.py:296
  23.0 16.3 %copy-start.9 = (bf16[256,512]{1,0:T(8,128)(2,1)}, bf16[256,512]{1,0:T(8,128)(2,1)S(1)}, u32[]{:S(2)}) copy-start(bf16[256,512]{1,0:T(8,128)(2,1)S(1)} %collective-permute-done.refs_1_) | copy-start | bytes 786436
  23.0 7.2 %collective-permute-start.1 = (bf16[256,512]{1,0:T(8,128)(2,1)S(1)}, bf16[256,512]{1,0:T(8,128)(2,1)S(1)}, u32[]{:S(2)}, u32[]{:S(2)}) collective-permute-start(bf16[256,512]{1,0:T(8,128)(2,1)S(1)} %collective-permute-done.refs_1_), channel_id=1, source_target_pairs={{0,1},{2,0},{4,2},{6,4},{7,6},{5,7},{3,5},{1,3},{8,9},{10,8},{12,1... | collective-permute-start | bytes 786440 | tf_op jit(solution)/shard_map/ppermute | solution.py:298
  28.6 10.6 %copy-start.10 = (bf16[256,512]{1,0:T(8,128)(2,1)}, bf16[256,512]{1,0:T(8,128)(2,1)S(1)}, u32[]{:S(2)}) copy-start(bf16[256,512]{1,0:T(8,128)(2,1)S(1)} %collective-permute-done.4.refs_6_) | copy-start | bytes 786436
  28.6 6.7 %collective-permute-start.5 = (bf16[256,512]{1,0:T(8,128)(2,1)S(1)}, bf16[256,512]{1,0:T(8,128)(2,1)S(1)}, u32[]{:S(2)}, u32[]{:S(2)}) collective-permute-start(bf16[256,512]{1,0:T(8,128)(2,1)S(1)} %collective-permute-done.4.refs_6_), channel_id=1, source_target_pairs={{0,2},{2,4},{4,6},{6,7},{7,5},{5,3},{3,1},{1,0},{8,10},{10,12},{12... | collective-permute-start | bytes 786440 | tf_op jit(solution)/shard_map/ppermute | solution.py:296
  30.2 9.1 %copy-start.11 = (bf16[256,512]{1,0:T(8,128)(2,1)}, bf16[256,512]{1,0:T(8,128)(2,1)S(1)}, u32[]{:S(2)}) copy-start(bf16[256,512]{1,0:T(8,128)(2,1)S(1)} %collective-permute-done.1.refs_2_) | copy-start | bytes 786436
  30.2 9.1 %collective-permute-start.2 = (bf16[256,512]{1,0:T(8,128)(2,1)S(1)}, bf16[256,512]{1,0:T(8,128)(2,1)S(1)}, u32[]{:S(2)}, u32[]{:S(2)}) collective-permute-start(bf16[256,512]{1,0:T(8,128)(2,1)S(1)} %collective-permute-done.1.refs_2_), channel_id=1, source_target_pairs={{0,1},{2,0},{4,2},{6,4},{7,6},{5,7},{3,5},{1,3},{8,9},{10,8},{12,1... | collective-permute-start | bytes 786440 | tf_op jit(solution)/shard_map/ppermute | solution.py:298
  35.3 4.0 %copy-start.12 = (bf16[256,512]{1,0:T(8,128)(2,1)}, bf16[256,512]{1,0:T(8,128)(2,1)S(1)}, u32[]{:S(2)}) copy-start(bf16[256,512]{1,0:T(8,128)(2,1)S(1)} %collective-permute-done.5.refs_5_) | copy-start | bytes 786436
  35.3 6.4 %collective-permute-start.6 = (bf16[256,512]{1,0:T(8,128)(2,1)S(1)}, bf16[256,512]{1,0:T(8,128)(2,1)S(1)}, u32[]{:S(2)}, u32[]{:S(2)}) collective-permute-start(bf16[256,512]{1,0:T(8,128)(2,1)S(1)} %collective-permute-done.5.refs_5_), channel_id=1, source_target_pairs={{0,2},{2,4},{4,6},{6,7},{7,5},{5,3},{3,1},{1,0},{8,10},{10,12},{12... | collective-permute-start | bytes 786440 | tf_op jit(solution)/shard_map/ppermute | solution.py:296
  39.3 8.6 %copy-start.6 = (s32[32,8]{0,1:T(8,128)S(1)}, s32[32,8]{0,1:T(8,128)}, u32[]{:S(2)}) copy-start(s32[32,8]{0,1:T(8,128)} %param.16) | copy-start | bytes 3076
  39.3 2.4 %copy-start.13 = (bf16[256,512]{1,0:T(8,128)(2,1)}, bf16[256,512]{1,0:T(8,128)(2,1)S(1)}, u32[]{:S(2)}) copy-start(bf16[256,512]{1,0:T(8,128)(2,1)S(1)} %collective-permute-done.2.refs_3_) | copy-start | bytes 786436
  41.7 0.7 copy-start.14
  42.4 40.4 %all-to-all-start = ((bf16[8,64,1024]{2,1,0:T(8,128)(2,1)}), bf16[8,64,1024]{2,1,0:T(8,128)(2,1)S(1)}, u32[]{:S(2)}, u32[]{:S(2)}) async-start(bf16[8,64,1024]{2,1,0:T(8,128)(2,1)} %bitcast.3), calls=%async_computation | async-start | bytes 2097152 | tf_op jit(solution)/shard_map/all_to_all | solution.py:348
  47.8 138.4 %reduce-scatter.3.cloned.1.call-start = ((), (), s32[]{:S(2)}) async-start(), calls=%async_computation.6 | async-start | bytes 5242880 | tf_op jit(solution)/shard_map/reduce_scatter | solution.py:363
  82.8 1.0 copy-start
  83.8 104.1 %reduce-scatter.5.cloned.1.call-start = ((), (), s32[]{:S(2)}) async-start(), calls=%async_computation.7 | async-start | bytes 5242880 | tf_op jit(solution)/shard_map/reduce_scatter | solution.py:363
  124.1 31.2 %all-to-all-start.3 = ((bf16[32,64,256]{2,1,0:T(8,128)(2,1)}), bf16[32,64,256]{2,1,0:T(8,128)(2,1)S(1)}, u32[]{:S(2)}, u32[]{:S(2)}) async-start(bf16[32,64,256]{2,1,0:T(8,128)(2,1)} %bitcast.24), calls=%async_computation.5 | async-start | bytes 2097152 | tf_op jit(solution)/shard_map/all_to_all | solution.py:368
  155.3 32.5 %copy-start.1 = (bf16[32,64,256]{2,1,0:T(8,128)(2,1)}, bf16[32,64,256]{2,1,0:T(8,128)(2,1)S(1)}, u32[]{:S(2)}) copy-start(bf16[32,64,256]{2,1,0:T(8,128)(2,1)S(1)} %all-to-all-done.3) | copy-start | bytes 3145732
Sparse Core Ops, SparseCore 0:
  9.9 60.9 all-gather.2
  82.9 46.0 reduce-scatter.2
  131.7 56.0 reduce-scatter.4

commit v4 on v3

--- a/solution.py
+++ b/solution.py
@@ -41,13 +41,11 @@
     return jnp.where(lax.rem(tok, 2) == 0, half, n_tok - 1 - half)
 
 
-def cross_kernel(
-    first_step, lists_ref, counts_ref, tok_ref, tokens_ref, gain_ref, wq_ref, wo_ref, *refs
-):
-    kv_refs = refs[:-5]
-    out_ref, k_ref, vt_ref, q_ref, mixed_ref = refs[-5:]
+def cross_kernel(lists_ref, counts_ref, tok_ref, tokens_ref, gain_ref, wq_ref, *refs):
+    kv_refs = refs[:-4]
+    out_ref, k_ref, vt_ref, q_ref = refs[-4:]
     step = pl.program_id(0)
-    rows, cols = mixed_ref.shape
+    rows, cols = out_ref.shape
     heads = cols // HD
     per_step = rows // BLOCK
     listed = lists_ref.shape[1]
@@ -67,7 +65,7 @@
     q_ref[...] = (f32_dot(normed, wq_ref[...]) * LOG2_SCALE).astype(jnp.bfloat16)
 
     def one_block(local, carry):
-        block = (first_step + step) * per_step + local
+        block = step * per_step + local
         row_start = pl.multiple_of(local * BLOCK, BLOCK)
         count = counts_ref[block]
         first = lists_ref[block, 0]
@@ -92,53 +90,46 @@
         mixed_t = f32_dot(values_t, jnp.concatenate(weights, axis=0)) / total
         for h in range(heads):
             part = slice(h * HD, (h + 1) * HD)
-            mixed_ref[pl.ds(row_start, BLOCK), part] = mixed_t[part, part].T.astype(jnp.bfloat16)
+            out_ref[pl.ds(row_start, BLOCK), part] = mixed_t[part, part].T.astype(jnp.bfloat16)
         return carry
 
     lax.fori_loop(0, per_step, one_block, 0, unroll=True)
-    out_ref[...] = f32_dot(mixed_ref[...], wo_ref[0]).astype(jnp.bfloat16)
-
-
-def cross_attention(
-    hires_tokens, gain, w_cross_q, w_out, kv_chunks, block_lists, block_counts, part, parts
-):
+
+
+def cross_attention(hires_tokens, gain, w_cross_q, kv_chunks, block_lists, block_counts):
     tok_index = lax.axis_index("tok").reshape(1)
     tok_rows, width = hires_tokens.shape
     cols = w_cross_q.shape[1]
     chunk = kv_chunks[0].shape[0]
     low_rows = chunk * len(kv_chunks)
-    tok_rows = tok_rows // parts
     rows = math.gcd(tok_rows, 4 * BLOCK)
-    first = part * tok_rows // rows
     return pl.pallas_call(
-        functools.partial(cross_kernel, first),
-        out_shape=jax.ShapeDtypeStruct((tok_rows, width), jnp.bfloat16),
+        cross_kernel,
+        out_shape=jax.ShapeDtypeStruct((tok_rows, cols), jnp.bfloat16),
         grid_spec=pltpu.PrefetchScalarGridSpec(
             num_scalar_prefetch=3,
             grid=(tok_rows // rows,),
             in_specs=[
-                pl.BlockSpec((rows, width), lambda i, *_: (first + i, 0)),
+                pl.BlockSpec((rows, width), lambda i, *_: (i, 0)),
                 pl.BlockSpec((1, width), lambda i, *_: (0, 0)),
                 pl.BlockSpec((width, cols), lambda i, *_: (0, 0)),
-                pl.BlockSpec((1, cols, width), lambda i, *_: (0, 0, 0)),
             ]
             + [pl.BlockSpec((chunk, 2 * cols), lambda i, *_: (0, 0)) for _ in kv_chunks],
-            out_specs=pl.BlockSpec((rows, width), lambda i, *_: (i, 0)),
+            out_specs=pl.BlockSpec((rows, cols), lambda i, *_: (i, 0)),
             scratch_shapes=[
                 pltpu.VMEM((low_rows, cols), jnp.bfloat16),
                 pltpu.VMEM((cols, low_rows), jnp.bfloat16),
                 pltpu.VMEM((rows, cols), jnp.bfloat16),
-                pltpu.VMEM((rows, cols), jnp.bfloat16),
             ],
         ),
         compiler_params=pltpu.CompilerParams(vmem_limit_bytes=VMEM_BYTES),
         cost_estimate=pl.CostEstimate(
-            flops=2 * tok_rows * cols * (2 * width + 2 * block_lists.shape[1] * BLOCK * 2),
-            bytes_accessed=4 * tok_rows * width,
+            flops=2 * tok_rows * cols * (width + 2 * block_lists.shape[1] * BLOCK * 2),
+            bytes_accessed=2 * tok_rows * (width + cols),
             transcendentals=tok_rows * block_lists.shape[1] * BLOCK * (cols // HD),
         ),
         name="cross",
-    )(block_lists, block_counts, tok_index, hires_tokens, gain, w_cross_q, w_out, *kv_chunks)
+    )(block_lists, block_counts, tok_index, hires_tokens, gain, w_cross_q, *kv_chunks)
 
 
 def view_kernel(
@@ -239,52 +230,60 @@
     )(tokens, gain, weights, weights)
 
 
-def add_kernel(chunks, steps, n_parts, index_ref, tokens_ref, *refs):
-    cross_refs, view_refs, out_ref = refs[:n_parts], refs[n_parts:-1], refs[-1]
-    h, c = pl.program_id(0), pl.program_id(1)
-    for part in range(n_parts):
-        for chunk in range(chunks):
-            @pl.when((lax.div(h, steps) == part) & (c == chunk))
-            def _():
-                terms = cross_refs[part][...].astype(jnp.float32)
-                terms = terms + view_refs[chunk][0].astype(jnp.float32)
-                out_ref[...] = (tokens_ref[...].astype(jnp.float32) + terms).astype(jnp.bfloat16)
-
-
-def add_terms(head_index, hires_tokens, cross_terms, view_terms):
-    cols = cross_terms[0].shape[1]
+def final_kernel(chunks, index_ref, tokens_ref, cross_ref, *refs):
+    view_refs, w_refs, out_ref = refs[:chunks], refs[chunks:-1], refs[-1]
+    parts = len(w_refs)
+    total = tokens_ref[...].astype(jnp.float32)
+    for k, w_ref in enumerate(w_refs):
+        group = lax.rem(index_ref[0] + parts - k, parts)
+        total = total + f32_dot(cross_ref[group], w_ref[...])
+    for chunk, view_ref in enumerate(view_refs):
+        @pl.when(pl.program_id(1) == chunk)
+        def _():
+            out_ref[...] = (total + view_ref[0].astype(jnp.float32)).astype(jnp.bfloat16)
+
+
+def final_sum(head_index, hires_tokens, cross_all, view_terms, w_columns):
+    parts, tok_rows, cols = cross_all.shape
     n_head, rows, _ = view_terms[0].shape
-    chunks, n_parts = len(view_terms), len(cross_terms)
-    steps = n_head // n_parts
-    cross_specs = [
-        pl.BlockSpec(
-            (rows, cols),
-            lambda h, c, index, part=part: (
-                jnp.clip(h * chunks + c - part * steps * chunks, 0, steps * chunks - 1), 0
-            ),
-        )
-        for part in range(n_parts)
-    ]
+    chunks = len(view_terms)
     view_spec = pl.BlockSpec((1, rows, cols), lambda h, c, index: (h, 0, 0))
+    w_spec = pl.BlockSpec((cols, cols), lambda h, c, index: (0, 0))
     return pl.pallas_call(
-        functools.partial(add_kernel, chunks, steps, n_parts),
-        out_shape=jax.ShapeDtypeStruct((n_head * chunks * rows, cols), jnp.bfloat16),
+        functools.partial(final_kernel, chunks),
+        out_shape=jax.ShapeDtypeStruct((tok_rows, cols), jnp.bfloat16),
         grid_spec=pltpu.PrefetchScalarGridSpec(
             num_scalar_prefetch=1,
             grid=(n_head, chunks),
-            in_specs=[pl.BlockSpec((rows, cols), lambda h, c, index: (h * chunks + c, index[0]))]
-            + cross_specs
-            + [view_spec] * chunks,
+            in_specs=[
+                pl.BlockSpec((rows, cols), lambda h, c, index: (h * chunks + c, index[0])),
+                pl.BlockSpec((parts, rows, cols), lambda h, c, index: (0, h * chunks + c, 0)),
+            ]
+            + [view_spec] * chunks
+            + [w_spec] * parts,
             out_specs=pl.BlockSpec((rows, cols), lambda h, c, index: (h * chunks + c, 0)),
         ),
         compiler_params=pltpu.CompilerParams(vmem_limit_bytes=VMEM_BYTES),
         cost_estimate=pl.CostEstimate(
-            flops=2 * n_head * chunks * rows * cols,
-            bytes_accessed=8 * n_head * chunks * rows * cols,
+            flops=2 * parts * tok_rows * cols * cols,
+            bytes_accessed=2 * tok_rows * cols * (parts + 3),
             transcendentals=0,
         ),
-        name="add",
-    )(head_index.reshape(1), hires_tokens, *cross_terms, *view_terms)
+        name="final",
+    )(head_index.reshape(1), hires_tokens, cross_all, *view_terms, *w_columns)
+
+
+def column_blocks(rows_of_w, head_index, n_head):
+    cols = rows_of_w.shape[1] // n_head
+    blocks = []
+    for k in range(n_head):
+        start = lax.rem(head_index + k, n_head) * cols
+        block = lax.dynamic_slice_in_dim(rows_of_w, start, cols, 1)
+        if k:
+            pairs = [(h, (h + k) % n_head) for h in range(n_head)]
+            block = lax.ppermute(block, "head", pairs)
+        blocks.append(block)
+    return blocks
 
 
 def ring_chunks(own, n_tok):
@@ -321,11 +320,7 @@
     run = quarter // n_tok
     chunks = 2 if run % 32 == 0 else 1
     run = run // chunks
-    parts = 2 if n_head % 2 == 0 else 1
-
-    low_kv = f32_dot(
-        rms_rows(lowres_tokens, norm_gain), w_low_kv.reshape(width, 2 * cols)
-    ).astype(jnp.bfloat16)
+
     own_weights = jnp.concatenate(
         [
             w_view_qkv.transpose(1, 0, 2),
@@ -334,34 +329,29 @@
         axis=0,
     )
     weights = lax.all_gather(own_weights, "head", axis=0, tiled=False)
+    low_kv = f32_dot(
+        rms_rows(lowres_tokens, norm_gain), w_low_kv.reshape(width, 2 * cols)
+    ).astype(jnp.bfloat16)
     kv_chunks = ring_chunks(low_kv, n_tok)
-
-    rows_of_chunk = [
+    w_columns = column_blocks(w_out[0], head_index, n_head)
+    sent = [
         lax.dynamic_slice_in_dim(
             hires_tokens, head_index * quarter + chunk * n_tok * run, n_tok * run, 0
         ).reshape(n_tok, run, width)
         for chunk in range(chunks)
     ]
-    kv_chunks, rows_of_chunk = lax.optimization_barrier((kv_chunks, rows_of_chunk))
+    kv_chunks, sent, w_columns = lax.optimization_barrier((kv_chunks, sent, w_columns))
 
     def arrive(rows):
         return lax.all_to_all(rows, "tok", split_axis=0, concat_axis=0, tiled=True)
 
-    arrived = [arrive(rows_of_chunk[0])]
-    partials = []
-    for part in range(parts):
-        partials.append(
-            cross_attention(
-                hires_tokens, gain, w_cross_q, w_out, kv_chunks, block_lists, block_counts,
-                part, parts,
-            )
-        )
-    partials, arrived, rows_of_chunk = lax.optimization_barrier((partials, arrived, rows_of_chunk))
-    arrived.extend(arrive(rows) for rows in rows_of_chunk[1:])
-    partials, weights = lax.optimization_barrier((partials, weights))
-    cross_terms = [
-        lax.psum_scatter(partial, "head", scatter_dimension=1, tiled=True) for partial in partials
-    ]
+    arrived = [arrive(sent[0])]
+    cross_out = cross_attention(
+        hires_tokens, gain, w_cross_q, kv_chunks, block_lists, block_counts
+    )
+    cross_out, arrived, sent = lax.optimization_barrier((cross_out, arrived, sent))
+    cross_all = lax.all_gather(cross_out, "head", axis=0, tiled=False)
+    arrived.extend(arrive(rows) for rows in sent[1:])
     view_terms = []
     for tokens in arrived:
         term = view_attention(tokens, gain, weights)
@@ -370,7 +360,7 @@
             ("head", "tok"), split_axis=0, concat_axis=0, tiled=True,
         )
         view_terms.append(term.reshape(n_head, n_tok * run, cols))
-    return add_terms(head_index, hires_tokens, cross_terms, view_terms)
+    return final_sum(head_index, hires_tokens, cross_all, view_terms, w_columns)
 
 
 def solution(mesh):

time: 202 us -> 206 us (1.020)
  Pallas kernels: 64.1 us -> 59.4 us
  blocking collectives: 59.1 us -> 62.9 us
  waiting for transfers between devices: 37 us -> 40.4 us
  starting transfers between devices: 17.4 us -> 19.6 us
    ppermute x0 -> x3, waiting for transfers between devices: none -> 7.85 us  [column_blocks(): block = lax.ppermute(block, 'head', pairs)]
    pallas_call x3 -> x2, Pallas kernels: 41.1 us -> 36.4 us  [the longest x1 26.6 us: cross_attention(): pl.pallas_call(cross_kernel, out_shape=jax.ShapeDtypeStruct((tok_rows, co...]
    all_to_all x1, blocking collectives: 28.2 us -> 31.9 us  [arrive(): return lax.all_to_all(rows, 'tok', split_axis=0, concat_axis=0, tiled=True)]
    ppermute x0 -> x3, starting transfers between devices: none -> 2.98 us  [column_blocks(): block = lax.ppermute(block, 'head', pairs)]
    ppermute x4, waiting for transfers between devices: 18.6 us -> 16.3 us  [ring_chunks(): behind.append(lax.ppermute(behind[-1], 'tok', upward))]
  transfers between devices with their start and end apart: 12 -> 14, of which waited for: 6 -> 8; matrix products, arithmetic and copies ran while one was open for 2% -> 2% of each run, Pallas kernels for 28% -> 24%
where the time goes in v4:
time: 206 us; the launch traced here: 205 us
  blocking collectives  62.9 us (31%)
  Pallas kernels  59.4 us (29%)
  waiting for transfers between devices  40.4 us (20%)
  starting transfers between devices  19.6 us (10%)
  between operations  13.6 us (7%)
  local copies, waits for them, and re-layouts  7.42 us (4%)
    all_to_all x1, blocking collectives, arrive(): return lax.all_to_all(rows, 'tok', split_axis=0, concat_axis=0, tiled=True)  31.9 us
    all_to_all x1, blocking collectives, shards(): lax.all_to_all(term.reshape(n_head * n_tok, run, cols), ('head', 'tok'),...  31 us
    pallas_call x1, Pallas kernels, cross_attention(): pl.pallas_call(cross_kernel, out_shape=jax.ShapeDtypeStruct((tok_rows, co...  26.6 us
    pallas_call x2, Pallas kernels, view_attention(): pl.pallas_call(view_kernel, out_shape=jax.ShapeDtypeStruct((parts, n_tok,...  23 us
    ppermute x4, waiting for transfers between devices, ring_chunks(): behind.append(lax.ppermute(behind[-1], 'tok', upward))  16.3 us
    all_to_all x1, waiting for transfers between devices, shards(): lax.all_to_all(term.reshape(n_head * n_tok, run, cols), ('head', 'tok'),...  16 us
    pallas_call x1, Pallas kernels, final_sum(): pl.pallas_call(functools.partial(final_kernel, chunks), out_shape=jax.Sha...  9.77 us
    ppermute x3, waiting for transfers between devices, column_blocks(): block = lax.ppermute(block, 'head', pairs)  7.85 us
  transfers between devices with their start and end apart: 14, of which 8 were waited for; matrix products, arithmetic and copies ran while one was open for 2% of the time, Pallas kernels for 24%

profile of v4, /device:TPU:0, one launch (start us, length us, event | category | flops | bytes accessed | tf_op | source)
XLA Modules:
  0.0 205.4 jit_solution(18180176869617316868)
XLA Ops:
  6.5 0.0 all-gather.7.cloned.1.call-start
  6.5 1.4 fusion.6
  7.9 0.4 reshape_squeeze.3
  8.3 0.1 copy.13
  8.4 1.5 pad_maximum_fusion
  9.9 0.0 all-gather.7.cloned.1.call-update
  9.9 1.2 copy-done.3
  11.1 0.2 copy.14
  11.4 0.0 copy-done.4
  11.4 0.2 fusion
  11.6 0.5 convolution_convert_fusion.refs_0_
  12.1 3.1 %collective-permute-start.3 = (bf16[256,512]{1,0:T(8,128)(2,1)S(1)}, bf16[256,512]{1,0:T(8,128)(2,1)S(1)}, u32[]{:S(2)}, u32[]{:S(2)}) collective-permute-start(bf16[256,512]{1,0:T(8,128)(2,1)S(1)} %convolution_convert_fusion.refs_0_), channel_id=1, source_target_pairs={{0,2},{2,4},{4,6},{6,7},{7,5},{5,3},{3,1},{1,0},{8,10},{10,12},{12... | collective-permute-start | bytes 786440 | tf_op jit(solution)/shard_map/ppermute | solution.py:295
  15.2 0.0 collective-permute-start
  15.2 6.2 %collective-permute-done.3.refs_7_ = bf16[256,512]{1,0:T(8,128)(2,1)S(1)} collective-permute-done((bf16[256,512]{1,0:T(8,128)(2,1)S(1)}, bf16[256,512]{1,0:T(8,128)(2,1)S(1)}, u32[]{:S(2)}, u32[]{:S(2)}) %collective-permute-start.3) | collective-permute-done | bytes 262176 | tf_op jit(solution)/shard_map/ppermute | solution.py:295
  21.4 1.8 collective-permute-start.4
  23.2 0.0 collective-permute-done.refs_1_
  23.2 0.2 collective-permute-start.1
  23.4 5.5 %collective-permute-done.4.refs_6_ = bf16[256,512]{1,0:T(8,128)(2,1)S(1)} collective-permute-done((bf16[256,512]{1,0:T(8,128)(2,1)S(1)}, bf16[256,512]{1,0:T(8,128)(2,1)S(1)}, u32[]{:S(2)}, u32[]{:S(2)}) %collective-permute-start.4) | collective-permute-done | bytes 262176 | tf_op jit(solution)/shard_map/ppermute | solution.py:295
  28.9 1.5 collective-permute-start.5
  30.4 0.0 collective-permute-done.1.refs_2_
  30.4 0.5 collective-permute-start.2
  30.9 4.6 %collective-permute-done.5.refs_5_ = bf16[256,512]{1,0:T(8,128)(2,1)S(1)} collective-permute-done((bf16[256,512]{1,0:T(8,128)(2,1)S(1)}, bf16[256,512]{1,0:T(8,128)(2,1)S(1)}, u32[]{:S(2)}, u32[]{:S(2)}) %collective-permute-start.5) | collective-permute-done | bytes 262176 | tf_op jit(solution)/shard_map/ppermute | solution.py:295
  35.5 1.2 collective-permute-start.6
  36.8 0.7 dynamic-slice_bitcast_fusion
  37.5 0.0 collective-permute-start.7
  37.5 1.5 collective-permute-start.8
  39.0 1.4 collective-permute-start.9
  40.4 2.7 %constant_dynamic-slice_fusion = (bf16[512,1024]{1,0:T(8,128)(2,1)S(1)}, bf16[512,1024]{1,0:T(8,128)(2,1)}) fusion(bf16[4096,1024]{1,0:T(8,128)(2,1)} %tokens_ref.3, s32[]{:T(128)S(6)} %select_n.19, s32[]{:T(128)S(6)} %select_n.18), kind=kLoop, calls=%fused_computation.13 | loop fusion | bytes 4194312 | tf_op jit(solution)/shard_map/dynamic_slice | solution.py:338
  43.2 0.0 copy-done.13
  43.2 0.0 copy-start.9
  43.2 2.6 %collective-permute-done.7.refs_3_ = bf16[256,256]{1,0:T(8,128)(2,1)S(1)} collective-permute-done((bf16[256,256]{1,0:T(8,128)(2,1)S(1)}, bf16[256,256]{1,0:T(8,128)(2,1)S(1)}, u32[]{:S(2)}, u32[]{:S(2)}) %collective-permute-start.7) | collective-permute-done | bytes 131104 | tf_op jit(solution)/shard_map/ppermute | solution.py:284
  45.8 0.8 collective-permute-done.8.refs_4_
  46.6 4.5 %collective-permute-done.9.refs_5_ = bf16[256,256]{1,0:T(8,128)(2,1)S(1)} collective-permute-done((bf16[256,256]{1,0:T(8,128)(2,1)S(1)}, bf16[256,256]{1,0:T(8,128)(2,1)S(1)}, u32[]{:S(2)}, u32[]{:S(2)}) %collective-permute-start.9) | collective-permute-done | bytes 131104 | tf_op jit(solution)/shard_map/ppermute | solution.py:284
  51.1 0.0 collective-permute-done.2.refs_3_
  51.1 0.0 collective-permute-done.6.refs_4_
  51.1 4.8 %all-to-all-start = ((bf16[8,64,1024]{2,1,0:T(8,128)(2,1)}), bf16[8,64,1024]{2,1,0:T(8,128)(2,1)S(1)}, u32[]{:S(2)}, u32[]{:S(2)}) async-start(bf16[8,64,1024]{2,1,0:T(8,128)(2,1)} %bitcast.3), calls=%async_computation | async-start | bytes 2097152 | tf_op jit(solution)/shard_map/all_to_all | solution.py:346
  55.9 0.0 all-gather.5.cloned.1.call-start
  56.0 0.7 copy.12.lists_ref
  56.6 26.6 %cross.1 = bf16[4096,256]{1,0:T(8,128)(2,1)} custom-call(s32[32,8]{1,0:T(8,128)} %copy.12.lists_ref, s32[32]{0:T(128)} %counts_ref.1, s32[1]{0:T(128)} %bitcast.1.tok_ref, bf16[4096,1024]{1,0:T(8,128)(2,1)} %tokens_ref.3, f32[1,1024]{1,0:T(1,128)} %bitcast.40, bf16[1024,256]{1,0:T(8,128)(2,1)} %wq_ref.1, bf16[256,512]{1,0:T(8,128)(2,1)} %copy-done.10, ...), custom_call_target="tpu_custom_call" | custom-call | flops 10737418240 | bytes 10485760 | tf_op jit(solution)/shard_map/cross/pallas_call | solution.py:106
  83.2 0.2 all-to-all-done.tokens_ref
  83.4 0.0 all-gather.5.cloned.1.call-update
  83.4 31.9 %all_to_all.20.tokens_ref = bf16[8,64,1024]{2,1,0:T(8,128)(2,1)} all-to-all(bf16[8,64,1024]{2,1,0:T(8,128)(2,1)S(1)} %bitcast.31), channel_id=1, replica_groups=mesh['head'=4,'tok'=8] {'tok'}, dimensions={0} | all-to-all | bytes 2097152 | tf_op jit(solution)/shard_map/all_to_all | solution.py:346
  115.4 11.5 %view.3 = bf16[4,8,64,256]{3,2,1,0:T(8,128)(2,1)} custom-call(bf16[8,64,1024]{2,1,0:T(8,128)(2,1)} %all_to_all.20.tokens_ref, f32[1,1024]{1,0:T(1,128)} %bitcast.41, bf16[4,4,1024,256]{3,2,1,0:T(8,128)(2,1)} %bitcast.26, bf16[4,4,1024,256]{3,2,1,0:T(8,128)(2,1)} %bitcast.27), custom_call_target="tpu_custom_call" | custom-call | flops 4831838208 | bytes 10485760 | tf_op jit(solution)/shard_map/view/pallas_call | solution.py:207
  126.8 3.4 %all-to-all-start.3 = ((bf16[32,64,256]{2,1,0:T(8,128)(2,1)}), bf16[32,64,256]{2,1,0:T(8,128)(2,1)S(1)}, u32[]{:S(2)}, u32[]{:S(2)}) async-start(bf16[32,64,256]{2,1,0:T(8,128)(2,1)} %bitcast.34), calls=%async_computation.3 | async-start | bytes 2097152 | tf_op jit(solution)/shard_map/all_to_all | solution.py:358
  130.3 11.6 %view.2 = bf16[4,8,64,256]{3,2,1,0:T(8,128)(2,1)} custom-call(bf16[8,64,1024]{2,1,0:T(8,128)(2,1)} %copy-done, f32[1,1024]{1,0:T(1,128)} %bitcast.42, bf16[4,4,1024,256]{3,2,1,0:T(8,128)(2,1)} %bitcast.28, bf16[4,4,1024,256]{3,2,1,0:T(8,128)(2,1)} %bitcast.29), custom_call_target="tpu_custom_call" | custom-call | flops 4831838208 | bytes 10485760 | tf_op jit(solution)/shard_map/view/pallas_call | solution.py:207
  141.8 16.0 %all-to-all-done.3 = bf16[32,64,256]{2,1,0:T(8,128)(2,1)S(1)} async-done(((bf16[32,64,256]{2,1,0:T(8,128)(2,1)}), bf16[32,64,256]{2,1,0:T(8,128)(2,1)S(1)}, u32[]{:S(2)}, u32[]{:S(2)}) %all-to-all-start.3) | async-done | bytes 1048608 | tf_op jit(solution)/shard_map/all_to_all | solution.py:358
  157.8 31.0 %all_to_all.21 = bf16[32,64,256]{2,1,0:T(8,128)(2,1)} all-to-all(bf16[32,64,256]{2,1,0:T(8,128)(2,1)} %bitcast.35), channel_id=1, replica_groups=mesh['head'=4,'tok'=8] {'head','tok'}, dimensions={0} | all-to-all | bytes 2097152 | tf_op jit(solution)/shard_map/all_to_all | solution.py:358
  188.8 9.8 %final.1 = bf16[4096,256]{1,0:T(8,128)(2,1)} custom-call(s32[1]{0:T(128)} %bitcast.index_ref, bf16[4096,1024]{1,0:T(8,128)(2,1)} %tokens_ref.3, bf16[4,4096,256]{2,1,0:T(8,128)(2,1)} %bitcast.30, bf16[4,512,256]{2,1,0:T(8,128)(2,1)} %bitcast.33, bf16[4,512,256]{2,1,0:T(8,128)(2,1)} %bitcast.32, bf16[256,256]{1,0:T(8,128)(2,1)} %get-tuple-element.35.refs_2_, ...), custom_call_target="tpu_custom_call" | custom-call | flops 2147483648 | bytes 14680064 | tf_op jit(solution)/shard_map/final/pallas_call | solution.py:252
  (31 shorter events, 0.1 us)
Async XLA Ops:
  6.5 1.9 copy-start.2
  6.5 108.9 %all-gather.7.cloned.1.call-start = ((), (), s32[]{:S(2)}) async-start(), calls=%async_computation.5 | async-start | bytes 10485760 | tf_op jit(solution)/shard_map/all_gather | solution.py:331
  9.9 1.2 copy-start.3
  9.9 1.5 copy-start.4
  9.9 1.7 copy-start.8
  12.1 31.1 %copy-start.10 = (bf16[256,512]{1,0:T(8,128)(2,1)}, bf16[256,512]{1,0:T(8,128)(2,1)S(1)}, u32[]{:S(2)}) copy-start(bf16[256,512]{1,0:T(8,128)(2,1)S(1)} %convolution_convert_fusion.refs_0_) | copy-start | bytes 786436
  12.1 9.3 %collective-permute-start.3 = (bf16[256,512]{1,0:T(8,128)(2,1)S(1)}, bf16[256,512]{1,0:T(8,128)(2,1)S(1)}, u32[]{:S(2)}, u32[]{:S(2)}) collective-permute-start(bf16[256,512]{1,0:T(8,128)(2,1)S(1)} %convolution_convert_fusion.refs_0_), channel_id=1, source_target_pairs={{0,2},{2,4},{4,6},{6,7},{7,5},{5,3},{3,1},{1,0},{8,10},{10,12},{12... | collective-permute-start | bytes 786440 | tf_op jit(solution)/shard_map/ppermute | solution.py:295
  15.2 8.1 %collective-permute-start = (bf16[256,512]{1,0:T(8,128)(2,1)S(1)}, bf16[256,512]{1,0:T(8,128)(2,1)S(1)}, u32[]{:S(2)}, u32[]{:S(2)}) collective-permute-start(bf16[256,512]{1,0:T(8,128)(2,1)S(1)} %convolution_convert_fusion.refs_0_), channel_id=1, source_target_pairs={{0,1},{2,0},{4,2},{6,4},{7,6},{5,7},{3,5},{1,3},{8,9},{10,8},{12,1... | collective-permute-start | bytes 786440 | tf_op jit(solution)/shard_map/ppermute | solution.py:297
  21.4 21.8 %copy-start.11 = (bf16[256,512]{1,0:T(8,128)(2,1)}, bf16[256,512]{1,0:T(8,128)(2,1)S(1)}, u32[]{:S(2)}) copy-start(bf16[256,512]{1,0:T(8,128)(2,1)S(1)} %collective-permute-done.3.refs_7_) | copy-start | bytes 786436
  21.4 7.5 %collective-permute-start.4 = (bf16[256,512]{1,0:T(8,128)(2,1)S(1)}, bf16[256,512]{1,0:T(8,128)(2,1)S(1)}, u32[]{:S(2)}, u32[]{:S(2)}) collective-permute-start(bf16[256,512]{1,0:T(8,128)(2,1)S(1)} %collective-permute-done.3.refs_7_), channel_id=1, source_target_pairs={{0,2},{2,4},{4,6},{6,7},{7,5},{5,3},{3,1},{1,0},{8,10},{10,12},{12... | collective-permute-start | bytes 786440 | tf_op jit(solution)/shard_map/ppermute | solution.py:295
  23.2 20.0 %copy-start.12 = (bf16[256,512]{1,0:T(8,128)(2,1)}, bf16[256,512]{1,0:T(8,128)(2,1)S(1)}, u32[]{:S(2)}) copy-start(bf16[256,512]{1,0:T(8,128)(2,1)S(1)} %collective-permute-done.refs_1_) | copy-start | bytes 786436
  23.2 7.2 %collective-permute-start.1 = (bf16[256,512]{1,0:T(8,128)(2,1)S(1)}, bf16[256,512]{1,0:T(8,128)(2,1)S(1)}, u32[]{:S(2)}, u32[]{:S(2)}) collective-permute-start(bf16[256,512]{1,0:T(8,128)(2,1)S(1)} %collective-permute-done.refs_1_), channel_id=1, source_target_pairs={{0,1},{2,0},{4,2},{6,4},{7,6},{5,7},{3,5},{1,3},{8,9},{10,8},{12,1... | collective-permute-start | bytes 786440 | tf_op jit(solution)/shard_map/ppermute | solution.py:297
  28.9 14.3 %copy-start.13 = (bf16[256,512]{1,0:T(8,128)(2,1)}, bf16[256,512]{1,0:T(8,128)(2,1)S(1)}, u32[]{:S(2)}) copy-start(bf16[256,512]{1,0:T(8,128)(2,1)S(1)} %collective-permute-done.4.refs_6_) | copy-start | bytes 786436
  28.9 6.7 %collective-permute-start.5 = (bf16[256,512]{1,0:T(8,128)(2,1)S(1)}, bf16[256,512]{1,0:T(8,128)(2,1)S(1)}, u32[]{:S(2)}, u32[]{:S(2)}) collective-permute-start(bf16[256,512]{1,0:T(8,128)(2,1)S(1)} %collective-permute-done.4.refs_6_), channel_id=1, source_target_pairs={{0,2},{2,4},{4,6},{6,7},{7,5},{5,3},{3,1},{1,0},{8,10},{10,12},{12... | collective-permute-start | bytes 786440 | tf_op jit(solution)/shard_map/ppermute | solution.py:295
  30.4 12.8 %copy-start.14 = (bf16[256,512]{1,0:T(8,128)(2,1)}, bf16[256,512]{1,0:T(8,128)(2,1)S(1)}, u32[]{:S(2)}) copy-start(bf16[256,512]{1,0:T(8,128)(2,1)S(1)} %collective-permute-done.1.refs_2_) | copy-start | bytes 786436
  30.4 20.7 %collective-permute-start.2 = (bf16[256,512]{1,0:T(8,128)(2,1)S(1)}, bf16[256,512]{1,0:T(8,128)(2,1)}, u32[]{:S(2)}, u32[]{:S(2)}) collective-permute-start(bf16[256,512]{1,0:T(8,128)(2,1)S(1)} %collective-permute-done.1.refs_2_), channel_id=1, source_target_pairs={{0,1},{2,0},{4,2},{6,4},{7,6},{5,7},{3,5},{1,3},{8,9},{10,8},{12,1... | collective-permute-start | bytes 786440 | tf_op jit(solution)/shard_map/ppermute | solution.py:297
  35.5 7.7 %copy-start.15 = (bf16[256,512]{1,0:T(8,128)(2,1)}, bf16[256,512]{1,0:T(8,128)(2,1)S(1)}, u32[]{:S(2)}) copy-start(bf16[256,512]{1,0:T(8,128)(2,1)S(1)} %collective-permute-done.5.refs_5_) | copy-start | bytes 786436
  35.5 15.6 %collective-permute-start.6 = (bf16[256,512]{1,0:T(8,128)(2,1)S(1)}, bf16[256,512]{1,0:T(8,128)(2,1)}, u32[]{:S(2)}, u32[]{:S(2)}) collective-permute-start(bf16[256,512]{1,0:T(8,128)(2,1)S(1)} %collective-permute-done.5.refs_5_), channel_id=1, source_target_pairs={{0,2},{2,4},{4,6},{6,7},{7,5},{5,3},{3,1},{1,0},{8,10},{10,12},{12... | collective-permute-start | bytes 786440 | tf_op jit(solution)/shard_map/ppermute | solution.py:295
  37.5 8.4 %collective-permute-start.7 = (bf16[256,256]{1,0:T(8,128)(2,1)S(1)}, bf16[256,256]{1,0:T(8,128)(2,1)S(1)}, u32[]{:S(2)}, u32[]{:S(2)}) collective-permute-start(bf16[256,256]{1,0:T(8,128)(2,1)S(1)} %get-tuple-element.45), channel_id=1, source_target_pairs={{0,8},{8,16},{16,24},{24,0},{1,9},{9,17},{17,25},{25,1},{2,10},{10... | collective-permute-start | bytes 393224 | tf_op jit(solution)/shard_map/ppermute | solution.py:284
  37.5 9.2 %collective-permute-start.8 = (bf16[256,256]{1,0:T(8,128)(2,1)S(1)}, bf16[256,256]{1,0:T(8,128)(2,1)S(1)}, u32[]{:S(2)}, u32[]{:S(2)}) collective-permute-start(bf16[256,256]{1,0:T(8,128)(2,1)S(1)} %get-tuple-element.44), channel_id=1, source_target_pairs={{0,16},{8,24},{16,0},{24,8},{1,17},{9,25},{17,1},{25,9},{2,18},{10... | collective-permute-start | bytes 393224 | tf_op jit(solution)/shard_map/ppermute | solution.py:284
  39.0 12.1 %collective-permute-start.9 = (bf16[256,256]{1,0:T(8,128)(2,1)S(1)}, bf16[256,256]{1,0:T(8,128)(2,1)S(1)}, u32[]{:S(2)}, u32[]{:S(2)}) collective-permute-start(bf16[256,256]{1,0:T(8,128)(2,1)S(1)} %get-tuple-element.43), channel_id=1, source_target_pairs={{0,24},{8,0},{16,8},{24,16},{1,25},{9,1},{17,9},{25,17},{2,26},{10... | collective-permute-start | bytes 393224 | tf_op jit(solution)/shard_map/ppermute | solution.py:284
  43.2 12.7 %copy-start.9 = (s32[32,8]{0,1:T(8,128)S(1)}, s32[32,8]{0,1:T(8,128)}, u32[]{:S(2)}) copy-start(s32[32,8]{0,1:T(8,128)} %param.16) | copy-start | bytes 3076
  45.8 37.4 %copy-start.5 = (bf16[256,256]{1,0:T(8,128)(2,1)}, bf16[256,256]{1,0:T(8,128)(2,1)S(1)}, u32[]{:S(2)}) copy-start(bf16[256,256]{1,0:T(8,128)(2,1)S(1)} %collective-permute-done.7.refs_3_) | copy-start | bytes 393220
  46.6 36.6 %copy-start.6 = (bf16[256,256]{1,0:T(8,128)(2,1)}, bf16[256,256]{1,0:T(8,128)(2,1)S(1)}, u32[]{:S(2)}) copy-start(bf16[256,256]{1,0:T(8,128)(2,1)S(1)} %collective-permute-done.8.refs_4_) | copy-start | bytes 393220
  51.1 32.1 %copy-start.7 = (bf16[256,256]{1,0:T(8,128)(2,1)}, bf16[256,256]{1,0:T(8,128)(2,1)S(1)}, u32[]{:S(2)}) copy-start(bf16[256,256]{1,0:T(8,128)(2,1)S(1)} %collective-permute-done.9.refs_5_) | copy-start | bytes 393220
  51.1 32.3 %all-to-all-start = ((bf16[8,64,1024]{2,1,0:T(8,128)(2,1)}), bf16[8,64,1024]{2,1,0:T(8,128)(2,1)S(1)}, u32[]{:S(2)}, u32[]{:S(2)}) async-start(bf16[8,64,1024]{2,1,0:T(8,128)(2,1)} %bitcast.3), calls=%async_computation | async-start | bytes 2097152 | tf_op jit(solution)/shard_map/all_to_all | solution.py:346
  55.9 132.9 %all-gather.5.cloned.1.call-start = ((), (), s32[]{:S(2)}) async-start(), calls=%async_computation.4 | async-start | bytes 10485760 | tf_op jit(solution)/shard_map/all_gather | solution.py:353
  83.4 32.0 %copy-start = (bf16[8,64,1024]{2,1,0:T(8,128)(2,1)}, bf16[8,64,1024]{2,1,0:T(8,128)(2,1)S(1)}, u32[]{:S(2)}) copy-start(bf16[8,64,1024]{2,1,0:T(8,128)(2,1)S(1)} %all-to-all-done.tokens_ref) | copy-start | bytes 3145732
  126.8 31.0 %all-to-all-start.3 = ((bf16[32,64,256]{2,1,0:T(8,128)(2,1)}), bf16[32,64,256]{2,1,0:T(8,128)(2,1)S(1)}, u32[]{:S(2)}, u32[]{:S(2)}) async-start(bf16[32,64,256]{2,1,0:T(8,128)(2,1)} %bitcast.34), calls=%async_computation.3 | async-start | bytes 2097152 | tf_op jit(solution)/shard_map/all_to_all | solution.py:358
  157.8 31.0 %copy-start.1 = (bf16[32,64,256]{2,1,0:T(8,128)(2,1)}, bf16[32,64,256]{2,1,0:T(8,128)(2,1)S(1)}, u32[]{:S(2)}) copy-start(bf16[32,64,256]{2,1,0:T(8,128)(2,1)S(1)} %all-to-all-done.3) | copy-start | bytes 3145732
Sparse Core Ops, SparseCore 0:
  10.1 66.5 all-gather.6
  83.6 70.3 all-gather.4

commit v5 on v4

--- a/solution.py
+++ b/solution.py
@@ -41,11 +41,11 @@
     return jnp.where(lax.rem(tok, 2) == 0, half, n_tok - 1 - half)
 
 
-def cross_kernel(lists_ref, counts_ref, tok_ref, tokens_ref, gain_ref, wq_ref, *refs):
-    kv_refs = refs[:-4]
-    out_ref, k_ref, vt_ref, q_ref = refs[-4:]
+def cross_kernel(halves, lists_ref, counts_ref, tok_ref, tokens_ref, gain_ref, wq_ref, *refs):
+    kv_refs, out_refs = refs[: -4 - halves], refs[-4 - halves : -4]
+    k_ref, vt_ref, q_ref, mixed_ref = refs[-4:]
     step = pl.program_id(0)
-    rows, cols = out_ref.shape
+    rows, cols = mixed_ref.shape
     heads = cols // HD
     per_step = rows // BLOCK
     listed = lists_ref.shape[1]
@@ -90,10 +90,15 @@
         mixed_t = f32_dot(values_t, jnp.concatenate(weights, axis=0)) / total
         for h in range(heads):
             part = slice(h * HD, (h + 1) * HD)
-            out_ref[pl.ds(row_start, BLOCK), part] = mixed_t[part, part].T.astype(jnp.bfloat16)
+            mixed_ref[pl.ds(row_start, BLOCK), part] = mixed_t[part, part].T.astype(jnp.bfloat16)
         return carry
 
     lax.fori_loop(0, per_step, one_block, 0, unroll=True)
+    half_steps = pl.num_programs(0) // halves
+    for half, out_ref in enumerate(out_refs):
+        @pl.when(lax.div(step, half_steps) == half)
+        def _():
+            out_ref[...] = mixed_ref[...]
 
 
 def cross_attention(hires_tokens, gain, w_cross_q, kv_chunks, block_lists, block_counts):
@@ -102,10 +107,12 @@
     cols = w_cross_q.shape[1]
     chunk = kv_chunks[0].shape[0]
     low_rows = chunk * len(kv_chunks)
-    rows = math.gcd(tok_rows, 4 * BLOCK)
+    halves = 2 if tok_rows % (2 * BLOCK) == 0 else 1
+    rows = math.gcd(tok_rows // halves, 4 * BLOCK)
+    half_steps = tok_rows // halves // rows
     return pl.pallas_call(
-        cross_kernel,
-        out_shape=jax.ShapeDtypeStruct((tok_rows, cols), jnp.bfloat16),
+        functools.partial(cross_kernel, halves),
+        out_shape=[jax.ShapeDtypeStruct((tok_rows // halves, cols), jnp.bfloat16)] * halves,
         grid_spec=pltpu.PrefetchScalarGridSpec(
             num_scalar_prefetch=3,
             grid=(tok_rows // rows,),
@@ -115,10 +122,17 @@
                 pl.BlockSpec((width, cols), lambda i, *_: (0, 0)),
             ]
             + [pl.BlockSpec((chunk, 2 * cols), lambda i, *_: (0, 0)) for _ in kv_chunks],
-            out_specs=pl.BlockSpec((rows, cols), lambda i, *_: (i, 0)),
+            out_specs=[
+                pl.BlockSpec(
+                    (rows, cols),
+                    lambda i, *_, half=half: (jnp.clip(i - half * half_steps, 0, half_steps - 1), 0),
+                )
+                for half in range(halves)
+            ],
             scratch_shapes=[
                 pltpu.VMEM((low_rows, cols), jnp.bfloat16),
                 pltpu.VMEM((cols, low_rows), jnp.bfloat16),
+                pltpu.VMEM((rows, cols), jnp.bfloat16),
                 pltpu.VMEM((rows, cols), jnp.bfloat16),
             ],
         ),
@@ -133,7 +147,7 @@
 
 
 def view_kernel(
-    tokens_ref, gain_ref, w_ref, wo_ref, out_ref, normed_ref, qkv_ref, mixed_ref
+    first_row, tokens_ref, gain_ref, w_ref, wo_ref, out_ref, normed_ref, qkv_ref, mixed_ref
 ):
     parts, sources, run, cols = out_ref.shape
     part_index = pl.program_id(0)
@@ -146,9 +160,10 @@
     @pl.when(pl.program_id(0) == 0)
     def _():
         gain = gain_ref[...]
-        step = max(1, tile // run)
+        step = math.gcd(sources, max(1, tile // run))
         for s in range(0, sources, step):
-            tokens = tokens_ref[s : s + step].reshape(step * run, gain.shape[1])
+            tokens = tokens_ref[s : s + step, first_row : first_row + run]
+            tokens = tokens.reshape(step * run, gain.shape[1])
             normed_ref[s * run : (s + step) * run] = rms_rows(tokens, gain)
 
     for start in range(0, rows, tile):
@@ -189,7 +204,7 @@
 
     @pl.when(part_index == parts - 1)
     def _():
-        step = max(1, tile // run)
+        step = math.gcd(sources, max(1, tile // run))
         for s in range(0, sources, step):
             rows_of = slice(s * run, (s + step) * run)
             for column in range(parts):
@@ -200,16 +215,16 @@
                 out_ref[column, s : s + step] = term.astype(jnp.bfloat16).reshape(step, run, cols)
 
 
-def view_attention(tokens, gain, weights):
-    n_tok, run, width = tokens.shape
+def view_attention(tokens, gain, weights, first_row, run):
+    n_tok, whole_run, width = tokens.shape
     parts, _, _, cols = weights.shape
     rows = n_tok * run
     return pl.pallas_call(
-        view_kernel,
+        functools.partial(view_kernel, first_row),
         out_shape=jax.ShapeDtypeStruct((parts, n_tok, run, cols), jnp.bfloat16),
         grid=(parts,),
         in_specs=[
-            pl.BlockSpec((n_tok, run, width), lambda i: (0, 0, 0)),
+            pl.BlockSpec((n_tok, whole_run, width), lambda i: (0, 0, 0)),
             pl.BlockSpec((1, width), lambda i: (0, 0)),
             pl.BlockSpec((1, 3, width, cols), lambda i: (i, 0, 0, 0)),
             pl.BlockSpec((parts, 1, width, cols), lambda i: (0, 3, 0, 0)),
@@ -230,38 +245,59 @@
     )(tokens, gain, weights, weights)
 
 
-def final_kernel(chunks, index_ref, tokens_ref, cross_ref, *refs):
-    view_refs, w_refs, out_ref = refs[:chunks], refs[chunks:-1], refs[-1]
+def final_kernel(bounds, halves, index_ref, tokens_ref, *refs):
+    chunks = len(bounds) - 1
+    cross_refs, view_refs = refs[:halves], refs[halves : halves + chunks]
+    w_refs, out_ref = refs[halves + chunks : -1], refs[-1]
     parts = len(w_refs)
-    total = tokens_ref[...].astype(jnp.float32)
-    for k, w_ref in enumerate(w_refs):
-        group = lax.rem(index_ref[0] + parts - k, parts)
-        total = total + f32_dot(cross_ref[group], w_ref[...])
-    for chunk, view_ref in enumerate(view_refs):
-        @pl.when(pl.program_id(1) == chunk)
+    sources, run, cols = out_ref.shape
+    half_steps = pl.num_programs(0) // halves
+    for half, cross_ref in enumerate(cross_refs):
+        @pl.when(lax.div(pl.program_id(0), half_steps) == half)
         def _():
-            out_ref[...] = (total + view_ref[0].astype(jnp.float32)).astype(jnp.bfloat16)
-
-
-def final_sum(head_index, hires_tokens, cross_all, view_terms, w_columns):
-    parts, tok_rows, cols = cross_all.shape
-    n_head, rows, _ = view_terms[0].shape
-    chunks = len(view_terms)
-    view_spec = pl.BlockSpec((1, rows, cols), lambda h, c, index: (h, 0, 0))
-    w_spec = pl.BlockSpec((cols, cols), lambda h, c, index: (0, 0))
-    return pl.pallas_call(
-        functools.partial(final_kernel, chunks),
-        out_shape=jax.ShapeDtypeStruct((tok_rows, cols), jnp.bfloat16),
+            total = tokens_ref[...].reshape(sources * run, cols).astype(jnp.float32)
+            for k, w_ref in enumerate(w_refs):
+                group = lax.rem(index_ref[0] + parts - k, parts)
+                total = total + f32_dot(cross_ref[group].reshape(sources * run, cols), w_ref[...])
+            total = total.reshape(sources, run, cols)
+            for view_ref, low, high in zip(view_refs, bounds, bounds[1:]):
+                terms = total[:, low:high] + view_ref[...].astype(jnp.float32)
+                out_ref[:, low:high] = terms.astype(jnp.bfloat16)
+
+
+def final_sum(head_index, hires_tokens, cross_all, view_terms, w_columns, bounds):
+    halves = len(cross_all)
+    parts, half_rows, cols = cross_all[0].shape
+    tok_rows = half_rows * halves
+    width = hires_tokens.shape[1]
+    places, run = view_terms[0].shape[0], bounds[-1]
+    sources = math.gcd(places // halves, 4)
+    half_steps = places // halves // sources
+    w_spec = pl.BlockSpec((cols, cols), lambda i, index: (0, 0))
+    out = pl.pallas_call(
+        functools.partial(final_kernel, bounds, halves),
+        out_shape=jax.ShapeDtypeStruct((places, run, cols), jnp.bfloat16),
         grid_spec=pltpu.PrefetchScalarGridSpec(
             num_scalar_prefetch=1,
-            grid=(n_head, chunks),
+            grid=(places // sources,),
             in_specs=[
-                pl.BlockSpec((rows, cols), lambda h, c, index: (h * chunks + c, index[0])),
-                pl.BlockSpec((parts, rows, cols), lambda h, c, index: (0, h * chunks + c, 0)),
+                pl.BlockSpec((sources, run, cols), lambda i, index: (i, 0, index[0])),
             ]
-            + [view_spec] * chunks
+            + [
+                pl.BlockSpec(
+                    (parts, sources, run, cols),
+                    lambda i, index, half=half: (
+                        0, jnp.clip(i - half * half_steps, 0, half_steps - 1), 0, 0
+                    ),
+                )
+                for half in range(halves)
+            ]
+            + [
+                pl.BlockSpec((sources, term.shape[1], cols), lambda i, index: (i, 0, 0))
+                for term in view_terms
+            ]
             + [w_spec] * parts,
-            out_specs=pl.BlockSpec((rows, cols), lambda h, c, index: (h * chunks + c, 0)),
+            out_specs=pl.BlockSpec((sources, run, cols), lambda i, index: (i, 0, 0)),
         ),
         compiler_params=pltpu.CompilerParams(vmem_limit_bytes=VMEM_BYTES),
         cost_estimate=pl.CostEstimate(
@@ -270,20 +306,30 @@
             transcendentals=0,
         ),
         name="final",
-    )(head_index.reshape(1), hires_tokens, cross_all, *view_terms, *w_columns)
+    )(
+        head_index.reshape(1),
+        hires_tokens.reshape(places, run, width),
+        *[half.reshape(parts, places // halves, run, cols) for half in cross_all],
+        *view_terms,
+        *w_columns,
+    )
+    return out.reshape(tok_rows, cols)
 
 
 def column_blocks(rows_of_w, head_index, n_head):
     cols = rows_of_w.shape[1] // n_head
-    blocks = []
-    for k in range(n_head):
-        start = lax.rem(head_index + k, n_head) * cols
-        block = lax.dynamic_slice_in_dim(rows_of_w, start, cols, 1)
-        if k:
-            pairs = [(h, (h + k) % n_head) for h in range(n_head)]
-            block = lax.ppermute(block, "head", pairs)
-        blocks.append(block)
-    return blocks
+    return [
+        lax.dynamic_slice_in_dim(rows_of_w, lax.rem(head_index + k, n_head) * cols, cols, 1)
+        for k in range(n_head)
+    ]
+
+
+def send_blocks(blocks):
+    n_head = len(blocks)
+    return [
+        lax.ppermute(block, "head", [(h, (h + k) % n_head) for h in range(n_head)]) if k else block
+        for k, block in enumerate(blocks)
+    ]
 
 
 def ring_chunks(own, n_tok):
@@ -318,8 +364,7 @@
     gain = norm_gain.reshape(1, width)
 
     run = quarter // n_tok
-    chunks = 2 if run % 32 == 0 else 1
-    run = run // chunks
+    bounds = (0, run // 4, run) if run % 64 == 0 else (0, run)
 
     own_weights = jnp.concatenate(
         [
@@ -334,33 +379,30 @@
     ).astype(jnp.bfloat16)
     kv_chunks = ring_chunks(low_kv, n_tok)
     w_columns = column_blocks(w_out[0], head_index, n_head)
-    sent = [
-        lax.dynamic_slice_in_dim(
-            hires_tokens, head_index * quarter + chunk * n_tok * run, n_tok * run, 0
-        ).reshape(n_tok, run, width)
-        for chunk in range(chunks)
-    ]
+    sent = lax.dynamic_slice_in_dim(hires_tokens, head_index * quarter, quarter, 0)
     kv_chunks, sent, w_columns = lax.optimization_barrier((kv_chunks, sent, w_columns))
 
-    def arrive(rows):
-        return lax.all_to_all(rows, "tok", split_axis=0, concat_axis=0, tiled=True)
-
-    arrived = [arrive(sent[0])]
+    arrived = lax.all_to_all(
+        sent.reshape(n_tok, run, width), "tok", split_axis=0, concat_axis=0, tiled=True
+    )
     cross_out = cross_attention(
         hires_tokens, gain, w_cross_q, kv_chunks, block_lists, block_counts
     )
-    cross_out, arrived, sent = lax.optimization_barrier((cross_out, arrived, sent))
-    cross_all = lax.all_gather(cross_out, "head", axis=0, tiled=False)
-    arrived.extend(arrive(rows) for rows in sent[1:])
+    w_columns = send_blocks(w_columns)
+    arrived, w_columns, last_half = lax.optimization_barrier((arrived, w_columns, cross_out[-1]))
+    cross_all = [
+        lax.all_gather(half, "head", axis=0, tiled=False) for half in [*cross_out[:-1], last_half]
+    ]
     view_terms = []
-    for tokens in arrived:
-        term = view_attention(tokens, gain, weights)
-        term = lax.all_to_all(
-            term.reshape(n_head * n_tok, run, cols),
-            ("head", "tok"), split_axis=0, concat_axis=0, tiled=True,
+    for low, high in zip(bounds, bounds[1:]):
+        term = view_attention(arrived, gain, weights, low, high - low)
+        view_terms.append(
+            lax.all_to_all(
+                term.reshape(n_head * n_tok, high - low, cols),
+                ("head", "tok"), split_axis=0, concat_axis=0, tiled=True,
+            )
         )
-        view_terms.append(term.reshape(n_head, n_tok * run, cols))
-    return final_sum(head_index, hires_tokens, cross_all, view_terms, w_columns)
+    return final_sum(head_index, hires_tokens, cross_all, view_terms, w_columns, bounds)
 
 
 def solution(mesh):

time: 206 us -> 213 us (1.034)
  blocking collectives: 62.9 us -> 0 us
  waiting for transfers between devices: 40.4 us -> 98.7 us
  starting transfers between devices: 19.6 us -> 25.5 us
  local copies, waits for them, and re-layouts: 7.42 us -> 10.9 us
  Pallas kernels: 59.4 us -> 61.8 us
    all_to_all x2 -> x0, blocking collectives: 62.9 us -> none  [the longest x1 31.9 us: arrive(): return lax.all_to_all(rows, 'tok', split_axis=0, concat_axis=0, tiled=True)]
    all_to_all x2 -> x3, waiting for transfers between devices: 16.2 us -> 71.3 us  [the longest x2 36.2 us: shards(): lax.all_to_all(term.reshape(n_head * n_tok, high - low, cols), ('head', '...]
    all_to_all x2 -> x3, starting transfers between devices: 8.21 us -> 14.1 us  [the longest x2 8.72 us: shards(): lax.all_to_all(term.reshape(n_head * n_tok, high - low, cols), ('head', '...]
    all_gather x1 -> x2, waiting for transfers between devices: 0.01 us -> 3.29 us  [shards(): lax.all_gather(half, 'head', axis=0, tiled=False)]
    unnamed x34 -> x40, local copies, waits for them, and re-layouts: 2.15 us -> 5.24 us
    pallas_call x4, Pallas kernels: 59.4 us -> 61.8 us  [the longest x1 27 us: cross_attention(): pl.pallas_call(functools.partial(cross_kernel, halves), out_shape=[jax.Sh...]
  transfers between devices with their start and end apart: 14 -> 16, of which waited for: 8 -> 11; matrix products, arithmetic and copies ran while one was open for 2% -> 3% of each run, Pallas kernels for 24% -> 25%
where the time goes in v5:
time: 213 us; the launch traced here: 212 us
  waiting for transfers between devices  98.7 us (46%)
  Pallas kernels  61.8 us (29%)
  starting transfers between devices  25.5 us (12%)
  between operations  13.3 us (6%)
  local copies, waits for them, and re-layouts  10.9 us (5%)
    all_to_all x2, waiting for transfers between devices, shards(): lax.all_to_all(term.reshape(n_head * n_tok, high - low, cols), ('head', '...  36.2 us
    all_to_all x1, waiting for transfers between devices, shards(): lax.all_to_all(sent.reshape(n_tok, run, width), 'tok', split_axis=0, conc...  35.1 us
    pallas_call x1, Pallas kernels, cross_attention(): pl.pallas_call(functools.partial(cross_kernel, halves), out_shape=[jax.Sh...  27 us
    pallas_call x2, Pallas kernels, view_attention(): pl.pallas_call(functools.partial(view_kernel, first_row), out_shape=jax.S...  25.2 us
    ppermute x4, waiting for transfers between devices, ring_chunks(): behind.append(lax.ppermute(behind[-1], 'tok', upward))  16.9 us
    pallas_call x1, Pallas kernels, final_sum(): pl.pallas_call(functools.partial(final_kernel, bounds, halves), out_shape...  9.55 us
    all_to_all x2, starting transfers between devices, shards(): lax.all_to_all(term.reshape(n_head * n_tok, high - low, cols), ('head', '...  8.72 us
    ppermute x4, starting transfers between devices, ring_chunks(): behind.append(lax.ppermute(behind[-1], 'tok', upward))  7.59 us
  transfers between devices with their start and end apart: 16, of which 11 were waited for; matrix products, arithmetic and copies ran while one was open for 3% of the time, Pallas kernels for 25%

profile of v5, /device:TPU:0, one launch (start us, length us, event | category | flops | bytes accessed | tf_op | source)
XLA Modules:
  0.0 212.4 jit_solution(8229223408581665350)
XLA Ops:
  6.5 1.4 fusion.6
  7.9 0.4 reshape_squeeze.3
  8.3 0.1 copy.13
  8.4 1.5 pad_maximum_fusion
  9.9 0.0 all-gather.11.cloned.1.call-update
  10.0 0.0 all-gather.7.cloned.1.call-start
  10.0 1.1 copy-done.4
  11.2 0.2 copy.14
  11.4 0.2 fusion
  11.6 0.5 convolution_convert_fusion.refs_0_
  12.1 3.1 %collective-permute-start.3 = (bf16[256,512]{1,0:T(8,128)(2,1)S(1)}, bf16[256,512]{1,0:T(8,128)(2,1)S(1)}, u32[]{:S(2)}, u32[]{:S(2)}) collective-permute-start(bf16[256,512]{1,0:T(8,128)(2,1)S(1)} %convolution_convert_fusion.refs_0_), channel_id=1, source_target_pairs={{0,2},{2,4},{4,6},{6,7},{7,5},{5,3},{3,1},{1,0},{8,10},{10,12},{12... | collective-permute-start | bytes 786440 | tf_op jit(solution)/shard_map/ppermute | solution.py:341
  15.2 6.2 %collective-permute-done.3.refs_7_ = bf16[256,512]{1,0:T(8,128)(2,1)S(1)} collective-permute-done((bf16[256,512]{1,0:T(8,128)(2,1)S(1)}, bf16[256,512]{1,0:T(8,128)(2,1)S(1)}, u32[]{:S(2)}, u32[]{:S(2)}) %collective-permute-start.3) | collective-permute-done | bytes 262176 | tf_op jit(solution)/shard_map/ppermute | solution.py:341
  21.4 1.8 collective-permute-start.4
  23.2 0.2 collective-permute-start.1
  23.4 5.5 %collective-permute-done.4.refs_6_ = bf16[256,512]{1,0:T(8,128)(2,1)S(1)} collective-permute-done((bf16[256,512]{1,0:T(8,128)(2,1)S(1)}, bf16[256,512]{1,0:T(8,128)(2,1)S(1)}, u32[]{:S(2)}, u32[]{:S(2)}) %collective-permute-start.4) | collective-permute-done | bytes 262176 | tf_op jit(solution)/shard_map/ppermute | solution.py:341
  28.9 1.5 collective-permute-start.5
  30.4 0.7 copy.12.lists_ref
  31.1 0.5 collective-permute-start.2
  31.6 4.0 %collective-permute-done.5.refs_5_ = bf16[256,512]{1,0:T(8,128)(2,1)S(1)} collective-permute-done((bf16[256,512]{1,0:T(8,128)(2,1)S(1)}, bf16[256,512]{1,0:T(8,128)(2,1)S(1)}, u32[]{:S(2)}, u32[]{:S(2)}) %collective-permute-start.5) | collective-permute-done | bytes 262176 | tf_op jit(solution)/shard_map/ppermute | solution.py:341
  35.6 1.2 collective-permute-start.6
  36.8 0.7 dynamic-slice_bitcast_fusion
  37.5 3.1 %constant_dynamic-slice_fusion = bf16[1024,1024]{1,0:T(8,128)(2,1)} fusion(bf16[4096,1024]{1,0:T(8,128)(2,1)} %tokens_ref.1, s32[]{:T(128)S(6)} %select_n.15), kind=kLoop, calls=%fused_computation.13 | loop fusion | bytes 4194308 | tf_op jit(solution)/shard_map/dynamic_slice | solution.py:382
  40.6 1.3 collective-permute-done.6.refs_4_
  42.0 0.7 copy-done.18
  42.7 27.0 %cross.1 = (bf16[2048,256]{1,0:T(8,128)(2,1)}, bf16[2048,256]{1,0:T(8,128)(2,1)}) custom-call(s32[32,8]{1,0:T(8,128)} %copy.12.lists_ref, s32[32]{0:T(128)} %counts_ref.1, s32[1]{0:T(128)} %bitcast.2.tok_ref, bf16[4096,1024]{1,0:T(8,128)(2,1)} %tokens_ref.1, f32[1,1024]{1,0:T(1,128)} %bitcast.39, bf16[1024,256]{1,0:T(8,128)(2,1)} %wq_ref.1, ...), custom_call_target="tpu_custom_call" | custom-call | flops 10737418240 | bytes 10485760 | tf_op jit(solution)/shard_map/cross/pallas_call | solution.py:113
  69.7 0.0 all-gather.7.cloned.1.call-update
  69.7 5.4 %all-to-all-start = ((bf16[8,128,1024]{2,1,0:T(8,128)(2,1)}), bf16[8,128,1024]{2,1,0:T(8,128)(2,1)S(1)}, u32[]{:S(2)}, u32[]{:S(2)}) async-start(bf16[8,128,1024]{2,1,0:T(8,128)(2,1)} %bitcast.9), calls=%async_computation | async-start | bytes 4194304 | tf_op jit(solution)/shard_map/all_to_all | solution.py:385
  75.1 0.0 all-gather.9.cloned.1.call-start
  75.1 0.1 collective-permute-start.7
  75.2 1.6 collective-permute-start.8
  76.8 1.4 collective-permute-start.9
  78.2 2.2 %collective-permute-done.7.refs_5_ = bf16[256,256]{1,0:T(8,128)(2,1)S(1)} collective-permute-done((bf16[256,256]{1,0:T(8,128)(2,1)S(1)}, bf16[256,256]{1,0:T(8,128)(2,1)S(1)}, u32[]{:S(2)}, u32[]{:S(2)}) %collective-permute-start.7) | collective-permute-done | bytes 131104 | tf_op jit(solution)/shard_map/ppermute | solution.py:330
  80.4 1.2 collective-permute-done.8.refs_6_
  81.6 3.6 %collective-permute-done.9.refs_7_ = bf16[256,256]{1,0:T(8,128)(2,1)S(1)} collective-permute-done((bf16[256,256]{1,0:T(8,128)(2,1)S(1)}, bf16[256,256]{1,0:T(8,128)(2,1)S(1)}, u32[]{:S(2)}, u32[]{:S(2)}) %collective-permute-start.9) | collective-permute-done | bytes 131104 | tf_op jit(solution)/shard_map/ppermute | solution.py:330
  85.2 35.1 %all-to-all-done.tokens_ref = bf16[8,128,1024]{2,1,0:T(8,128)(2,1)S(1)} async-done(((bf16[8,128,1024]{2,1,0:T(8,128)(2,1)}), bf16[8,128,1024]{2,1,0:T(8,128)(2,1)S(1)}, u32[]{:S(2)}, u32[]{:S(2)}) %all-to-all-start) | async-done | bytes 2097184 | tf_op jit(solution)/shard_map/all_to_all | solution.py:385
  120.4 0.0 all-gather.9.cloned.1.call-update
  120.4 0.0 all-gather.11.cloned.1.call-done
  120.4 1.3 copy-done
  121.7 9.7 %view.2 = bf16[4,8,32,256]{3,2,1,0:T(8,128)(2,1)} custom-call(bf16[8,128,1024]{2,1,0:T(8,128)(2,1)} %copy-done, f32[1,1024]{1,0:T(1,128)} %bitcast.40, bf16[4,4,1024,256]{3,2,1,0:T(8,128)(2,1)} %bitcast.26, bf16[4,4,1024,256]{3,2,1,0:T(8,128)(2,1)} %bitcast.27), custom_call_target="tpu_custom_call" | custom-call | flops 2415919104 | bytes 9437184 | tf_op jit(solution)/shard_map/view/pallas_call | solution.py:222
  131.4 3.7 %all-to-all-start.1 = ((bf16[32,32,256]{2,1,0:T(8,128)(2,1)}), bf16[32,32,256]{2,1,0:T(8,128)(2,1)S(1)}, u32[]{:S(2)}, u32[]{:S(2)}) async-start(bf16[32,32,256]{2,1,0:T(8,128)(2,1)} %bitcast.34), calls=%async_computation.1 | async-start | bytes 1048576 | tf_op jit(solution)/shard_map/all_to_all | solution.py:400
  135.2 15.5 %view.3 = bf16[4,8,96,256]{3,2,1,0:T(8,128)(2,1)} custom-call(bf16[8,128,1024]{2,1,0:T(8,128)(2,1)} %copy-done, f32[1,1024]{1,0:T(1,128)} %bitcast.41, bf16[4,4,1024,256]{3,2,1,0:T(8,128)(2,1)} %bitcast.28, bf16[4,4,1024,256]{3,2,1,0:T(8,128)(2,1)} %bitcast.29), custom_call_target="tpu_custom_call" | custom-call | flops 7247757312 | bytes 11534336 | tf_op jit(solution)/shard_map/view/pallas_call | solution.py:222
  150.7 0.7 all-to-all-done.1.refs_2_
  151.3 5.0 %all-to-all-start.2 = ((bf16[32,96,256]{2,1,0:T(8,128)(2,1)}), bf16[32,96,256]{2,1,0:T(8,128)(2,1)S(1)}, u32[]{:S(2)}, u32[]{:S(2)}) async-start(bf16[32,96,256]{2,1,0:T(8,128)(2,1)} %bitcast.35), calls=%async_computation.2 | async-start | bytes 3145728 | tf_op jit(solution)/shard_map/all_to_all | solution.py:400
  156.3 0.0 all-gather.7.cloned.1.call-done
  156.4 3.3 %all-gather.9.cloned.1.call-done = bf16[8192,256]{1,0:T(8,128)(2,1)} async-done(((bf16[2048,256]{1,0:T(8,128)(2,1)}), bf16[8192,256]{1,0:T(8,128)(2,1)}) %all-gather.9.cloned.1.call-update) | async-done | bytes 4194320 | tf_op jit(solution)/shard_map/all_gather | solution.py:394
  159.6 35.5 %all-to-all-done.2.refs_3_ = bf16[32,96,256]{2,1,0:T(8,128)(2,1)S(1)} async-done(((bf16[32,96,256]{2,1,0:T(8,128)(2,1)}), bf16[32,96,256]{2,1,0:T(8,128)(2,1)S(1)}, u32[]{:S(2)}, u32[]{:S(2)}) %all-to-all-start.2) | async-done | bytes 1572896 | tf_op jit(solution)/shard_map/all_to_all | solution.py:400
  195.2 1.2 copy-done.1
  196.3 9.5 %final.1 = bf16[32,128,256]{2,1,0:T(8,128)(2,1)} custom-call(s32[1]{0:T(128)} %bitcast.index_ref, bf16[32,128,1024]{2,1,0:T(8,128)(2,1)} %bitcast.30, bf16[4,16,128,256]{3,2,1,0:T(8,128)(2,1)} %bitcast.31, bf16[4,16,128,256]{3,2,1,0:T(8,128)(2,1)} %bitcast.32, bf16[32,32,256]{2,1,0:T(8,128)(2,1)} %copy-done.2, bf16[32,96,256]{2,1,0:T(8,128)(2,1)} %copy-done.1, ...), custom_call_target="tpu_custom_call" | custom-call | flops 2147483648 | bytes 14680064 | tf_op jit(solution)/shard_map/final/pallas_call | solution.py:277
  (40 shorter events, 0.1 us)
Async XLA Ops:
  6.5 1.9 copy-start.3
  6.5 113.9 %all-gather.11.cloned.1.call-start = ((), (), s32[]{:S(2)}) async-start(), calls=%async_computation.5 | async-start | bytes 10485760 | tf_op jit(solution)/shard_map/all_gather | solution.py:376
  9.9 1.2 copy-start.4
  9.9 1.5 copy-start.5
  9.9 1.7 copy-start.10
  10.0 146.4 %all-gather.7.cloned.1.call-start = ((), (), s32[]{:S(2)}) async-start(), calls=%async_computation.3 | async-start | bytes 5242880 | tf_op jit(solution)/shard_map/all_gather | solution.py:394
  11.2 19.2 %copy-start.9 = (s32[32,8]{0,1:T(8,128)S(1)}, s32[32,8]{0,1:T(8,128)}, u32[]{:S(2)}) copy-start(s32[32,8]{0,1:T(8,128)} %param.16) | copy-start | bytes 3076
  12.1 28.5 %copy-start.11 = (bf16[256,512]{1,0:T(8,128)(2,1)}, bf16[256,512]{1,0:T(8,128)(2,1)S(1)}, u32[]{:S(2)}) copy-start(bf16[256,512]{1,0:T(8,128)(2,1)S(1)} %convolution_convert_fusion.refs_0_) | copy-start | bytes 786436
  12.1 9.3 %collective-permute-start.3 = (bf16[256,512]{1,0:T(8,128)(2,1)S(1)}, bf16[256,512]{1,0:T(8,128)(2,1)S(1)}, u32[]{:S(2)}, u32[]{:S(2)}) collective-permute-start(bf16[256,512]{1,0:T(8,128)(2,1)S(1)} %convolution_convert_fusion.refs_0_), channel_id=1, source_target_pairs={{0,2},{2,4},{4,6},{6,7},{7,5},{5,3},{3,1},{1,0},{8,10},{10,12},{12... | collective-permute-start | bytes 786440 | tf_op jit(solution)/shard_map/ppermute | solution.py:341
  15.2 8.0 %collective-permute-start = (bf16[256,512]{1,0:T(8,128)(2,1)S(1)}, bf16[256,512]{1,0:T(8,128)(2,1)S(1)}, u32[]{:S(2)}, u32[]{:S(2)}) collective-permute-start(bf16[256,512]{1,0:T(8,128)(2,1)S(1)} %convolution_convert_fusion.refs_0_), channel_id=1, source_target_pairs={{0,1},{2,0},{4,2},{6,4},{7,6},{5,7},{3,5},{1,3},{8,9},{10,8},{12,1... | collective-permute-start | bytes 786440 | tf_op jit(solution)/shard_map/ppermute | solution.py:343
  21.4 19.2 %copy-start.12 = (bf16[256,512]{1,0:T(8,128)(2,1)}, bf16[256,512]{1,0:T(8,128)(2,1)S(1)}, u32[]{:S(2)}) copy-start(bf16[256,512]{1,0:T(8,128)(2,1)S(1)} %collective-permute-done.3.refs_7_) | copy-start | bytes 786436
  21.4 7.5 %collective-permute-start.4 = (bf16[256,512]{1,0:T(8,128)(2,1)S(1)}, bf16[256,512]{1,0:T(8,128)(2,1)S(1)}, u32[]{:S(2)}, u32[]{:S(2)}) collective-permute-start(bf16[256,512]{1,0:T(8,128)(2,1)S(1)} %collective-permute-done.3.refs_7_), channel_id=1, source_target_pairs={{0,2},{2,4},{4,6},{6,7},{7,5},{5,3},{3,1},{1,0},{8,10},{10,12},{12... | collective-permute-start | bytes 786440 | tf_op jit(solution)/shard_map/ppermute | solution.py:341
  23.2 17.4 %copy-start.13 = (bf16[256,512]{1,0:T(8,128)(2,1)}, bf16[256,512]{1,0:T(8,128)(2,1)S(1)}, u32[]{:S(2)}) copy-start(bf16[256,512]{1,0:T(8,128)(2,1)S(1)} %collective-permute-done.refs_1_) | copy-start | bytes 786436
  23.2 7.8 %collective-permute-start.1 = (bf16[256,512]{1,0:T(8,128)(2,1)S(1)}, bf16[256,512]{1,0:T(8,128)(2,1)S(1)}, u32[]{:S(2)}, u32[]{:S(2)}) collective-permute-start(bf16[256,512]{1,0:T(8,128)(2,1)S(1)} %collective-permute-done.refs_1_), channel_id=1, source_target_pairs={{0,1},{2,0},{4,2},{6,4},{7,6},{5,7},{3,5},{1,3},{8,9},{10,8},{12,1... | collective-permute-start | bytes 786440 | tf_op jit(solution)/shard_map/ppermute | solution.py:343
  28.9 11.7 %copy-start.14 = (bf16[256,512]{1,0:T(8,128)(2,1)}, bf16[256,512]{1,0:T(8,128)(2,1)S(1)}, u32[]{:S(2)}) copy-start(bf16[256,512]{1,0:T(8,128)(2,1)S(1)} %collective-permute-done.4.refs_6_) | copy-start | bytes 786436
  28.9 6.7 %collective-permute-start.5 = (bf16[256,512]{1,0:T(8,128)(2,1)S(1)}, bf16[256,512]{1,0:T(8,128)(2,1)S(1)}, u32[]{:S(2)}, u32[]{:S(2)}) collective-permute-start(bf16[256,512]{1,0:T(8,128)(2,1)S(1)} %collective-permute-done.4.refs_6_), channel_id=1, source_target_pairs={{0,2},{2,4},{4,6},{6,7},{7,5},{5,3},{3,1},{1,0},{8,10},{10,12},{12... | collective-permute-start | bytes 786440 | tf_op jit(solution)/shard_map/ppermute | solution.py:341
  31.1 9.5 %copy-start.15 = (bf16[256,512]{1,0:T(8,128)(2,1)}, bf16[256,512]{1,0:T(8,128)(2,1)S(1)}, u32[]{:S(2)}) copy-start(bf16[256,512]{1,0:T(8,128)(2,1)S(1)} %collective-permute-done.1.refs_2_) | copy-start | bytes 786436
  31.1 9.6 %collective-permute-start.2 = (bf16[256,512]{1,0:T(8,128)(2,1)S(1)}, bf16[256,512]{1,0:T(8,128)(2,1)S(1)}, u32[]{:S(2)}, u32[]{:S(2)}) collective-permute-start(bf16[256,512]{1,0:T(8,128)(2,1)S(1)} %collective-permute-done.1.refs_2_), channel_id=1, source_target_pairs={{0,1},{2,0},{4,2},{6,4},{7,6},{5,7},{3,5},{1,3},{8,9},{10,8},{12,1... | collective-permute-start | bytes 786440 | tf_op jit(solution)/shard_map/ppermute | solution.py:343
  35.6 5.0 %copy-start.16 = (bf16[256,512]{1,0:T(8,128)(2,1)}, bf16[256,512]{1,0:T(8,128)(2,1)S(1)}, u32[]{:S(2)}) copy-start(bf16[256,512]{1,0:T(8,128)(2,1)S(1)} %collective-permute-done.5.refs_5_) | copy-start | bytes 786436
  35.6 6.4 %collective-permute-start.6 = (bf16[256,512]{1,0:T(8,128)(2,1)S(1)}, bf16[256,512]{1,0:T(8,128)(2,1)S(1)}, u32[]{:S(2)}, u32[]{:S(2)}) collective-permute-start(bf16[256,512]{1,0:T(8,128)(2,1)S(1)} %collective-permute-done.5.refs_5_), channel_id=1, source_target_pairs={{0,2},{2,4},{4,6},{6,7},{7,5},{5,3},{3,1},{1,0},{8,10},{10,12},{12... | collective-permute-start | bytes 786440 | tf_op jit(solution)/shard_map/ppermute | solution.py:341
  40.6 1.3 copy-start.17
  41.9 0.7 copy-start.18
  69.7 50.6 %all-to-all-start = ((bf16[8,128,1024]{2,1,0:T(8,128)(2,1)}), bf16[8,128,1024]{2,1,0:T(8,128)(2,1)S(1)}, u32[]{:S(2)}, u32[]{:S(2)}) async-start(bf16[8,128,1024]{2,1,0:T(8,128)(2,1)} %bitcast.9), calls=%async_computation | async-start | bytes 4194304 | tf_op jit(solution)/shard_map/all_to_all | solution.py:385
  75.1 84.5 %all-gather.9.cloned.1.call-start = ((), (), s32[]{:S(2)}) async-start(), calls=%async_computation.4 | async-start | bytes 5242880 | tf_op jit(solution)/shard_map/all_gather | solution.py:394
  75.1 5.2 %collective-permute-start.7 = (bf16[256,256]{1,0:T(8,128)(2,1)S(1)}, bf16[256,256]{1,0:T(8,128)(2,1)S(1)}, u32[]{:S(2)}, u32[]{:S(2)}) collective-permute-start(bf16[256,256]{1,0:T(8,128)(2,1)S(1)} %get-tuple-element.37), channel_id=1, source_target_pairs={{0,8},{8,16},{16,24},{24,0},{1,9},{9,17},{17,25},{25,1},{2,10},{10... | collective-permute-start | bytes 393224 | tf_op jit(solution)/shard_map/ppermute | solution.py:330
  75.2 6.4 %collective-permute-start.8 = (bf16[256,256]{1,0:T(8,128)(2,1)S(1)}, bf16[256,256]{1,0:T(8,128)(2,1)S(1)}, u32[]{:S(2)}, u32[]{:S(2)}) collective-permute-start(bf16[256,256]{1,0:T(8,128)(2,1)S(1)} %get-tuple-element.38), channel_id=1, source_target_pairs={{0,16},{8,24},{16,0},{24,8},{1,17},{9,25},{17,1},{25,9},{2,18},{10... | collective-permute-start | bytes 393224 | tf_op jit(solution)/shard_map/ppermute | solution.py:330
  76.8 8.4 %collective-permute-start.9 = (bf16[256,256]{1,0:T(8,128)(2,1)S(1)}, bf16[256,256]{1,0:T(8,128)(2,1)S(1)}, u32[]{:S(2)}, u32[]{:S(2)}) collective-permute-start(bf16[256,256]{1,0:T(8,128)(2,1)S(1)} %get-tuple-element.39), channel_id=1, source_target_pairs={{0,24},{8,0},{16,8},{24,16},{1,25},{9,1},{17,9},{25,17},{2,26},{10... | collective-permute-start | bytes 393224 | tf_op jit(solution)/shard_map/ppermute | solution.py:330
  80.4 51.0 %copy-start.6 = (bf16[256,256]{1,0:T(8,128)(2,1)}, bf16[256,256]{1,0:T(8,128)(2,1)S(1)}, u32[]{:S(2)}) copy-start(bf16[256,256]{1,0:T(8,128)(2,1)S(1)} %collective-permute-done.7.refs_5_) | copy-start | bytes 393220
  81.6 49.8 %copy-start.7 = (bf16[256,256]{1,0:T(8,128)(2,1)}, bf16[256,256]{1,0:T(8,128)(2,1)S(1)}, u32[]{:S(2)}) copy-start(bf16[256,256]{1,0:T(8,128)(2,1)S(1)} %collective-permute-done.8.refs_6_) | copy-start | bytes 393220
  85.2 46.2 %copy-start.8 = (bf16[256,256]{1,0:T(8,128)(2,1)}, bf16[256,256]{1,0:T(8,128)(2,1)S(1)}, u32[]{:S(2)}) copy-start(bf16[256,256]{1,0:T(8,128)(2,1)S(1)} %collective-permute-done.9.refs_7_) | copy-start | bytes 393220
  120.4 1.3 copy-start
  131.4 19.9 %all-to-all-start.1 = ((bf16[32,32,256]{2,1,0:T(8,128)(2,1)}), bf16[32,32,256]{2,1,0:T(8,128)(2,1)S(1)}, u32[]{:S(2)}, u32[]{:S(2)}) async-start(bf16[32,32,256]{2,1,0:T(8,128)(2,1)} %bitcast.34), calls=%async_computation.1 | async-start | bytes 1048576 | tf_op jit(solution)/shard_map/all_to_all | solution.py:400
  151.3 43.8 %copy-start.2 = (bf16[32,32,256]{2,1,0:T(8,128)(2,1)}, bf16[32,32,256]{2,1,0:T(8,128)(2,1)S(1)}, u32[]{:S(2)}) copy-start(bf16[32,32,256]{2,1,0:T(8,128)(2,1)S(1)} %all-to-all-done.1.refs_2_) | copy-start | bytes 1572868
  151.3 43.8 %all-to-all-start.2 = ((bf16[32,96,256]{2,1,0:T(8,128)(2,1)}), bf16[32,96,256]{2,1,0:T(8,128)(2,1)S(1)}, u32[]{:S(2)}, u32[]{:S(2)}) async-start(bf16[32,96,256]{2,1,0:T(8,128)(2,1)} %bitcast.35), calls=%async_computation.2 | async-start | bytes 3145728 | tf_op jit(solution)/shard_map/all_to_all | solution.py:400
  195.2 1.2 copy-start.1
Sparse Core Ops, SparseCore 0:
  10.1 60.9 all-gather.10
  72.7 35.1 all-gather.6
  120.5 39.0 all-gather.8
